TPU v7x, 32 devices: a whole 2x2x4 slice. The times are simulated.
32 devices in a mesh: parts: 2 (over x), depth: 8 (over z, y), tile: 2 (over core).
Axes of the slice: x: 2, y: 2, z: 4, core: 2. Of those that a mesh axis runs over, the one named last changes fastest.
Arguments:
- volume: bfloat16 [4, 256, 32, 4096], P(None, ('parts', 'depth'), 'tile'), parts along dimension 1, may hold values from -6 to 6
- brick_mask: int32 [16, 32], P(('parts', 'depth')), parts along dimension 0, may hold values 0 or 1
- brick_order: int32 [16], P('parts'), parts along dimension 0, may hold values from 0 to 7, each once
Outputs:
- picture: float32 [4, 64, 4096], P(None, 'parts', 'depth'), parts along dimension 1
There are 2 independent parts, one for each index of `parts`. A program takes and returns all parts, laid end to end along the dimension named above; each array names one. Nothing has to cross between parts.
Inputs may be any that keep to these rules, and one draw needn't show every extreme that they name: `brick_order`: each slab appears once; position 0 is the front.
All inputs are finite; a program needn't handle non-finite values. No bound on the sum of `brick_mask` on one device may be relied on, other than what follows from the above.
Results may differ from a plain program's by a relative error of at most 0.0003.
Values may be sent and summed in bfloat16 or wider, within the bound.
No kernel may reach another device: no remote copies, remote signals or barrier semaphores. Data moves between devices by JAX's collectives and lax.ppermute only.
A program may use at most 64 MiB of HBM per device.

v0:
```python
import jax
import jax.numpy as jnp
from jax import lax
from jax.sharding import PartitionSpec as P


def with_halo(block, sides, width):
    for axis, dim in sides:
        count = lax.axis_size(axis)
        forward = [(i, i + 1) for i in range(count - 1)]
        backward = [(target, source) for source, target in forward]
        low = lax.ppermute(
            lax.slice_in_dim(block, block.shape[dim] - width, None, axis=dim), axis, forward
        )
        high = lax.ppermute(lax.slice_in_dim(block, 0, width, axis=dim), axis, backward)
        block = jnp.concatenate([low, block, high], axis=dim)
    return block


def march(padded, emission, step_size):
    density = padded[1:-1, 1:-1, 1:-1]
    grad_depth = 0.5 * (padded[2:, 1:-1, 1:-1] - padded[:-2, 1:-1, 1:-1])
    grad_rows = 0.5 * (padded[1:-1, 2:, 1:-1] - padded[1:-1, :-2, 1:-1])
    grad_cols = 0.5 * (padded[1:-1, 1:-1, 2:] - padded[1:-1, 1:-1, :-2])
    inverse = lax.rsqrt(
        1.0 + grad_depth * grad_depth + grad_rows * grad_rows + grad_cols * grad_cols
    )
    shading = 0.3 + 0.7 * jnp.abs(0.8 * grad_depth + 0.36 * grad_rows + 0.48 * grad_cols) * inverse
    extinction = density * density * step_size
    through = jnp.cumsum(extinction, axis=0)
    before = through - extinction
    weights = (jnp.exp(-before) - jnp.exp(-through)) * shading
    emitted = jax.nn.sigmoid(emission.astype(jnp.float32))
    colour = jnp.sum(weights[None] * emitted, axis=1)
    return (colour, through[-1])


def on_device(volume, brick_mask, brick_order):
    channels, slab_cells, rows, cols = volume.shape
    slabs = lax.axis_size("depth")
    blocks = brick_mask.shape[1]
    block_cols = cols // blocks
    step_size = 3.0 / (slab_cells * slabs)
    keep_cols = jnp.repeat(brick_mask[0], block_cols).astype(jnp.bfloat16)
    density = volume[0] * keep_cols[None, None, :]
    ghosted = with_halo(density, (("depth", 0), ("tile", 1)), 1)
    padded = jnp.pad(ghosted.astype(jnp.float32), ((0, 0), (0, 0), (1, 1)))
    emission = volume[1:]
    colour, optical = march(padded, emission, step_size)
    positions = jnp.arange(slabs, dtype=jnp.int32)
    ranking = jnp.sum(
        jnp.where(brick_order[:, None] == positions[None, :], positions[:, None], 0), axis=0
    )
    own_index = lax.axis_index("depth")
    strip = cols // slabs
    gathered = lax.all_gather(optical[None], "depth", axis=0, tiled=True)
    own_rank = ranking[own_index]
    in_front = ranking < own_rank
    covered = jnp.sum(jnp.where(in_front[:, None, None], gathered, 0.0), axis=0)
    terms = jnp.exp(-covered)[None] * colour
    blended = lax.psum_scatter(terms, "depth", scatter_dimension=2, tiled=True)
    summed = lax.dynamic_slice_in_dim(jnp.sum(gathered, axis=0), own_index * strip, strip, 1)
    opacity = 1.0 - jnp.exp(-summed)
    picture = jnp.concatenate([blended, opacity[None]], axis=0)
    return lax.all_gather(picture, "tile", axis=1, tiled=True)


def solution(mesh):
    return jax.shard_map(
        on_device,
        mesh=mesh,
        in_specs=(
            P(None, ("parts", "depth"), "tile", None),
            P(("parts", "depth"), None),
            P("parts"),
        ),
        out_specs=P(None, "parts", "depth"),
        check_vma=False,
    )
```

profile of v0, /device:TPU:0, one launch (start us, length us, event | category | flops | bytes accessed | tf_op | source)
XLA Modules:
  0.0 165.5 jit_solution(9184333961611137345)
XLA Ops:
  6.5 0.0 all-gather.2.cloned.1.call-start
  6.5 0.7 convert_bitcast_fusion
  7.2 0.1 broadcast_bitcast_fusion
  7.3 1.7 %bitcast_multiply_fusion = bf16[16,16,4096]{2,1,0:T(8,128)(2,1)S(1)} fusion(bf16[4,16,16,4096]{3,2,1,0:T(8,128)(2,1)} %param.3, bf16[4096]{0:T(1024)(128)(2,1)S(1)} %broadcast_bitcast_fusion), kind=kLoop, calls=%fused_computation.11 | loop fusion | flops 1048576 | bytes 4202496 | tf_op jit(solution)/shard_map/mul | solution.py:45
  9.0 4.9 %collective-permute-start = (bf16[1,16,4096]{2,1,0:T(8,128)(2,1)S(1)}, bf16[1,16,4096]{2,1,0:T(8,128)(2,1)S(1)}, u32[]{:S(2)}, u32[]{:S(2)}) collective-permute-start(bf16[1,16,4096]{2,1,0:T(8,128)(2,1)S(1)} %get-tuple-element.9), channel_id=1, source_target_pairs={{0,2},{2,4},{4,6},{6,8},{8,10},{10,12},{12,14},{1,3},{3,5},{5,7},{... | collective-permute-start | bytes 393224 | tf_op jit(solution)/shard_map/ppermute | solution.py:12
  13.9 1.3 collective-permute-start.1
  15.2 1.4 collective-permute-done
  16.7 4.1 %collective-permute-done.1 = bf16[1,16,4096]{2,1,0:T(8,128)(2,1)S(1)} collective-permute-done((bf16[1,16,4096]{2,1,0:T(8,128)(2,1)S(1)}, bf16[1,16,4096]{2,1,0:T(8,128)(2,1)S(1)}, u32[]{:S(2)}, u32[]{:S(2)}) %collective-permute-start.1) | collective-permute-done | bytes 131104 | tf_op jit(solution)/shard_map/ppermute | solution.py:15
  20.8 0.6 pad_maximum_fusion.2
  21.4 1.3 collective-permute-start.2
  22.7 1.3 collective-permute-start.3
  24.0 0.0 collective-permute-done.2
  24.0 2.2 %collective-permute-done.3 = bf16[18,1,4096]{2,1,0:T(2,128)(2,1)S(1)} collective-permute-done((bf16[18,1,4096]{2,1,0:T(2,128)(2,1)S(1)}, bf16[18,1,4096]{2,1,0:T(2,128)(2,1)S(1)}, u32[]{:S(2)}, u32[]{:S(2)}) %collective-permute-start.3) | collective-permute-done | bytes 147488 | tf_op jit(solution)/shard_map/ppermute | solution.py:15
  26.2 1.7 %maximum_convert_fusion = f32[18,18,4096]{2,1,0:T(8,128)S(1)} fusion(bf16[18,1,4096]{2,1,0:T(2,128)(2,1)S(1)} %collective-permute-done.3, bf16[1,16,4096]{2,1,0:T(8,128)(2,1)S(1)} %collective-permute-done.1, bf16[16,16,4096]{2,1,0:T(8,128)(2,1)S(1)} %bitcast_multiply_fusion, bf16[1,16,4096]{2,1,0:T(8,128)(2,1)S(1)} %collective-permute-done, ...), kind=kLoop, calls=%fused_computation.9 | loop fusion | flops 13271040 | bytes 7962624 | tf_op jit(solution)/shard_map/convert_element_type | solution.py:47
  27.9 0.0 copy-start
  27.9 9.9 %add_multiply_fusion = (f32[16,16,4096]{2,1,0:T(8,128)}, f32[16,16,4096]{2,1,0:T(8,128)}) fusion(f32[18,18,4096]{2,1,0:T(8,128)S(1)} %maximum_convert_fusion), kind=kOutput, calls=%fused_computation.8 | output fusion | flops 47185920 | bytes 40632320 | tf_op jit(solution)/shard_map/jit(cumsum)/reduce_window_sum | solution.py:30
  37.8 1.7 %slice.64 = f32[1,16,4096]{2,1,0:T(8,128)} slice(f32[16,16,4096]{2,1,0:T(8,128)} %get-tuple-element.12), slice={[15:16], [0:16], [0:4096]} | slice | bytes 524288 | tf_op jit(solution)/shard_map/slice | solution.py:35
  39.5 0.0 all-gather.2.cloned.1.call-update
  39.5 0.0 reduce-scatter.2.cloned.1.call-start
  39.5 0.0 copy-done
  39.6 0.1 select_reduce_fusion.1
  39.6 0.6 dynamic_slice.6
  40.2 0.6 broadcast_compare_fusion
  40.8 6.5 %multiply_reduce_fusion = f32[3,16,4096]{2,1,0:T(8,128)S(1)} fusion(bf16[4,16,16,4096]{3,2,1,0:T(8,128)(2,1)} %param.3, f32[16,16,4096]{2,1,0:T(8,128)} %get-tuple-element.11), kind=kLoop, calls=%fused_computation | loop fusion | flops 18677760 | bytes 11272192 | tf_op jit(solution)/shard_map/reduce_sum | solution.py:34
  47.3 42.7 %all-gather.2.cloned.1.call-done = f32[8,16,4096]{2,1,0:T(8,128)} async-done(((f32[1,16,4096]{2,1,0:T(8,128)}), f32[8,16,4096]{2,1,0:T(8,128)}) %all-gather.2.cloned.1.call-update) | async-done | bytes 2097168 | tf_op jit(solution)/shard_map/all_gather | solution.py:56
  90.1 1.9 %select_reduce_fusion = (f32[16,4096]{1,0:T(8,128)S(1)}, f32[16,4096]{1,0:T(8,128)S(1)}) fusion(f32[8,16,4096]{2,1,0:T(8,128)} %all-gather.2.cloned.1.call-done, pred[8]{0:T(512)(128)(4,1)S(1)} %broadcast_compare_fusion), kind=kLoop, calls=%fused_computation.12 | loop fusion | flops 1441792 | bytes 2621448 | tf_op jit(solution)/shard_map/reduce_sum | solution.py:59
  92.0 0.9 broadcast_multiply_fusion
  93.0 0.0 reduce-scatter.2.cloned.1.call-update
  93.0 62.0 %reduce-scatter.2.cloned.1.call-done = f32[3,16,512]{2,1,0:T(8,128)} async-done(((f32[3,16,4096]{2,1,0:T(8,128)}), f32[3,16,512]{2,1,0:T(8,128)}) %reduce-scatter.2.cloned.1.call-update) | async-done | bytes 98320 | tf_op jit(solution)/shard_map/reduce_scatter | solution.py:61
  155.1 0.9 pad_maximum_fusion.3
  156.0 2.0 %all_gather.7 = f32[4,32,512]{2,1,0:T(8,128)S(1)} all-gather(f32[4,16,512]{2,1,0:T(8,128)S(1)} %pad_maximum_fusion.3), channel_id=1, replica_groups=mesh['parts'=2,'depth'=8,'tile'=2] {'tile'}, dimensions={1}, use_global_device_ids=true | all-gather | bytes 393216 | tf_op jit(solution)/shard_map/all_gather | solution.py:65
  158.0 0.7 copy.5
  (3 shorter events, 0.1 us)
Async XLA Ops:
  6.5 83.5 %all-gather.2.cloned.1.call-start = ((), (), s32[]{:S(2)}) async-start(), calls=%async_computation.1 | async-start | bytes 2359296 | tf_op jit(solution)/shard_map/all_gather | solution.py:56
  9.0 7.6 %collective-permute-start = (bf16[1,16,4096]{2,1,0:T(8,128)(2,1)S(1)}, bf16[1,16,4096]{2,1,0:T(8,128)(2,1)S(1)}, u32[]{:S(2)}, u32[]{:S(2)}) collective-permute-start(bf16[1,16,4096]{2,1,0:T(8,128)(2,1)S(1)} %get-tuple-element.9), channel_id=1, source_target_pairs={{0,2},{2,4},{4,6},{6,8},{8,10},{10,12},{12,14},{1,3},{3,5},{5,7},{... | collective-permute-start | bytes 393224 | tf_op jit(solution)/shard_map/ppermute | solution.py:12
  13.9 6.9 %collective-permute-start.1 = (bf16[1,16,4096]{2,1,0:T(8,128)(2,1)S(1)}, bf16[1,16,4096]{2,1,0:T(8,128)(2,1)S(1)}, u32[]{:S(2)}, u32[]{:S(2)}) collective-permute-start(bf16[1,16,4096]{2,1,0:T(8,128)(2,1)S(1)} %get-tuple-element.10), channel_id=1, source_target_pairs={{2,0},{4,2},{6,4},{8,6},{10,8},{12,10},{14,12},{3,1},{5,3},{7,5},{... | collective-permute-start | bytes 393224 | tf_op jit(solution)/shard_map/ppermute | solution.py:15
  21.4 2.6 %collective-permute-start.2 = (bf16[18,1,4096]{2,1,0:T(2,128)(2,1)S(1)}, bf16[18,1,4096]{2,1,0:T(2,128)(2,1)S(1)}, u32[]{:S(2)}, u32[]{:S(2)}) collective-permute-start(bf16[18,1,4096]{2,1,0:T(2,128)(2,1)S(1)} %get-tuple-element.7), channel_id=1, source_target_pairs={{0,1},{2,3},{4,5},{6,7},{8,9},{10,11},{12,13},{14,15},{16,17},{18,... | collective-permute-start | bytes 442376 | tf_op jit(solution)/shard_map/ppermute | solution.py:12
  22.7 3.5 %collective-permute-start.3 = (bf16[18,1,4096]{2,1,0:T(2,128)(2,1)S(1)}, bf16[18,1,4096]{2,1,0:T(2,128)(2,1)S(1)}, u32[]{:S(2)}, u32[]{:S(2)}) collective-permute-start(bf16[18,1,4096]{2,1,0:T(2,128)(2,1)S(1)} %get-tuple-element.8), channel_id=1, source_target_pairs={{1,0},{3,2},{5,4},{7,6},{9,8},{11,10},{13,12},{15,14},{17,16},{19,... | collective-permute-start | bytes 442376 | tf_op jit(solution)/shard_map/ppermute | solution.py:15
  27.9 11.6 %copy-start = (s32[8]{0:T(128)S(1)}, s32[8]{0:T(128)}, u32[]{:S(2)}) copy-start(s32[8]{0:T(128)} %param.5) | copy-start | bytes 100
  39.5 115.6 %reduce-scatter.2.cloned.1.call-start = ((), (), s32[]{:S(2)}) async-start(), calls=%async_computation.2 | async-start | bytes 884736 | tf_op jit(solution)/shard_map/reduce_scatter | solution.py:61
Sparse Core Ops, SparseCore 0:
  39.6 50.4 all-gather.1
  93.4 61.6 reduce-scatter.1
where the time goes:
time: 166 us; the launch traced here: 165 us
  waiting for transfers between devices  113 us (68%)
  other arithmetic  25.6 us (15%)
  between operations  13.5 us (8%)
  starting transfers between devices  8.81 us (5%)
  local copies, waits for them, and re-layouts  3.06 us (2%)
  blocking collectives  1.99 us (1%)
    reduce_scatter x1, waiting for transfers between devices, on_device(): blended = lax.psum_scatter(terms, 'depth', scatter_dimension=2, tiled=True)  62 us
    all_gather x1, waiting for transfers between devices, on_device(): gathered = lax.all_gather(optical[None], 'depth', axis=0, tiled=True)  42.7 us
    another operation x1, other arithmetic, march(): through = jnp.cumsum(extinction, axis=0)  9.85 us
    reduce_sum x1, other arithmetic, march(): colour = jnp.sum(weights[None] * emitted, axis=1)  6.51 us
    ppermute x2, waiting for transfers between devices, with_halo(): lax.ppermute(lax.slice_in_dim(block, 0, width, axis=dim), axis, backward)  6.3 us
    ppermute x2, starting transfers between devices, with_halo(): lax.ppermute(lax.slice_in_dim(block, block.shape[dim] - width, None, axis...  6.19 us
  transfers between devices with their start and end apart: 6, of which 5 were waited for; matrix products, arithmetic and copies ran while one was open for 5% of the time, Pallas kernels for 0%

commit v1 on v0

v1 whole, which is shorter than its diff:
```python
import functools
import math

import jax
import jax.numpy as jnp
from jax import lax
from jax.experimental import pallas as pl
from jax.experimental.pallas import tpu as pltpu
from jax.sharding import PartitionSpec as P

LANES = 128


def partners(n, k):
    if n & (n - 1) == 0:
        return [(i, i ^ k) for i in range(n)]
    return [(i, (i + k) % n) for i in range(n)]


def target(n, me, k):
    if n & (n - 1) == 0:
        return lax.bitwise_xor(me, k)
    return lax.rem(me + k, n)


def source(n, me, k):
    if n & (n - 1) == 0:
        return lax.bitwise_xor(me, k)
    return lax.rem(me + n - k, n)


def march_kernel(
    step_size, bricks, strips_ref, mask_ref, side_ref, vol, left, right, low, high, rows_halo, out
):
    depth, rows = vol.shape[1], vol.shape[2]
    strip = strips_ref[pl.program_id(0)]
    lane = lax.broadcasted_iota(jnp.int32, (rows, LANES), 1)
    row = lax.broadcasted_iota(jnp.int32, (rows, LANES), 0)
    first_row, last_row = row == 0, row == rows - 1
    first_lane, last_lane = lane == 0, lane == LANES - 1
    right_half = lane >= LANES // 2
    rate = -step_size * math.log2(math.e)
    to_top = side_ref[0].astype(jnp.float32)
    to_bottom = side_ref[1].astype(jnp.float32)

    for brick in range(bricks):
        cols = pl.ds(brick * LANES, LANES)
        place = strip * bricks + brick + 1
        keep = mask_ref[place] != 0

        @pl.when(jnp.logical_not(keep))
        def _():
            out[0, :, :, cols] = jnp.zeros((4, rows, LANES), jnp.float32)

        @pl.when(keep)
        def _():
            keep_left = mask_ref[place - 1].astype(jnp.float32)
            keep_right = mask_ref[place + 1].astype(jnp.float32)
            keep_side = jnp.where(right_half, keep_left, keep_right)
            halo = rows_halo[:, cols].astype(jnp.float32)
            top, bottom = halo * to_top, halo * to_bottom
            before = low[:, cols].astype(jnp.float32)
            here = vol[0, 0, :, cols].astype(jnp.float32)
            total = jnp.zeros((rows, LANES), jnp.float32)
            clear = jnp.ones((rows, LANES), jnp.float32)
            plain = jnp.zeros((rows, LANES), jnp.float32)
            sums = [jnp.zeros((rows, LANES), jnp.float32) for _ in range(3)]
            for d in range(depth):
                after = (vol[0, d + 1, :, cols] if d + 1 < depth else high[:, cols]).astype(
                    jnp.float32
                )
                prev = vol[0, d, :, pl.ds((brick - 1) * LANES, LANES)] if brick else left[0, d]
                nxt = (
                    vol[0, d, :, pl.ds((brick + 1) * LANES, LANES)]
                    if brick + 1 < bricks
                    else right[0, d]
                )
                side = jnp.where(
                    right_half, prev.astype(jnp.float32), nxt.astype(jnp.float32)
                ) * keep_side
                less = pltpu.roll(jnp.where(last_lane, side, here), 1, 1)
                more = pltpu.roll(jnp.where(first_lane, side, here), LANES - 1, 1)
                up = jnp.where(first_row, top[d : d + 1], pltpu.roll(here, 1, 0))
                down = jnp.where(last_row, bottom[d : d + 1], pltpu.roll(here, rows - 1, 0))
                g_depth, g_rows, g_cols = after - before, down - up, more - less
                square = g_depth * g_depth + g_rows * g_rows + g_cols * g_cols
                toward = jnp.abs(0.28 * g_depth + 0.126 * g_rows + 0.168 * g_cols)
                shading = 0.3 + toward * lax.rsqrt(1.0 + 0.25 * square)
                total = total + here * here
                left_over = jnp.exp2(total * rate)
                weight = (clear - left_over) * shading
                clear = left_over
                plain = plain + weight
                for k in range(3):
                    emission = vol[1 + k, d, :, cols].astype(jnp.float32)
                    sums[k] = sums[k] + weight * jnp.tanh(0.5 * emission)
                before, here = here, after
            for k in range(3):
                out[0, k, :, cols] = 0.5 * (plain + sums[k])
            out[0, 3, :, cols] = total * step_size


def march(volume, low, high, rows_halo, strips, mask, side, step_size, n):
    channels, depth, rows, cols = volume.shape
    strip = cols // n
    bricks = strip // LANES
    blocks = cols // LANES
    spec = pltpu.PrefetchScalarGridSpec(
        num_scalar_prefetch=3,
        grid=(n,),
        in_specs=[
            pl.BlockSpec((channels, depth, rows, strip), lambda j, s, m, t: (0, 0, 0, s[j])),
            pl.BlockSpec(
                (1, depth, rows, LANES),
                lambda j, s, m, t: (0, 0, 0, jnp.maximum(s[j] * bricks - 1, 0)),
            ),
            pl.BlockSpec(
                (1, depth, rows, LANES),
                lambda j, s, m, t: (0, 0, 0, jnp.minimum((s[j] + 1) * bricks, blocks - 1)),
            ),
            pl.BlockSpec((rows, strip), lambda j, s, m, t: (0, s[j])),
            pl.BlockSpec((rows, strip), lambda j, s, m, t: (0, s[j])),
            pl.BlockSpec((depth, strip), lambda j, s, m, t: (0, s[j])),
        ],
        out_specs=pl.BlockSpec((1, 4, rows, strip), lambda j, s, m, t: (j, 0, 0, 0)),
    )
    cells = depth * rows * cols
    return pl.pallas_call(
        functools.partial(march_kernel, step_size, bricks),
        grid_spec=spec,
        out_shape=jax.ShapeDtypeStruct((n, 4, rows, strip), jnp.float32),
        cost_estimate=pl.CostEstimate(
            flops=40 * cells, bytes_accessed=8 * cells, transcendentals=5 * cells
        ),
        compiler_params=pltpu.CompilerParams(
            dimension_semantics=("arbitrary",), vmem_limit_bytes=32 * 1024 * 1024
        ),
        name="march",
    )(strips, mask, side, volume, volume, volume, low, high, rows_halo)


def composite_kernel(n, rank_ref, *refs):
    parts, out = refs[:n], refs[n]
    optical = [part[3] for part in parts]
    whole = optical[0]
    for k in range(1, n):
        whole = whole + optical[k]
    for k in range(n):
        covered = jnp.zeros_like(whole)
        for e in range(n):
            if e != k:
                covered = covered + jnp.where(rank_ref[e] < rank_ref[k], 1.0, 0.0) * optical[e]
        through = jnp.exp(-covered)
        for c in range(3):
            term = through * parts[k][c]
            out[c] = term if k == 0 else out[c] + term
    out[3] = 1.0 - jnp.exp(-whole)


def composite(ranks, parts):
    n = len(parts)
    shape = parts[0].shape
    return pl.pallas_call(
        functools.partial(composite_kernel, n),
        grid_spec=pltpu.PrefetchScalarGridSpec(
            num_scalar_prefetch=1,
            grid=(1,),
            in_specs=[pl.BlockSpec(shape, lambda i, r: (0, 0, 0)) for _ in parts],
            out_specs=pl.BlockSpec(shape, lambda i, r: (0, 0, 0)),
        ),
        out_shape=jax.ShapeDtypeStruct(shape, jnp.float32),
        name="composite",
    )(ranks, *parts)


def on_device(volume, brick_mask, brick_order):
    channels, depth, rows, cols = volume.shape
    n = lax.axis_size("depth")
    tiles = lax.axis_size("tile")
    blocks = brick_mask.shape[1]
    step_size = 3.0 / (depth * n)
    me, tile = lax.axis_index("depth"), lax.axis_index("tile")
    keep = jnp.repeat(brick_mask[0], cols // blocks).astype(jnp.bfloat16)
    mask = jnp.pad(jnp.repeat(brick_mask[0], cols // blocks // LANES), 1)

    up = [(i, i + 1) for i in range(n - 1)]
    down = [(i + 1, i) for i in range(n - 1)]
    assert tiles == 2
    edge = jnp.where(tile == 0, volume[0, :, rows - 1], volume[0, :, 0]) * keep
    rows_halo = lax.ppermute(edge, "tile", [(0, 1), (1, 0)])
    side = jnp.stack([tile, 1 - tile]).astype(jnp.int32)
    low = lax.ppermute(volume[0, depth - 1] * keep, "depth", up)
    high = lax.ppermute(volume[0, 0] * keep, "depth", down)

    strips = jnp.stack([target(n, me, k) for k in range(n)]).astype(jnp.int32)
    bricks = march(volume, low, high, rows_halo, strips, mask, side, step_size, n)
    parts = [bricks[0]]
    for k in range(1, n):
        parts.append(lax.ppermute(bricks[k], "depth", partners(n, k)))
    ranking = jnp.sum(
        jnp.where(
            brick_order[:, None] == jnp.arange(n, dtype=jnp.int32)[None, :],
            jnp.arange(n, dtype=jnp.int32)[:, None],
            0,
        ),
        axis=0,
    )
    sources = jnp.stack([source(n, me, k) for k in range(n)])
    picture = composite(ranking[sources].astype(jnp.int32), parts)
    return lax.all_gather(picture, "tile", axis=1, tiled=True)


def solution(mesh):
    return jax.shard_map(
        on_device,
        mesh=mesh,
        in_specs=(
            P(None, ("parts", "depth"), "tile", None),
            P(("parts", "depth"), None),
            P("parts"),
        ),
        out_specs=P(None, "parts", "depth"),
        check_vma=False,
    )
```

time: 166 us -> 62.4 us (0.38)
  waiting for transfers between devices: 113 us -> 9.82 us
  other arithmetic: 25.6 us -> 2.11 us
  starting transfers between devices: 8.81 us -> 28.3 us
  between operations: 13.5 us -> 0.13 us
  Pallas kernels: 0 us -> 9.91 us
  local copies, waits for them, and re-layouts: 3.06 us -> 9.8 us
    reduce_scatter x1 -> x0, waiting for transfers between devices: 62 us -> none  [on_device(): blended = lax.psum_scatter(terms, 'depth', scatter_dimension=2, tiled=True)]
    all_gather x1 -> x0, waiting for transfers between devices: 42.7 us -> none  [on_device(): gathered = lax.all_gather(optical[None], 'depth', axis=0, tiled=True)]
    ppermute x4 -> x10, starting transfers between devices: 8.77 us -> 28.3 us  [the longest x7 21.4 us: on_device(): parts.append(lax.ppermute(bricks[k], 'depth', partners(n, k)))]
    pallas_call x0 -> x2, Pallas kernels: none -> 9.91 us  [the longest x1 7.12 us: march(): pl.pallas_call(functools.partial(march_kernel, step_size, bricks), grid_s...]
    another operation x1, other arithmetic: 9.85 us -> 0.07 us  [on_device(): side = jnp.stack([tile, 1 - tile]).astype(jnp.int32)]
    reduce_sum x3 -> x1, other arithmetic: 8.5 us -> 0.08 us  [on_device(): jnp.sum(jnp.where(brick_order[:, None] == jnp.arange(n, dtype=jnp.int32)[...]
    unnamed x3 -> x19, local copies, waits for them, and re-layouts: 0.71 us -> 4.76 us
    ppermute x4 -> x10, waiting for transfers between devices: 7.73 us -> 9.82 us  [the longest x7 6.38 us: on_device(): parts.append(lax.ppermute(bricks[k], 'depth', partners(n, k)))]
  transfers between devices with their start and end apart: 6 -> 10, of which waited for: 5 -> 5; matrix products, arithmetic and copies ran while one was open for 5% -> 4% of each run, Pallas kernels for 0% -> 0%
where the time goes in v1:
time: 62.4 us
  starting transfers between devices  28.3 us (45%)
  Pallas kernels  9.91 us (16%)
  waiting for transfers between devices  9.82 us (16%)
  local copies, waits for them, and re-layouts  9.8 us (16%)
  blocking collectives  2.29 us (4%)
  other arithmetic  2.11 us (3%)
    ppermute x7, starting transfers between devices, on_device(): parts.append(lax.ppermute(bricks[k], 'depth', partners(n, k)))  21.4 us
    pallas_call x1, Pallas kernels, march(): pl.pallas_call(functools.partial(march_kernel, step_size, bricks), grid_s...  7.12 us
    ppermute x7, waiting for transfers between devices, on_device(): parts.append(lax.ppermute(bricks[k], 'depth', partners(n, k)))  6.38 us
    ppermute x1, starting transfers between devices, on_device(): low = lax.ppermute(volume[0, depth - 1] * keep, 'depth', up)  5.51 us
    unnamed x19, local copies, waits for them, and re-layouts  4.76 us
    ppermute x1, waiting for transfers between devices, on_device(): low = lax.ppermute(volume[0, depth - 1] * keep, 'depth', up)  2.96 us
    pallas_call x1, Pallas kernels, composite(): pl.pallas_call(functools.partial(composite_kernel, n), grid_spec=pltpu.Pr...  2.79 us
    all_gather x1, blocking collectives, on_device(): return lax.all_gather(picture, 'tile', axis=1, tiled=True)  2.29 us
  transfers between devices with their start and end apart: 10, of which 5 were waited for; matrix products, arithmetic and copies ran while one was open for 4% of the time, Pallas kernels for 0%

profile of v1, /device:TPU:0, one launch (start us, length us, event | category | flops | bytes accessed | tf_op | source)
XLA Modules:
  0.0 62.4 jit_solution(4898127660898939300)
XLA Ops:
  0.0 0.7 %bitcast_convert_fusion = bf16[32]{0:T(256)(128)(2,1)S(1)} fusion(s32[1,32]{1,0:T(1,128)} %param.4), kind=kLoop, calls=%fused_computation.21 | loop fusion | flops 32 | bytes 192 | tf_op jit(solution)/shard_map/convert_element_type | solution.py:183
  0.7 0.1 broadcast_bitcast_fusion
  0.7 2.1 %fusion.3 = (bf16[1,16,1,4096]{3,2,1,0:T(2,128)(2,1)S(1)}, bf16[1,16,1,4096]{3,2,1,0:T(2,128)(2,1)S(1)}) fusion(bf16[4,16,16,4096]{3,2,1,0:T(8,128)(2,1)} %right.1), kind=kLoop, calls=%fused_computation.22 | loop fusion | bytes 524288 | tf_op jit(solution)/shard_map/slice | solution.py:189
  2.9 1.3 %bitcast_multiply_fusion = (bf16[16,4096]{1,0:T(8,128)(2,1)S(1)}, bf16[16,4096]{1,0:T(8,128)(2,1)S(1)}, bf16[16,4096]{1,0:T(8,128)(2,1)S(1)}) fusion(bf16[4,16,16,4096]{3,2,1,0:T(8,128)(2,1)} %right.1, bf16[4096]{0:T(1024)(128)(2,1)S(1)} %broadcast_bitcast_fusion, bf16[1,16,1,4096]{3,2,1,0:T(2,128)(2,1)S(1)} %get-tuple-element.8, ...), kind=kLoop, calls=%fused_computation.12 | loop fusion | flops 262144 | bytes 925697 | tf_op jit(solution)/shard_map/mul | solution.py:193
  4.1 1.3 %collective-permute-start.1 = (bf16[16,4096]{1,0:T(8,128)(2,1)S(1)}, bf16[16,4096]{1,0:T(8,128)(2,1)S(1)}, u32[]{:S(2)}, u32[]{:S(2)}) collective-permute-start(bf16[16,4096]{1,0:T(8,128)(2,1)S(1)} %get-tuple-element.5), channel_id=1, source_target_pairs={{2,0},{4,2},{6,4},{8,6},{10,8},{12,10},{14,12},{3,1},{5,3},{7,5},{... | collective-permute-start | bytes 393224 | tf_op jit(solution)/shard_map/ppermute | solution.py:193
  5.4 5.5 %collective-permute-start = (bf16[16,4096]{1,0:T(8,128)(2,1)S(1)}, bf16[16,4096]{1,0:T(8,128)(2,1)S(1)}, u32[]{:S(2)}, u32[]{:S(2)}) collective-permute-start(bf16[16,4096]{1,0:T(8,128)(2,1)S(1)} %get-tuple-element.6), channel_id=1, source_target_pairs={{0,2},{2,4},{4,6},{6,8},{8,10},{10,12},{12,14},{1,3},{3,5},{5,7},{... | collective-permute-start | bytes 393224 | tf_op jit(solution)/shard_map/ppermute | solution.py:192
  11.0 0.1 collective-permute-start.2
  11.0 0.7 %pad.4.mask_ref = s32[34]{0:T(128)S(1)} pad(s32[32]{0:T(128)} %bitcast.48, s32[]{:T(128)} %constant.11.clone.1), padding=1_1 | pad | bytes 268 | tf_op jit(solution)/shard_map/jit(_pad)/pad | solution.py:184
  11.8 0.1 stack.71
  11.9 0.1 stack.80.strips_ref
  12.0 0.0 copy-start.8
  12.0 0.1 pad_add_fusion.side_ref
  12.0 0.5 collective-permute-done.1.high
  12.5 3.0 %collective-permute-done.low = bf16[16,4096]{1,0:T(8,128)(2,1)S(1)} collective-permute-done((bf16[16,4096]{1,0:T(8,128)(2,1)S(1)}, bf16[16,4096]{1,0:T(8,128)(2,1)S(1)}, u32[]{:S(2)}, u32[]{:S(2)}) %collective-permute-start) | collective-permute-done | bytes 131104 | tf_op jit(solution)/shard_map/ppermute | solution.py:192
  15.5 0.0 collective-permute-done.2.rows_halo
  15.5 0.0 copy-start
  15.5 3.4 %copy-done = bf16[4,16,16,4096]{3,2,1,0:T(8,128)(2,1)S(1)} copy-done((bf16[4,16,16,4096]{3,2,1,0:T(8,128)(2,1)S(1)}, bf16[4,16,16,4096]{3,2,1,0:T(8,128)(2,1)}, u32[]{:S(2)}) %copy-start) | copy-done | bytes 8388632
  18.9 7.1 %march.1 = f32[8,4,16,512]{3,2,1,0:T(8,128)S(1)} custom-call(s32[8]{0:T(128)S(1)} %stack.80.strips_ref, s32[34]{0:T(128)S(1)} %pad.4.mask_ref, s32[2]{0:T(128)S(1)} %pad_add_fusion.side_ref, bf16[4,16,16,4096]{3,2,1,0:T(8,128)(2,1)S(1)} %copy-done, bf16[4,16,16,4096]{3,2,1,0:T(8,128)(2,1)S(1)} %copy-done, bf16[4,16,16,4096]{3,2,1,0:T(8,128)(2,1)S(1)} %copy-done, ...), custom_call_target="tpu_custom_call" | custom-call | flops 41943040 | bytes 8388608 | tf_op jit(solution)/shard_map/march/pallas_call | solution.py:128
  26.0 0.8 %slice_bitcast_fusion = (f32[4,16,512]{2,1,0:T(8,128)S(1)}, f32[4,16,512]{2,1,0:T(8,128)S(1)}, f32[4,16,512]{2,1,0:T(8,128)S(1)}, f32[4,16,512]{2,1,0:T(8,128)S(...) fusion(f32[8,4,16,512]{3,2,1,0:T(8,128)S(1)} %march.1), kind=kLoop, calls=%fused_computation.1 | loop fusion | bytes 2097152 | tf_op jit(solution)/shard_map/squeeze | solution.py:199
  26.7 3.7 %collective-permute-start.9 = (f32[4,16,512]{2,1,0:T(8,128)S(1)}, f32[4,16,512]{2,1,0:T(8,128)S(1)}, u32[]{:S(2)}, u32[]{:S(2)}) collective-permute-start(f32[4,16,512]{2,1,0:T(8,128)S(1)} %get-tuple-element.9), channel_id=1, source_target_pairs={{0,14},{2,12},{4,10},{6,8},{8,6},{10,4},{12,2},{14,0},{1,15},{3,13... | collective-permute-start | bytes 393224 | tf_op jit(solution)/shard_map/ppermute | solution.py:199
  30.5 0.4 collective-permute-start.8
  30.8 1.2 %collective-permute-start.7 = (f32[4,16,512]{2,1,0:T(8,128)S(1)}, f32[4,16,512]{2,1,0:T(8,128)S(1)}, u32[]{:S(2)}, u32[]{:S(2)}) collective-permute-start(f32[4,16,512]{2,1,0:T(8,128)S(1)} %get-tuple-element.11), channel_id=1, source_target_pairs={{0,10},{2,8},{4,14},{6,12},{8,2},{10,0},{12,6},{14,4},{1,11},{3,9}... | collective-permute-start | bytes 393224 | tf_op jit(solution)/shard_map/ppermute | solution.py:199
  32.0 2.6 %collective-permute-start.6 = (f32[4,16,512]{2,1,0:T(8,128)S(1)}, f32[4,16,512]{2,1,0:T(8,128)S(1)}, u32[]{:S(2)}, u32[]{:S(2)}) collective-permute-start(f32[4,16,512]{2,1,0:T(8,128)S(1)} %get-tuple-element.12), channel_id=1, source_target_pairs={{0,8},{2,10},{4,12},{6,14},{8,0},{10,2},{12,4},{14,6},{1,9},{3,11}... | collective-permute-start | bytes 393224 | tf_op jit(solution)/shard_map/ppermute | solution.py:199
  34.7 1.5 %collective-permute-start.5 = (f32[4,16,512]{2,1,0:T(8,128)S(1)}, f32[4,16,512]{2,1,0:T(8,128)S(1)}, u32[]{:S(2)}, u32[]{:S(2)}) collective-permute-start(f32[4,16,512]{2,1,0:T(8,128)S(1)} %get-tuple-element.13), channel_id=1, source_target_pairs={{0,6},{2,4},{4,2},{6,0},{8,14},{10,12},{12,10},{14,8},{1,7},{3,5},... | collective-permute-start | bytes 393224 | tf_op jit(solution)/shard_map/ppermute | solution.py:199
  36.1 0.0 collective-permute-done.9.refs_7_
  36.1 0.0 copy-start.1
  36.1 12.1 %collective-permute-start.4 = (f32[4,16,512]{2,1,0:T(8,128)S(1)}, f32[4,16,512]{2,1,0:T(8,128)S(1)}, u32[]{:S(2)}, u32[]{:S(2)}) collective-permute-start(f32[4,16,512]{2,1,0:T(8,128)S(1)} %get-tuple-element.14), channel_id=1, source_target_pairs={{0,4},{2,6},{4,0},{6,2},{8,12},{10,14},{12,8},{14,10},{1,5},{3,7},... | collective-permute-start | bytes 393224 | tf_op jit(solution)/shard_map/ppermute | solution.py:199
  48.2 0.0 collective-permute-done.8.refs_6_
  48.2 0.0 copy-start.2
  48.2 0.0 collective-permute-start.3
  48.2 0.0 copy-done.8
  48.2 0.1 select_reduce_fusion
  48.3 1.2 %gather_fusion = s32[8]{0:T(128)} fusion(s32[8]{0:T(128)S(1)} %select_reduce_fusion, s32[1024]{0:T(1024)S(1)} %pad_clamp_fusion), kind=kCustom, calls=%fused_computation | custom fusion | bytes 96 | tf_op jit(solution)/shard_map/gather | solution.py:209
  49.5 2.9 %collective-permute-done.7.refs_5_ = f32[4,16,512]{2,1,0:T(8,128)S(1)} collective-permute-done((f32[4,16,512]{2,1,0:T(8,128)S(1)}, f32[4,16,512]{2,1,0:T(8,128)S(1)}, u32[]{:S(2)}, u32[]{:S(2)}) %collective-permute-start.7) | collective-permute-done | bytes 131104 | tf_op jit(solution)/shard_map/ppermute | solution.py:199
  52.4 0.0 copy-start.3
  52.4 0.8 %collective-permute-done.6.refs_4_ = f32[4,16,512]{2,1,0:T(8,128)S(1)} collective-permute-done((f32[4,16,512]{2,1,0:T(8,128)S(1)}, f32[4,16,512]{2,1,0:T(8,128)S(1)}, u32[]{:S(2)}, u32[]{:S(2)}) %collective-permute-start.6) | collective-permute-done | bytes 131104 | tf_op jit(solution)/shard_map/ppermute | solution.py:199
  53.2 0.0 copy-start.4
  53.2 0.0 collective-permute-done.5.refs_3_
  53.2 0.0 copy-start.5
  53.2 2.7 %collective-permute-done.4.refs_2_ = f32[4,16,512]{2,1,0:T(8,128)S(1)} collective-permute-done((f32[4,16,512]{2,1,0:T(8,128)S(1)}, f32[4,16,512]{2,1,0:T(8,128)S(1)}, u32[]{:S(2)}, u32[]{:S(2)}) %collective-permute-start.4) | collective-permute-done | bytes 131104 | tf_op jit(solution)/shard_map/ppermute | solution.py:199
  55.9 0.0 copy-start.6
  55.9 0.0 collective-permute-done.3.refs_1_
  55.9 0.0 copy-start.7
  55.9 0.0 copy-done.1
  55.9 0.0 copy-done.2
  55.9 0.0 copy-done.3
  55.9 0.0 copy-done.4
  55.9 0.0 copy-done.5
  55.9 0.6 copy-done.6
  56.5 0.1 copy-done.7
  56.6 2.8 %composite.1 = f32[4,16,512]{2,1,0:T(8,128)} custom-call(s32[8]{0:T(128)} %gather_fusion, f32[4,16,512]{2,1,0:T(8,128)} %get-tuple-element.16.refs_0_, f32[4,16,512]{2,1,0:T(8,128)} %copy-done.7, f32[4,16,512]{2,1,0:T(8,128)} %copy-done.6, f32[4,16,512]{2,1,0:T(8,128)} %copy-done.5, f32[4,16,512]{2,1,0:T(8,128)} %copy-done.4, f32[4,16,512]{2,1,0:T(8,128)} %copy-done.3, ...), custom_call_target="tpu_custom_call" | custom-call | tf_op jit(solution)/shard_map/composite/pallas_call | solution.py:163
  59.4 2.3 %all_gather.3 = f32[4,32,512]{2,1,0:T(8,128)S(1)} all-gather(f32[4,16,512]{2,1,0:T(8,128)} %composite.1), channel_id=1, replica_groups=mesh['parts'=2,'depth'=8,'tile'=2] {'tile'}, dimensions={1}, use_global_device_ids=true | all-gather | bytes 393216 | tf_op jit(solution)/shard_map/all_gather | solution.py:210
  61.7 0.7 %copy.19 = f32[4,32,512]{2,1,0:T(8,128)} copy(f32[4,32,512]{2,1,0:T(8,128)S(1)} %all_gather.3) | data formatting | bytes 524288
  (2 shorter events, 0.0 us)
Async XLA Ops:
  4.1 8.4 %collective-permute-start.1 = (bf16[16,4096]{1,0:T(8,128)(2,1)S(1)}, bf16[16,4096]{1,0:T(8,128)(2,1)S(1)}, u32[]{:S(2)}, u32[]{:S(2)}) collective-permute-start(bf16[16,4096]{1,0:T(8,128)(2,1)S(1)} %get-tuple-element.5), channel_id=1, source_target_pairs={{2,0},{4,2},{6,4},{8,6},{10,8},{12,10},{14,12},{3,1},{5,3},{7,5},{... | collective-permute-start | bytes 393224 | tf_op jit(solution)/shard_map/ppermute | solution.py:193
  5.4 10.0 %collective-permute-start = (bf16[16,4096]{1,0:T(8,128)(2,1)S(1)}, bf16[16,4096]{1,0:T(8,128)(2,1)S(1)}, u32[]{:S(2)}, u32[]{:S(2)}) collective-permute-start(bf16[16,4096]{1,0:T(8,128)(2,1)S(1)} %get-tuple-element.6), channel_id=1, source_target_pairs={{0,2},{2,4},{4,6},{6,8},{8,10},{10,12},{12,14},{1,3},{3,5},{5,7},{... | collective-permute-start | bytes 393224 | tf_op jit(solution)/shard_map/ppermute | solution.py:192
  11.0 4.5 %collective-permute-start.2 = (bf16[16,4096]{1,0:T(8,128)(2,1)S(1)}, bf16[16,4096]{1,0:T(8,128)(2,1)S(1)}, u32[]{:S(2)}, u32[]{:S(2)}) collective-permute-start(bf16[16,4096]{1,0:T(8,128)(2,1)S(1)} %get-tuple-element.17), channel_id=1, source_target_pairs={{0,1},{1,0},{2,3},{3,2},{4,5},{5,4},{6,7},{7,6},{8,9},{9,8},{10,11... | collective-permute-start | bytes 393224 | tf_op jit(solution)/shard_map/ppermute | solution.py:190
  12.0 36.2 %copy-start.8 = (s32[8]{0:T(128)S(1)}, s32[8]{0:T(128)}, u32[]{:S(2)}) copy-start(s32[8]{0:T(128)} %param.5) | copy-start | bytes 100
  15.5 3.4 %copy-start = (bf16[4,16,16,4096]{3,2,1,0:T(8,128)(2,1)S(1)}, bf16[4,16,16,4096]{3,2,1,0:T(8,128)(2,1)}, u32[]{:S(2)}) copy-start(bf16[4,16,16,4096]{3,2,1,0:T(8,128)(2,1)} %right.1) | copy-start | bytes 25165828
  26.7 9.4 %collective-permute-start.9 = (f32[4,16,512]{2,1,0:T(8,128)S(1)}, f32[4,16,512]{2,1,0:T(8,128)S(1)}, u32[]{:S(2)}, u32[]{:S(2)}) collective-permute-start(f32[4,16,512]{2,1,0:T(8,128)S(1)} %get-tuple-element.9), channel_id=1, source_target_pairs={{0,14},{2,12},{4,10},{6,8},{8,6},{10,4},{12,2},{14,0},{1,15},{3,13... | collective-permute-start | bytes 393224 | tf_op jit(solution)/shard_map/ppermute | solution.py:199
  30.5 17.7 %collective-permute-start.8 = (f32[4,16,512]{2,1,0:T(8,128)S(1)}, f32[4,16,512]{2,1,0:T(8,128)S(1)}, u32[]{:S(2)}, u32[]{:S(2)}) collective-permute-start(f32[4,16,512]{2,1,0:T(8,128)S(1)} %get-tuple-element.10), channel_id=1, source_target_pairs={{0,12},{2,14},{4,8},{6,10},{8,4},{10,6},{12,0},{14,2},{1,13},{3,15... | collective-permute-start | bytes 393224 | tf_op jit(solution)/shard_map/ppermute | solution.py:199
  30.8 21.6 %collective-permute-start.7 = (f32[4,16,512]{2,1,0:T(8,128)S(1)}, f32[4,16,512]{2,1,0:T(8,128)S(1)}, u32[]{:S(2)}, u32[]{:S(2)}) collective-permute-start(f32[4,16,512]{2,1,0:T(8,128)S(1)} %get-tuple-element.11), channel_id=1, source_target_pairs={{0,10},{2,8},{4,14},{6,12},{8,2},{10,0},{12,6},{14,4},{1,11},{3,9}... | collective-permute-start | bytes 393224 | tf_op jit(solution)/shard_map/ppermute | solution.py:199
  32.0 21.1 %collective-permute-start.6 = (f32[4,16,512]{2,1,0:T(8,128)S(1)}, f32[4,16,512]{2,1,0:T(8,128)S(1)}, u32[]{:S(2)}, u32[]{:S(2)}) collective-permute-start(f32[4,16,512]{2,1,0:T(8,128)S(1)} %get-tuple-element.12), channel_id=1, source_target_pairs={{0,8},{2,10},{4,12},{6,14},{8,0},{10,2},{12,4},{14,6},{1,9},{3,11}... | collective-permute-start | bytes 393224 | tf_op jit(solution)/shard_map/ppermute | solution.py:199
  34.7 18.5 %collective-permute-start.5 = (f32[4,16,512]{2,1,0:T(8,128)S(1)}, f32[4,16,512]{2,1,0:T(8,128)S(1)}, u32[]{:S(2)}, u32[]{:S(2)}) collective-permute-start(f32[4,16,512]{2,1,0:T(8,128)S(1)} %get-tuple-element.13), channel_id=1, source_target_pairs={{0,6},{2,4},{4,2},{6,0},{8,14},{10,12},{12,10},{14,8},{1,7},{3,5},... | collective-permute-start | bytes 393224 | tf_op jit(solution)/shard_map/ppermute | solution.py:199
  36.1 19.8 %copy-start.1 = (f32[4,16,512]{2,1,0:T(8,128)}, f32[4,16,512]{2,1,0:T(8,128)S(1)}, u32[]{:S(2)}) copy-start(f32[4,16,512]{2,1,0:T(8,128)S(1)} %collective-permute-done.9.refs_7_) | copy-start | bytes 393220
  36.1 19.7 %collective-permute-start.4 = (f32[4,16,512]{2,1,0:T(8,128)S(1)}, f32[4,16,512]{2,1,0:T(8,128)S(1)}, u32[]{:S(2)}, u32[]{:S(2)}) collective-permute-start(f32[4,16,512]{2,1,0:T(8,128)S(1)} %get-tuple-element.14), channel_id=1, source_target_pairs={{0,4},{2,6},{4,0},{6,2},{8,12},{10,14},{12,8},{14,10},{1,5},{3,7},... | collective-permute-start | bytes 393224 | tf_op jit(solution)/shard_map/ppermute | solution.py:199
  48.2 7.7 %copy-start.2 = (f32[4,16,512]{2,1,0:T(8,128)}, f32[4,16,512]{2,1,0:T(8,128)S(1)}, u32[]{:S(2)}) copy-start(f32[4,16,512]{2,1,0:T(8,128)S(1)} %collective-permute-done.8.refs_6_) | copy-start | bytes 393220
  48.2 7.7 %collective-permute-start.3 = (f32[4,16,512]{2,1,0:T(8,128)S(1)}, f32[4,16,512]{2,1,0:T(8,128)S(1)}, u32[]{:S(2)}, u32[]{:S(2)}) collective-permute-start(f32[4,16,512]{2,1,0:T(8,128)S(1)} %get-tuple-element.15), channel_id=1, source_target_pairs={{0,2},{2,0},{4,6},{6,4},{8,10},{10,8},{12,14},{14,12},{1,3},{3,1},... | collective-permute-start | bytes 393224 | tf_op jit(solution)/shard_map/ppermute | solution.py:199
  52.4 3.5 %copy-start.3 = (f32[4,16,512]{2,1,0:T(8,128)}, f32[4,16,512]{2,1,0:T(8,128)S(1)}, u32[]{:S(2)}) copy-start(f32[4,16,512]{2,1,0:T(8,128)S(1)} %collective-permute-done.7.refs_5_) | copy-start | bytes 393220
  53.2 2.7 %copy-start.4 = (f32[4,16,512]{2,1,0:T(8,128)}, f32[4,16,512]{2,1,0:T(8,128)S(1)}, u32[]{:S(2)}) copy-start(f32[4,16,512]{2,1,0:T(8,128)S(1)} %collective-permute-done.6.refs_4_) | copy-start | bytes 393220
  53.2 2.7 %copy-start.5 = (f32[4,16,512]{2,1,0:T(8,128)}, f32[4,16,512]{2,1,0:T(8,128)S(1)}, u32[]{:S(2)}) copy-start(f32[4,16,512]{2,1,0:T(8,128)S(1)} %collective-permute-done.5.refs_3_) | copy-start | bytes 393220
  55.9 0.6 %copy-start.6 = (f32[4,16,512]{2,1,0:T(8,128)}, f32[4,16,512]{2,1,0:T(8,128)S(1)}, u32[]{:S(2)}) copy-start(f32[4,16,512]{2,1,0:T(8,128)S(1)} %collective-permute-done.4.refs_2_) | copy-start | bytes 393220
  55.9 0.7 %copy-start.7 = (f32[4,16,512]{2,1,0:T(8,128)}, f32[4,16,512]{2,1,0:T(8,128)S(1)}, u32[]{:S(2)}) copy-start(f32[4,16,512]{2,1,0:T(8,128)S(1)} %collective-permute-done.3.refs_1_) | copy-start | bytes 393220

commit v2 on v0

v2 whole, which is shorter than its diff:
```python
import functools
import math

import jax
import jax.numpy as jnp
from jax import lax
from jax.experimental import pallas as pl
from jax.experimental.pallas import tpu as pltpu
from jax.sharding import PartitionSpec as P

LANES = 128
TOP = 65535.0
HALF = 32768
LARGEST = 36.0
TAU_STEPS = 32000.0

VMEM = pl.BlockSpec(memory_space=pltpu.VMEM)
SMEM = pl.BlockSpec(memory_space=pltpu.SMEM)
HBM = pl.BlockSpec(memory_space=pltpu.HBM)


def rounds(n):
    return list(range(n - 1, -1, -1))


def partners(n, k):
    if n & (n - 1) == 0:
        return [(i, i ^ k) for i in range(n)]
    return [(i, (i + k) % n) for i in range(n)]


def target(n, me, k):
    if n & (n - 1) == 0:
        return lax.bitwise_xor(me, k)
    return lax.rem(me + k, n)


def source(n, me, k):
    if n & (n - 1) == 0:
        return lax.bitwise_xor(me, k)
    return lax.rem(me + n - k, n)


def mask_at(mask, place, blocks):
    inside = jnp.logical_and(place >= 0, place < blocks)
    kept = mask[0, jnp.clip(place, 0, blocks - 1)]
    return jnp.where(inside, kept, 0)


def columns(place):
    return pl.ds(pl.multiple_of(place * LANES, LANES), LANES)


def edges_kernel(mask_hbm, vol, density, first, last, edge, mask, sem, mask_sem):
    depth, rows, cols = density.shape
    copy = pltpu.make_async_copy(vol.at[0], density, sem)
    copy.start()
    mask_copy = pltpu.make_async_copy(mask_hbm, mask, mask_sem)
    mask_copy.start()
    tile = lax.axis_index("tile")
    row = jnp.where(tile == 0, rows - 1, 0)
    at = lax.broadcasted_iota(jnp.int32, (depth, depth * rows), 1)
    cell = lax.broadcasted_iota(jnp.int32, (depth, depth * rows), 0)
    pick = (at == cell * rows + row).astype(jnp.bfloat16)
    mask_copy.wait()
    copy.wait()
    for b in range(cols // LANES):
        keep = mask[0, b].astype(jnp.float32)
        here = pl.ds(b * LANES, LANES)
        planes = density[:, :, here].reshape(depth * rows, LANES)
        border = jnp.dot(pick, planes, preferred_element_type=jnp.float32)
        edge[:, here] = (border * keep).astype(jnp.bfloat16)
        first[:, here] = (density[0, :, here].astype(jnp.float32) * keep).astype(jnp.bfloat16)
        last[:, here] = (density[depth - 1, :, here].astype(jnp.float32) * keep).astype(
            jnp.bfloat16
        )


def edges(volume, mask):
    channels, depth, rows, cols = volume.shape
    plane = jax.ShapeDtypeStruct((rows, cols), jnp.bfloat16)
    return pl.pallas_call(
        edges_kernel,
        in_specs=[HBM, HBM],
        out_specs=[VMEM] * 4,
        out_shape=[
            jax.ShapeDtypeStruct((depth, rows, cols), jnp.bfloat16),
            plane,
            plane,
            jax.ShapeDtypeStruct((depth, cols), jnp.bfloat16),
        ],
        scratch_shapes=[
            pltpu.SMEM(mask.shape, jnp.int32),
            pltpu.SemaphoreType.DMA,
            pltpu.SemaphoreType.DMA,
        ],
        compiler_params=pltpu.CompilerParams(vmem_limit_bytes=48 * 1024 * 1024),
        cost_estimate=pl.CostEstimate(
            flops=1000000, bytes_accessed=2 * depth * rows * cols, transcendentals=0
        ),
        name="edges",
    )(mask, volume)


def march_kernel(step_size, n, mask, vol, density, border, sums_out, ends):
    depth, rows, cols = density.shape
    blocks = cols // LANES
    bricks = blocks // n
    strip = cols // n
    me, tile = lax.axis_index("depth"), lax.axis_index("tile")
    order = rounds(n)

    lane = lax.broadcasted_iota(jnp.int32, (rows, LANES), 1)
    row = lax.broadcasted_iota(jnp.int32, (rows, LANES), 0)
    first_row, last_row = row == 0, row == rows - 1
    first_lane, last_lane = lane == 0, lane == LANES - 1
    right_half = lane >= LANES // 2
    rate = -step_size * math.log2(math.e)
    to_top = tile.astype(jnp.float32)
    to_bottom = 1.0 - to_top

    def one_brick(place):
        here_at = columns(place)
        left_at = columns(jnp.maximum(place - 1, 0))
        right_at = columns(jnp.minimum(place + 1, blocks - 1))
        keep_left = mask_at(mask, place - 1, blocks).astype(jnp.float32)
        keep_right = mask_at(mask, place + 1, blocks).astype(jnp.float32)
        keep_side = jnp.where(right_half, keep_left, keep_right)
        halo = border[:, here_at].astype(jnp.float32)
        top, bottom = halo * to_top, halo * to_bottom
        zeros = jnp.zeros((rows, LANES), jnp.float32)
        total, clear, plain = zeros, jnp.ones((rows, LANES), jnp.float32), zeros
        sums = [zeros for _ in range(3)]
        before = None
        here = density[0, :, here_at].astype(jnp.float32)
        for d in range(depth):
            after = density[d + 1, :, here_at].astype(jnp.float32) if d + 1 < depth else None
            side = (
                jnp.where(
                    right_half,
                    density[d, :, left_at].astype(jnp.float32),
                    density[d, :, right_at].astype(jnp.float32),
                )
                * keep_side
            )
            less = pltpu.roll(jnp.where(last_lane, side, here), 1, 1)
            more = pltpu.roll(jnp.where(first_lane, side, here), LANES - 1, 1)
            up = jnp.where(first_row, top[d : d + 1], pltpu.roll(here, 1, 0))
            down = jnp.where(last_row, bottom[d : d + 1], pltpu.roll(here, rows - 1, 0))
            g_rows, g_cols = down - up, more - less
            flat = g_rows * g_rows + g_cols * g_cols
            slope = 0.126 * g_rows + 0.168 * g_cols
            total = total + here * here
            left_over = jnp.exp2(total * rate)
            weight = clear - left_over
            clear = left_over
            glow = [jnp.tanh(0.5 * vol[1 + k, d, :, here_at].astype(jnp.float32)) for k in range(3)]
            if before is None or after is None:
                end = 0 if before is None else 1
                ends[end, 0, :, here_at] = after if before is None else before
                ends[end, 1, :, here_at] = flat
                ends[end, 2, :, here_at] = slope
                half = 0.5 * weight
                for k in range(3):
                    ends[end, 3 + k, :, here_at] = half + half * glow[k]
            else:
                g_depth = after - before
                shading = 0.3 + jnp.abs(0.28 * g_depth + slope) * lax.rsqrt(
                    1.0 + 0.25 * (g_depth * g_depth + flat)
                )
                weight = weight * shading
                plain = plain + weight
                for k in range(3):
                    sums[k] = sums[k] + weight * glow[k]
            before, here = here, after
        for k in range(3):
            sums_out[k, :, here_at] = 0.5 * (plain + sums[k])
        sums_out[3, :, here_at] = total

    def one_strip(j, carry):
        at = target(n, me, order[0] - j)

        def maybe(b, inner):
            place = at * bricks + b

            @pl.when(mask[0, place] != 0)
            def _():
                one_brick(place)

            return inner

        lax.fori_loop(0, bricks, maybe, 0)
        return carry

    lax.fori_loop(0, n, one_strip, 0)


def march(volume, density, border, mask, step_size, n):
    channels, depth, rows, cols = volume.shape
    cells = depth * rows * cols
    return pl.pallas_call(
        functools.partial(march_kernel, step_size, n),
        in_specs=[SMEM, VMEM, VMEM, VMEM],
        out_specs=[VMEM] * 2,
        out_shape=[
            jax.ShapeDtypeStruct((4, rows, cols), jnp.float32),
            jax.ShapeDtypeStruct((2, 6, rows, cols), jnp.float32),
        ],
        cost_estimate=pl.CostEstimate(
            flops=40 * cells, bytes_accessed=8 * cells, transcendentals=5 * cells
        ),
        compiler_params=pltpu.CompilerParams(vmem_limit_bytes=20 * 1024 * 1024),
        name="march",
    )(mask, volume, density, border)


def finish_kernel(step_size, depth, n, mask, density, sums, ends, low, high, *outs):
    rows, cols = low.shape
    bricks = cols // LANES // n
    me = lax.axis_index("depth")
    scale = TAU_STEPS / (LARGEST * step_size * depth)

    def one_brick(out, place, b):
        here_at, there = columns(place), columns(b)
        colours = [sums[k, :, here_at] for k in range(3)]
        for end, halo in enumerate((low, high)):
            g_depth = ends[end, 0, :, here_at] - halo[:, here_at].astype(jnp.float32)
            if end == 1:
                g_depth = -g_depth
            flat, slope = ends[end, 1, :, here_at], ends[end, 2, :, here_at]
            shading = 0.3 + jnp.abs(0.28 * g_depth + slope) * lax.rsqrt(
                1.0 + 0.25 * (g_depth * g_depth + flat)
            )
            for k in range(3):
                colours[k] = colours[k] + shading * ends[end, 3 + k, :, here_at]
        ticks = sums[3, :, here_at] * (step_size * scale)
        upper = jnp.minimum(ticks.astype(jnp.int32), HALF - 1)
        lower = jnp.minimum((ticks - upper.astype(jnp.float32)) * (2.0 * HALF), TOP)
        lower = lower.astype(jnp.int32)
        optical = (upper.astype(jnp.float32) + lower.astype(jnp.float32) * (0.5 / HALF)) / scale
        opacity = 1.0 - jnp.exp(-optical)
        gain = TOP / jnp.maximum(opacity, 1e-30)
        for k in range(3):
            level = jnp.minimum(colours[k] * gain + 0.5, TOP)
            out[k, :, there] = (level.astype(jnp.int32) - HALF).astype(jnp.int16)
        out[3, :, there] = (upper).astype(jnp.int16)
        out[4, :, there] = (lower - HALF).astype(jnp.int16)

    for j, k in enumerate(rounds(n)):
        at = target(n, me, k)
        out = outs[j]

        def maybe(b, carry, at=at, out=out):
            place = at * bricks + b
            keep = mask[0, place] != 0

            @pl.when(keep)
            def _():
                one_brick(out, place, b)

            @pl.when(jnp.logical_not(keep))
            def _():
                empty = jnp.full((rows, LANES), -HALF, jnp.int32).astype(jnp.int16)
                for c in range(5):
                    out[c, :, columns(b)] = jnp.zeros((rows, LANES), jnp.int16) if c == 3 else empty

            return carry

        lax.fori_loop(0, bricks, maybe, 0)


def finish(density, sums, ends, low, high, mask, step_size, n):
    depth, rows, cols = density.shape
    strip = cols // n
    return pl.pallas_call(
        functools.partial(finish_kernel, step_size, depth, n),
        in_specs=[SMEM] + [VMEM] * 5,
        out_specs=[VMEM] * n,
        out_shape=[jax.ShapeDtypeStruct((5, rows, strip), jnp.int16)] * n,
        cost_estimate=pl.CostEstimate(
            flops=60 * rows * cols, bytes_accessed=64 * rows * cols, transcendentals=4 * rows * cols
        ),
        compiler_params=pltpu.CompilerParams(vmem_limit_bytes=16 * 1024 * 1024),
        name="finish",
    )(mask, density, sums, ends, low, high)


def composite_kernel(step_size, depth, n, order, *refs):
    parts, out, ranks = refs[:n], refs[n], refs[n + 1]
    me = lax.axis_index("depth")
    scale = TAU_STEPS / (LARGEST * step_size * depth)
    for p in range(n):
        ranks[order[p]] = p
    rank = [ranks[source(n, me, k)] for k in rounds(n)]
    rows, strip = out.shape[1:]
    for b in range(strip // LANES):
        at = pl.ds(b * LANES, LANES)
        optical = [
            (
                part[3, :, at].astype(jnp.float32)
                + (part[4, :, at].astype(jnp.float32) + float(HALF)) * (0.5 / HALF)
            )
            / scale
            for part in parts
        ]
        whole = optical[0]
        for k in range(1, n):
            whole = whole + optical[k]
        picture = [None] * 3
        for k in range(n):
            covered = jnp.zeros_like(whole)
            for e in range(n):
                if e != k:
                    covered = covered + jnp.where(rank[e] < rank[k], 1.0, 0.0) * optical[e]
            share = jnp.exp(-covered) * (1.0 - jnp.exp(-optical[k])) * (1.0 / TOP)
            for c in range(3):
                term = share * (parts[k][c, :, at].astype(jnp.float32) + float(HALF))
                picture[c] = term if k == 0 else picture[c] + term
        for c in range(3):
            out[c, :, at] = picture[c]
        out[3, :, at] = 1.0 - jnp.exp(-whole)


def composite(order, parts, step_size, depth):
    n = len(parts)
    rows, strip = parts[0].shape[1:]
    return pl.pallas_call(
        functools.partial(composite_kernel, step_size, depth, n),
        in_specs=[SMEM] + [VMEM] * n,
        out_specs=VMEM,
        out_shape=jax.ShapeDtypeStruct((4, rows, strip), jnp.float32),
        scratch_shapes=[pltpu.SMEM((n,), jnp.int32)],
        compiler_params=pltpu.CompilerParams(vmem_limit_bytes=16 * 1024 * 1024),
        name="composite",
    )(order, *parts)


def on_device(volume, brick_mask, brick_order):
    channels, depth, rows, cols = volume.shape
    n = lax.axis_size("depth")
    assert lax.axis_size("tile") == 2
    step_size = 3.0 / (depth * n)
    mask = jnp.repeat(brick_mask, cols // brick_mask.shape[1] // LANES, axis=1)

    up = [(i, i + 1) for i in range(n - 1)]
    down = [(i + 1, i) for i in range(n - 1)]
    density, first, last, edge = edges(volume, mask)
    border = lax.ppermute(edge, "tile", [(0, 1), (1, 0)])
    low = lax.ppermute(last, "depth", up)
    high = lax.ppermute(first, "depth", down)
    sums, ends = march(volume, density, border, mask, step_size, n)
    strips = finish(density, sums, ends, low, high, mask, step_size, n)
    parts = [
        lax.ppermute(strip, "depth", partners(n, k)) if k else strip
        for strip, k in zip(strips, rounds(n))
    ]
    picture = composite(brick_order, parts, step_size, depth)
    return lax.all_gather(picture, "tile", axis=1, tiled=True)


def solution(mesh):
    return jax.shard_map(
        on_device,
        mesh=mesh,
        in_specs=(
            P(None, ("parts", "depth"), "tile", None),
            P(("parts", "depth"), None),
            P("parts"),
        ),
        out_specs=P(None, "parts", "depth"),
        check_vma=False,
    )
```

time: 166 us -> 41 us (0.25)
  waiting for transfers between devices: 113 us -> 5.35 us
  other arithmetic: 25.6 us -> 0 us
  between operations: 13.5 us -> 0.08 us
  starting transfers between devices: 8.81 us -> 21.3 us
  Pallas kernels: 0 us -> 10.3 us
    reduce_scatter x1 -> x0, waiting for transfers between devices: 62 us -> none  [on_device(): blended = lax.psum_scatter(terms, 'depth', scatter_dimension=2, tiled=True)]
    all_gather x1 -> x0, waiting for transfers between devices: 42.7 us -> none  [on_device(): gathered = lax.all_gather(optical[None], 'depth', axis=0, tiled=True)]
    ppermute x4 -> x10, starting transfers between devices: 8.77 us -> 21.3 us  [the longest x7 15 us: on_device(): lax.ppermute(strip, 'depth', partners(n, k))]
    pallas_call x0 -> x4, Pallas kernels: none -> 10.3 us  [the longest x1 5.33 us: march(): pl.pallas_call(functools.partial(march_kernel, step_size, n), in_specs=[S...]
    another operation x1 -> x0, other arithmetic: 9.85 us -> none  [march(): through = jnp.cumsum(extinction, axis=0)]
    reduce_sum x3 -> x0, other arithmetic: 8.5 us -> none  [the longest x1 6.51 us: march(): colour = jnp.sum(weights[None] * emitted, axis=1)]
    mul x2 -> x0, other arithmetic: 2.68 us -> none  [the longest x1 1.74 us: on_device(): density = volume[0] * keep_cols[None, None, :]]
    ppermute x4 -> x10, waiting for transfers between devices: 7.73 us -> 5.35 us  [the longest x7 4.65 us: on_device(): lax.ppermute(strip, 'depth', partners(n, k))]
  transfers between devices with their start and end apart: 6 -> 10, of which waited for: 5 -> 3; matrix products, arithmetic and copies ran while one was open for 5% -> 0% of each run, Pallas kernels for 0% -> 13%
where the time goes in v2:
time: 41 us; the launch traced here: 40.5 us
  starting transfers between devices  21.3 us (52%)
  Pallas kernels  10.3 us (25%)
  waiting for transfers between devices  5.35 us (13%)
  blocking collectives  1.99 us (5%)
  local copies, waits for them, and re-layouts  1.51 us (4%)
    ppermute x7, starting transfers between devices, on_device(): lax.ppermute(strip, 'depth', partners(n, k))  15 us
    pallas_call x1, Pallas kernels, march(): pl.pallas_call(functools.partial(march_kernel, step_size, n), in_specs=[S...  5.33 us
    ppermute x7, waiting for transfers between devices, on_device(): lax.ppermute(strip, 'depth', partners(n, k))  4.65 us
    ppermute x1, starting transfers between devices, on_device(): low = lax.ppermute(last, 'depth', up)  4.57 us
    pallas_call x1, Pallas kernels, edges(): pl.pallas_call(edges_kernel, in_specs=[HBM, HBM], out_specs=[VMEM] * 4, o...  2.11 us
    all_gather x1, blocking collectives, on_device(): return lax.all_gather(picture, 'tile', axis=1, tiled=True)  1.99 us
    pallas_call x1, Pallas kernels, finish(): pl.pallas_call(functools.partial(finish_kernel, step_size, depth, n), in_...  1.8 us
    unnamed x7, local copies, waits for them, and re-layouts  1.51 us
  transfers between devices with their start and end apart: 10, of which 3 were waited for; matrix products, arithmetic and copies ran while one was open for 0% of the time, Pallas kernels for 13%

profile of v2, /device:TPU:0, one launch (start us, length us, event | category | flops | bytes accessed | tf_op | source)
XLA Modules:
  0.0 40.5 jit_solution(15783399908604787219)
XLA Ops:
  0.0 0.0 copy-start
  0.0 0.0 copy-start.1
  0.0 0.8 %copy-done.1 = s32[1,32]{1,0:T(1,128)S(1)} copy-done((s32[1,32]{1,0:T(1,128)S(1)}, s32[1,32]{1,0:T(1,128)}, u32[]{:S(2)}) %copy-start.1) | copy-done | bytes 152
  0.8 2.1 %edges.1 = (bf16[16,16,4096]{2,1,0:T(8,128)(2,1)S(1)}, bf16[16,4096]{1,0:T(8,128)(2,1)S(1)}, bf16[16,4096]{1,0:T(8,128)(2,1)S(1)}, bf16[16,4096]{1,0:T(8,128)(2,1)S(1)}) custom-call(s32[1,32]{1,0:T(1,128)S(1)} %copy-done.1, bf16[4,16,16,4096]{3,2,1,0:T(8,128)(2,1)} %vol.3), custom_call_target="tpu_custom_call" | custom-call | flops 1000000 | bytes 2097152 | tf_op jit(solution)/shard_map/edges/pallas_call | solution.py:82
  2.9 0.5 %collective-permute-start = (bf16[16,4096]{1,0:T(8,128)(2,1)S(1)}, bf16[16,4096]{1,0:T(8,128)(2,1)S(1)}, u32[]{:S(2)}, u32[]{:S(2)}) collective-permute-start(bf16[16,4096]{1,0:T(8,128)(2,1)S(1)} %get-tuple-element.20), channel_id=1, source_target_pairs={{0,1},{1,0},{2,3},{3,2},{4,5},{5,4},{6,7},{7,6},{8,9},{9,8},{10,11... | collective-permute-start | bytes 393224 | tf_op jit(solution)/shard_map/ppermute | solution.py:348
  3.4 4.6 %collective-permute-start.1 = (bf16[16,4096]{1,0:T(8,128)(2,1)S(1)}, bf16[16,4096]{1,0:T(8,128)(2,1)S(1)}, u32[]{:S(2)}, u32[]{:S(2)}) collective-permute-start(bf16[16,4096]{1,0:T(8,128)(2,1)S(1)} %get-tuple-element.23), channel_id=1, source_target_pairs={{0,2},{2,4},{4,6},{6,8},{8,10},{10,12},{12,14},{1,3},{3,5},{5,7},{... | collective-permute-start | bytes 393224 | tf_op jit(solution)/shard_map/ppermute | solution.py:349
  8.0 1.3 %collective-permute-start.2 = (bf16[16,4096]{1,0:T(8,128)(2,1)S(1)}, bf16[16,4096]{1,0:T(8,128)(2,1)S(1)}, u32[]{:S(2)}, u32[]{:S(2)}) collective-permute-start(bf16[16,4096]{1,0:T(8,128)(2,1)S(1)} %get-tuple-element.24), channel_id=1, source_target_pairs={{2,0},{4,2},{6,4},{8,6},{10,8},{12,10},{14,12},{3,1},{5,3},{7,5},{... | collective-permute-start | bytes 393224 | tf_op jit(solution)/shard_map/ppermute | solution.py:350
  9.3 0.0 collective-permute-done.border
  9.3 0.0 copy-done
  9.3 5.3 %march.1 = (f32[4,16,4096]{2,1,0:T(8,128)S(1)}, f32[2,6,16,4096]{3,2,1,0:T(8,128)S(1)}) custom-call(s32[1,32]{1,0:T(1,128)S(1)} %copy-done.1, bf16[4,16,16,4096]{3,2,1,0:T(8,128)(2,1)S(1)} %copy-done, bf16[16,16,4096]{2,1,0:T(8,128)(2,1)S(1)} %get-tuple-element.19.density, bf16[16,4096]{1,0:T(8,128)(2,1)S(1)} %collective-permute-done.border), custom_call_target="tpu_custom_call" | custom-call | flops 41943040 | bytes 8388608 | tf_op jit(solution)/shard_map/march/pallas_call | solution.py:201
  14.7 0.0 collective-permute-done.1.low
  14.7 0.7 %collective-permute-done.2.high = bf16[16,4096]{1,0:T(8,128)(2,1)S(1)} collective-permute-done((bf16[16,4096]{1,0:T(8,128)(2,1)S(1)}, bf16[16,4096]{1,0:T(8,128)(2,1)S(1)}, u32[]{:S(2)}, u32[]{:S(2)}) %collective-permute-start.2) | collective-permute-done | bytes 131104 | tf_op jit(solution)/shard_map/ppermute | solution.py:350
  15.4 0.0 copy-start.2
  15.4 1.8 %finish.1 = (s16[5,16,512]{2,1,0:T(8,128)(2,1)S(1)}, s16[5,16,512]{2,1,0:T(8,128)(2,1)S(1)}, s16[5,16,512]{2,1,0:T(8,128)(2,1)S(1)}, s16[5,16,512]{2,1,0:T(8,128...) custom-call(s32[1,32]{1,0:T(1,128)S(1)} %copy-done.1, ...), custom_call_target="tpu_custom_call" | custom-call | flops 3932160 | bytes 4194304 | tf_op jit(solution)/shard_map/finish/pallas_call | solution.py:275
  17.2 5.6 %collective-permute-start.3 = (s16[5,16,512]{2,1,0:T(8,128)(2,1)S(1)}, s16[5,16,512]{2,1,0:T(8,128)(2,1)S(1)}, u32[]{:S(2)}, u32[]{:S(2)}) collective-permute-start(s16[5,16,512]{2,1,0:T(8,128)(2,1)S(1)} %get-tuple-element.25), channel_id=1, source_target_pairs={{0,14},{2,12},{4,10},{6,8},{8,6},{10,4},{12,2},{14,0},{1,15},{3,13... | collective-permute-start | bytes 245768 | tf_op jit(solution)/shard_map/ppermute | solution.py:354
  22.9 0.0 collective-permute-start.4
  22.9 1.0 %collective-permute-start.5 = (s16[5,16,512]{2,1,0:T(8,128)(2,1)S(1)}, s16[5,16,512]{2,1,0:T(8,128)(2,1)S(1)}, u32[]{:S(2)}, u32[]{:S(2)}) collective-permute-start(s16[5,16,512]{2,1,0:T(8,128)(2,1)S(1)} %get-tuple-element.27), channel_id=1, source_target_pairs={{0,10},{2,8},{4,14},{6,12},{8,2},{10,0},{12,6},{14,4},{1,11},{3,9}... | collective-permute-start | bytes 245768 | tf_op jit(solution)/shard_map/ppermute | solution.py:354
  23.8 2.0 %collective-permute-start.6 = (s16[5,16,512]{2,1,0:T(8,128)(2,1)S(1)}, s16[5,16,512]{2,1,0:T(8,128)(2,1)S(1)}, u32[]{:S(2)}, u32[]{:S(2)}) collective-permute-start(s16[5,16,512]{2,1,0:T(8,128)(2,1)S(1)} %get-tuple-element.28), channel_id=1, source_target_pairs={{0,8},{2,10},{4,12},{6,14},{8,0},{10,2},{12,4},{14,6},{1,9},{3,11}... | collective-permute-start | bytes 245768 | tf_op jit(solution)/shard_map/ppermute | solution.py:354
  25.9 2.3 %collective-permute-start.7 = (s16[5,16,512]{2,1,0:T(8,128)(2,1)S(1)}, s16[5,16,512]{2,1,0:T(8,128)(2,1)S(1)}, u32[]{:S(2)}, u32[]{:S(2)}) collective-permute-start(s16[5,16,512]{2,1,0:T(8,128)(2,1)S(1)} %get-tuple-element.29), channel_id=1, source_target_pairs={{0,6},{2,4},{4,2},{6,0},{8,14},{10,12},{12,10},{14,8},{1,7},{3,5},... | collective-permute-start | bytes 245768 | tf_op jit(solution)/shard_map/ppermute | solution.py:354
  28.1 0.0 collective-permute-done.3.refs_0_
  28.2 3.9 %collective-permute-start.8 = (s16[5,16,512]{2,1,0:T(8,128)(2,1)S(1)}, s16[5,16,512]{2,1,0:T(8,128)(2,1)S(1)}, u32[]{:S(2)}, u32[]{:S(2)}) collective-permute-start(s16[5,16,512]{2,1,0:T(8,128)(2,1)S(1)} %get-tuple-element.30), channel_id=1, source_target_pairs={{0,4},{2,6},{4,0},{6,2},{8,12},{10,14},{12,8},{14,10},{1,5},{3,7},... | collective-permute-start | bytes 245768 | tf_op jit(solution)/shard_map/ppermute | solution.py:354
  32.1 0.0 collective-permute-done.4.refs_1_
  32.1 0.1 collective-permute-start.9
  32.2 3.8 %collective-permute-done.5.refs_2_ = s16[5,16,512]{2,1,0:T(8,128)(2,1)S(1)} collective-permute-done((s16[5,16,512]{2,1,0:T(8,128)(2,1)S(1)}, s16[5,16,512]{2,1,0:T(8,128)(2,1)S(1)}, u32[]{:S(2)}, u32[]{:S(2)}) %collective-permute-start.5) | collective-permute-done | bytes 81952 | tf_op jit(solution)/shard_map/ppermute | solution.py:354
  36.0 0.0 collective-permute-done.6.refs_3_
  36.0 0.0 collective-permute-done.7.refs_4_
  36.0 0.8 %collective-permute-done.8.refs_5_ = s16[5,16,512]{2,1,0:T(8,128)(2,1)S(1)} collective-permute-done((s16[5,16,512]{2,1,0:T(8,128)(2,1)S(1)}, s16[5,16,512]{2,1,0:T(8,128)(2,1)S(1)}, u32[]{:S(2)}, u32[]{:S(2)}) %collective-permute-start.8) | collective-permute-done | bytes 81952 | tf_op jit(solution)/shard_map/ppermute | solution.py:354
  36.8 0.0 collective-permute-done.9.refs_6_
  36.8 0.0 copy-done.2
  36.8 1.0 %composite.1 = f32[4,16,512]{2,1,0:T(8,128)S(1)} custom-call(s32[8]{0:T(128)S(1)} %copy-done.2, s16[5,16,512]{2,1,0:T(8,128)(2,1)S(1)} %collective-permute-done.3.refs_0_, s16[5,16,512]{2,1,0:T(8,128)(2,1)S(1)} %collective-permute-done.4.refs_1_, s16[5,16,512]{2,1,0:T(8,128)(2,1)S(1)} %collective-permute-done.5.refs_2_, ...), custom_call_target="tpu_custom_call" | custom-call | tf_op jit(solution)/shard_map/composite/pallas_call | solution.py:327
  37.8 2.0 %all_gather.3 = f32[4,32,512]{2,1,0:T(8,128)S(1)} all-gather(f32[4,16,512]{2,1,0:T(8,128)S(1)} %composite.1), channel_id=1, replica_groups=mesh['parts'=2,'depth'=8,'tile'=2] {'tile'}, dimensions={1}, use_global_device_ids=true | all-gather | bytes 393216 | tf_op jit(solution)/shard_map/all_gather | solution.py:358
  39.8 0.7 %copy.5 = f32[4,32,512]{2,1,0:T(8,128)} copy(f32[4,32,512]{2,1,0:T(8,128)S(1)} %all_gather.3) | data formatting | bytes 524288
Async XLA Ops:
  0.0 9.3 %copy-start = (bf16[4,16,16,4096]{3,2,1,0:T(8,128)(2,1)S(1)}, bf16[4,16,16,4096]{3,2,1,0:T(8,128)(2,1)}, u32[]{:S(2)}) copy-start(bf16[4,16,16,4096]{3,2,1,0:T(8,128)(2,1)} %vol.3) | copy-start | bytes 25165828
  0.0 0.8 %copy-start.1 = (s32[1,32]{1,0:T(1,128)S(1)}, s32[1,32]{1,0:T(1,128)}, u32[]{:S(2)}) copy-start(s32[1,32]{1,0:T(1,128)} %mask.3) | copy-start | bytes 388
  2.9 6.4 %collective-permute-start = (bf16[16,4096]{1,0:T(8,128)(2,1)S(1)}, bf16[16,4096]{1,0:T(8,128)(2,1)S(1)}, u32[]{:S(2)}, u32[]{:S(2)}) collective-permute-start(bf16[16,4096]{1,0:T(8,128)(2,1)S(1)} %get-tuple-element.20), channel_id=1, source_target_pairs={{0,1},{1,0},{2,3},{3,2},{4,5},{5,4},{6,7},{7,6},{8,9},{9,8},{10,11... | collective-permute-start | bytes 393224 | tf_op jit(solution)/shard_map/ppermute | solution.py:348
  3.4 11.2 %collective-permute-start.1 = (bf16[16,4096]{1,0:T(8,128)(2,1)S(1)}, bf16[16,4096]{1,0:T(8,128)(2,1)S(1)}, u32[]{:S(2)}, u32[]{:S(2)}) collective-permute-start(bf16[16,4096]{1,0:T(8,128)(2,1)S(1)} %get-tuple-element.23), channel_id=1, source_target_pairs={{0,2},{2,4},{4,6},{6,8},{8,10},{10,12},{12,14},{1,3},{3,5},{5,7},{... | collective-permute-start | bytes 393224 | tf_op jit(solution)/shard_map/ppermute | solution.py:349
  8.0 7.4 %collective-permute-start.2 = (bf16[16,4096]{1,0:T(8,128)(2,1)S(1)}, bf16[16,4096]{1,0:T(8,128)(2,1)S(1)}, u32[]{:S(2)}, u32[]{:S(2)}) collective-permute-start(bf16[16,4096]{1,0:T(8,128)(2,1)S(1)} %get-tuple-element.24), channel_id=1, source_target_pairs={{2,0},{4,2},{6,4},{8,6},{10,8},{12,10},{14,12},{3,1},{5,3},{7,5},{... | collective-permute-start | bytes 393224 | tf_op jit(solution)/shard_map/ppermute | solution.py:350
  15.4 21.4 %copy-start.2 = (s32[8]{0:T(128)S(1)}, s32[8]{0:T(128)}, u32[]{:S(2)}) copy-start(s32[8]{0:T(128)} %order.1) | copy-start | bytes 100
  17.2 10.9 %collective-permute-start.3 = (s16[5,16,512]{2,1,0:T(8,128)(2,1)S(1)}, s16[5,16,512]{2,1,0:T(8,128)(2,1)S(1)}, u32[]{:S(2)}, u32[]{:S(2)}) collective-permute-start(s16[5,16,512]{2,1,0:T(8,128)(2,1)S(1)} %get-tuple-element.25), channel_id=1, source_target_pairs={{0,14},{2,12},{4,10},{6,8},{8,6},{10,4},{12,2},{14,0},{1,15},{3,13... | collective-permute-start | bytes 245768 | tf_op jit(solution)/shard_map/ppermute | solution.py:354
  22.9 9.2 %collective-permute-start.4 = (s16[5,16,512]{2,1,0:T(8,128)(2,1)S(1)}, s16[5,16,512]{2,1,0:T(8,128)(2,1)S(1)}, u32[]{:S(2)}, u32[]{:S(2)}) collective-permute-start(s16[5,16,512]{2,1,0:T(8,128)(2,1)S(1)} %get-tuple-element.26), channel_id=1, source_target_pairs={{0,12},{2,14},{4,8},{6,10},{8,4},{10,6},{12,0},{14,2},{1,13},{3,15... | collective-permute-start | bytes 245768 | tf_op jit(solution)/shard_map/ppermute | solution.py:354
  22.9 13.1 %collective-permute-start.5 = (s16[5,16,512]{2,1,0:T(8,128)(2,1)S(1)}, s16[5,16,512]{2,1,0:T(8,128)(2,1)S(1)}, u32[]{:S(2)}, u32[]{:S(2)}) collective-permute-start(s16[5,16,512]{2,1,0:T(8,128)(2,1)S(1)} %get-tuple-element.27), channel_id=1, source_target_pairs={{0,10},{2,8},{4,14},{6,12},{8,2},{10,0},{12,6},{14,4},{1,11},{3,9}... | collective-permute-start | bytes 245768 | tf_op jit(solution)/shard_map/ppermute | solution.py:354
  23.8 12.2 %collective-permute-start.6 = (s16[5,16,512]{2,1,0:T(8,128)(2,1)S(1)}, s16[5,16,512]{2,1,0:T(8,128)(2,1)S(1)}, u32[]{:S(2)}, u32[]{:S(2)}) collective-permute-start(s16[5,16,512]{2,1,0:T(8,128)(2,1)S(1)} %get-tuple-element.28), channel_id=1, source_target_pairs={{0,8},{2,10},{4,12},{6,14},{8,0},{10,2},{12,4},{14,6},{1,9},{3,11}... | collective-permute-start | bytes 245768 | tf_op jit(solution)/shard_map/ppermute | solution.py:354
  25.9 10.2 %collective-permute-start.7 = (s16[5,16,512]{2,1,0:T(8,128)(2,1)S(1)}, s16[5,16,512]{2,1,0:T(8,128)(2,1)S(1)}, u32[]{:S(2)}, u32[]{:S(2)}) collective-permute-start(s16[5,16,512]{2,1,0:T(8,128)(2,1)S(1)} %get-tuple-element.29), channel_id=1, source_target_pairs={{0,6},{2,4},{4,2},{6,0},{8,14},{10,12},{12,10},{14,8},{1,7},{3,5},... | collective-permute-start | bytes 245768 | tf_op jit(solution)/shard_map/ppermute | solution.py:354
  28.2 8.7 %collective-permute-start.8 = (s16[5,16,512]{2,1,0:T(8,128)(2,1)S(1)}, s16[5,16,512]{2,1,0:T(8,128)(2,1)S(1)}, u32[]{:S(2)}, u32[]{:S(2)}) collective-permute-start(s16[5,16,512]{2,1,0:T(8,128)(2,1)S(1)} %get-tuple-element.30), channel_id=1, source_target_pairs={{0,4},{2,6},{4,0},{6,2},{8,12},{10,14},{12,8},{14,10},{1,5},{3,7},... | collective-permute-start | bytes 245768 | tf_op jit(solution)/shard_map/ppermute | solution.py:354
  32.1 4.7 %collective-permute-start.9 = (s16[5,16,512]{2,1,0:T(8,128)(2,1)S(1)}, s16[5,16,512]{2,1,0:T(8,128)(2,1)S(1)}, u32[]{:S(2)}, u32[]{:S(2)}) collective-permute-start(s16[5,16,512]{2,1,0:T(8,128)(2,1)S(1)} %get-tuple-element.31), channel_id=1, source_target_pairs={{0,2},{2,0},{4,6},{6,4},{8,10},{10,8},{12,14},{14,12},{1,3},{3,1},... | collective-permute-start | bytes 245768 | tf_op jit(solution)/shard_map/ppermute | solution.py:354

commit v3 on v2

v3 whole, which is shorter than its diff:
```python
import functools
import math

import jax
import jax.numpy as jnp
from jax import lax
from jax.experimental import pallas as pl
from jax.experimental.pallas import tpu as pltpu
from jax.sharding import PartitionSpec as P

LANES = 128
TOP = 65535.0
HALF = 32768
LARGEST = 36.0
TAU_STEPS = 32000.0

VMEM = pl.BlockSpec(memory_space=pltpu.VMEM)
SMEM = pl.BlockSpec(memory_space=pltpu.SMEM)
HBM = pl.BlockSpec(memory_space=pltpu.HBM)


def rounds(n):
    return list(range(n - 1, -1, -1))


def partners(n, k):
    if n & (n - 1) == 0:
        return [(i, i ^ k) for i in range(n)]
    return [(i, (i + k) % n) for i in range(n)]


def target(n, me, k):
    if n & (n - 1) == 0:
        return lax.bitwise_xor(me, k)
    return lax.rem(me + k, n)


def source(n, me, k):
    if n & (n - 1) == 0:
        return lax.bitwise_xor(me, k)
    return lax.rem(me + n - k, n)


def mask_at(mask, place, blocks):
    inside = jnp.logical_and(place >= 0, place < blocks)
    kept = mask[0, jnp.clip(place, 0, blocks - 1)]
    return jnp.where(inside, kept, 0)


def columns(place):
    return pl.ds(pl.multiple_of(place * LANES, LANES), LANES)


def edges_kernel(mask_hbm, vol, density, near, far, edge, mask, sem, mask_sem):
    depth, rows, cols = density.shape
    copy = pltpu.make_async_copy(vol.at[0], density, sem)
    copy.start()
    mask_copy = pltpu.make_async_copy(mask_hbm, mask, mask_sem)
    mask_copy.start()
    row = jnp.where(lax.axis_index("tile") == 0, rows - 1, 0)
    even = lax.rem(lax.axis_index("depth"), 2) == 0
    at = lax.broadcasted_iota(jnp.int32, (depth, depth * rows), 1)
    cell = lax.broadcasted_iota(jnp.int32, (depth, depth * rows), 0)
    pick = (at == cell * rows + row).astype(jnp.bfloat16)
    mask_copy.wait()
    copy.wait()
    for b in range(cols // LANES):
        keep = mask[0, b].astype(jnp.float32)
        here = pl.ds(b * LANES, LANES)
        planes = density[:, :, here].reshape(depth * rows, LANES)
        border = jnp.dot(pick, planes, preferred_element_type=jnp.float32)
        edge[:, here] = (border * keep).astype(jnp.bfloat16)
        first = density[0, :, here].astype(jnp.float32) * keep
        last = density[depth - 1, :, here].astype(jnp.float32) * keep
        near[:, here] = jnp.where(even, last, first).astype(jnp.bfloat16)
        far[:, here] = jnp.where(even, first, last).astype(jnp.bfloat16)


def edges(volume, mask):
    channels, depth, rows, cols = volume.shape
    plane = jax.ShapeDtypeStruct((rows, cols), jnp.bfloat16)
    return pl.pallas_call(
        edges_kernel,
        in_specs=[HBM, HBM],
        out_specs=[VMEM] * 4 + [SMEM],
        out_shape=[
            jax.ShapeDtypeStruct((depth, rows, cols), jnp.bfloat16),
            plane,
            plane,
            jax.ShapeDtypeStruct((depth, cols), jnp.bfloat16),
            jax.ShapeDtypeStruct(mask.shape, jnp.int32),
        ],
        scratch_shapes=[pltpu.SemaphoreType.DMA, pltpu.SemaphoreType.DMA],
        compiler_params=pltpu.CompilerParams(vmem_limit_bytes=48 * 1024 * 1024),
        cost_estimate=pl.CostEstimate(
            flops=1000000, bytes_accessed=2 * depth * rows * cols, transcendentals=0
        ),
        name="edges",
    )(mask, volume)


def shade(g_depth, flat, slope):
    return 0.3 + jnp.abs(0.28 * g_depth + slope) * lax.rsqrt(1.0 + 0.25 * (g_depth * g_depth + flat))


def halves(even, near, far, where):
    near = near[:, where].astype(jnp.float32)
    far = far[:, where].astype(jnp.float32)
    return jnp.where(even, far, near), jnp.where(even, near, far)


def march_brick(step_size, vol, density, border, mask, place, planes, put_end, put):
    depth, rows, cols = density.shape
    blocks = cols // LANES
    lane = lax.broadcasted_iota(jnp.int32, (rows, LANES), 1)
    row = lax.broadcasted_iota(jnp.int32, (rows, LANES), 0)
    first_row, last_row = row == 0, row == rows - 1
    first_lane, last_lane = lane == 0, lane == LANES - 1
    right_half = lane >= LANES // 2
    rate = -step_size * math.log2(math.e)
    to_top = lax.axis_index("tile").astype(jnp.float32)
    here_at = columns(place)
    left_at = columns(jnp.maximum(place - 1, 0))
    right_at = columns(jnp.minimum(place + 1, blocks - 1))
    keep_left = mask_at(mask, place - 1, blocks).astype(jnp.float32)
    keep_right = mask_at(mask, place + 1, blocks).astype(jnp.float32)
    keep_side = jnp.where(right_half, keep_left, keep_right)
    halo = border[:, here_at].astype(jnp.float32)
    top, bottom = halo * to_top, halo * (1.0 - to_top)
    zeros = jnp.zeros((rows, LANES), jnp.float32)
    total, clear, plain = zeros, jnp.ones((rows, LANES), jnp.float32), zeros
    sums = [zeros for _ in range(3)]
    before = planes[0] if planes else None
    here = density[0, :, here_at].astype(jnp.float32)
    for d in range(depth):
        if d + 1 < depth:
            after = density[d + 1, :, here_at].astype(jnp.float32)
        else:
            after = planes[1] if planes else None
        left = density[d, :, left_at].astype(jnp.float32)
        right = density[d, :, right_at].astype(jnp.float32)
        side = jnp.where(right_half, left, right) * keep_side
        less = pltpu.roll(jnp.where(last_lane, side, here), 1, 1)
        more = pltpu.roll(jnp.where(first_lane, side, here), LANES - 1, 1)
        up = jnp.where(first_row, top[d : d + 1], pltpu.roll(here, 1, 0))
        down = jnp.where(last_row, bottom[d : d + 1], pltpu.roll(here, rows - 1, 0))
        g_rows, g_cols = down - up, more - less
        flat = g_rows * g_rows + g_cols * g_cols
        slope = 0.126 * g_rows + 0.168 * g_cols
        total = total + here * here
        left_over = jnp.exp2(total * rate)
        weight = clear - left_over
        clear = left_over
        glow = [jnp.tanh(0.5 * vol[1 + k, d, :, here_at].astype(jnp.float32)) for k in range(3)]
        if before is None or after is None:
            inner = after if before is None else before
            half = 0.5 * weight
            put_end(0 if d == 0 else 1, [inner, flat, slope] + [half + half * g for g in glow])
        else:
            weight = weight * shade(after - before, flat, slope)
            plain = plain + weight
            for k in range(3):
                sums[k] = sums[k] + weight * glow[k]
        before, here = here, after
    put([0.5 * (plain + sums[k]) for k in range(3)], total)


def scale_of(step_size, depth):
    return TAU_STEPS / (LARGEST * step_size * depth)


def encode(out, there, colours, total, step_size, depth):
    scale = scale_of(step_size, depth)
    ticks = total * (step_size * scale)
    upper = jnp.minimum(ticks.astype(jnp.int32), HALF - 1)
    lower = jnp.minimum((ticks - upper.astype(jnp.float32)) * (2.0 * HALF), TOP).astype(jnp.int32)
    optical = (upper.astype(jnp.float32) + lower.astype(jnp.float32) * (0.5 / HALF)) * (1.0 / scale)
    opacity = 1.0 - jnp.exp(-optical)
    gain = TOP / jnp.maximum(opacity, 1e-30)
    for k in range(3):
        level = jnp.minimum(colours[k] * gain + 0.5, TOP)
        out[k, :, there] = (level.astype(jnp.int32) - HALF).astype(jnp.int16)
    out[3, :, there] = upper.astype(jnp.int16)
    out[4, :, there] = (lower - HALF).astype(jnp.int16)


def far_kernel(step_size, n, ks, mask, vol, density, border, sums_out, ends):
    depth, rows, cols = density.shape
    bricks = cols // LANES // n
    me = lax.axis_index("depth")

    def step(i, carry):
        place = target(n, me, ks[0] - i // bricks) * bricks + i % bricks
        here = columns(i)

        def put_end(end, values):
            for v, value in enumerate(values):
                ends[end, v, :, here] = value

        def put(colours, total):
            for v, value in enumerate(colours + [total]):
                sums_out[v, :, here] = value

        keep = mask[0, place] != 0

        @pl.when(keep)
        def _():
            march_brick(
                step_size, vol, density, border, mask, place, None, put_end, put
            )

        @pl.when(jnp.logical_not(keep))
        def _():
            empty = jnp.zeros((rows, LANES), jnp.float32)
            put([empty] * 3, empty)
            put_end(0, [empty] * 6)
            put_end(1, [empty] * 6)

        return carry

    lax.fori_loop(0, len(ks) * bricks, step, 0)


def costs(cells):
    return pl.CostEstimate(flops=40 * cells, bytes_accessed=8 * cells, transcendentals=5 * cells)


def march_far(volume, density, border, mask, step_size, n, ks):
    channels, depth, rows, cols = volume.shape
    width = cols // n * len(ks)
    return pl.pallas_call(
        functools.partial(far_kernel, step_size, n, ks),
        in_specs=[SMEM, VMEM, VMEM, VMEM],
        out_specs=[VMEM] * 2,
        out_shape=[
            jax.ShapeDtypeStruct((4, rows, width), jnp.float32),
            jax.ShapeDtypeStruct((2, 6, rows, width), jnp.float32),
        ],
        cost_estimate=costs(depth * rows * width),
        compiler_params=pltpu.CompilerParams(vmem_limit_bytes=20 * 1024 * 1024),
        name="march_far",
    )(mask, volume, density, border)


def finish_kernel(step_size, depth, n, ks, sums, ends, near, far, *outs):
    rows, cols = near.shape
    strip = cols // n
    width = math.gcd(strip, 2 * LANES)
    me = lax.axis_index("depth")
    even = lax.rem(me, 2) == 0
    for j, k in enumerate(ks):
        at = target(n, me, k) * strip
        for c in range(strip // width):
            here = pl.ds(j * strip + c * width, width)
            planes = halves(
                even, near, far, pl.ds(pl.multiple_of(at + c * width, LANES), width)
            )
            colours = [sums[v, :, here] for v in range(3)]
            for end in range(2):
                g_depth = ends[end, 0, :, here] - planes[end]
                if end == 1:
                    g_depth = -g_depth
                shading = shade(g_depth, ends[end, 1, :, here], ends[end, 2, :, here])
                for v in range(3):
                    colours[v] = colours[v] + shading * ends[end, 3 + v, :, here]
            encode(outs[j], pl.ds(c * width, width), colours, sums[3, :, here], step_size, depth)


def finish(sums, ends, near, far, step_size, depth, n, ks):
    rows, cols = near.shape
    cells = rows * cols // n * len(ks)
    return pl.pallas_call(
        functools.partial(finish_kernel, step_size, depth, n, ks),
        in_specs=[VMEM] * 4,
        out_specs=[VMEM] * len(ks),
        out_shape=[jax.ShapeDtypeStruct((5, rows, cols // n), jnp.int16)] * len(ks),
        cost_estimate=pl.CostEstimate(
            flops=60 * cells, bytes_accessed=64 * cells, transcendentals=4 * cells
        ),
        compiler_params=pltpu.CompilerParams(vmem_limit_bytes=16 * 1024 * 1024),
        name="finish",
    )(sums, ends, near, far)


def near_kernel(step_size, n, ks, mask, vol, density, border, near, far, *outs):
    depth, rows, cols = density.shape
    bricks = cols // LANES // n
    me = lax.axis_index("depth")
    even = lax.rem(me, 2) == 0
    for k, out in zip(ks, outs):
        at = target(n, me, k)

        def step(b, carry, at=at, out=out):
            place = at * bricks + b
            there = columns(b)
            keep = mask[0, place] != 0

            @pl.when(keep)
            def _():
                planes = halves(even, near, far, columns(place))

                def put(colours, total):
                    encode(out, there, colours, total, step_size, depth)

                march_brick(
                    step_size, vol, density, border, mask, place, planes, None, put
                )

            @pl.when(jnp.logical_not(keep))
            def _():
                low = jnp.full((rows, LANES), -HALF, jnp.int32).astype(jnp.int16)
                for c in range(5):
                    out[c, :, there] = jnp.zeros((rows, LANES), jnp.int16) if c == 3 else low

            return carry

        lax.fori_loop(0, bricks, step, 0)


def march_near(volume, density, border, near, far, mask, step_size, n, ks):
    channels, depth, rows, cols = volume.shape
    width = cols // n * len(ks)
    return pl.pallas_call(
        functools.partial(near_kernel, step_size, n, ks),
        in_specs=[SMEM] + [VMEM] * 5,
        out_specs=[VMEM] * len(ks),
        out_shape=[jax.ShapeDtypeStruct((5, rows, cols // n), jnp.int16)] * len(ks),
        cost_estimate=costs(depth * rows * width),
        compiler_params=pltpu.CompilerParams(vmem_limit_bytes=20 * 1024 * 1024),
        name="march_near",
    )(mask, volume, density, border, near, far)


def composite_kernel(step_size, depth, n, order, *refs):
    parts, out, ranks = refs[:n], refs[n], refs[n + 1]
    me = lax.axis_index("depth")
    scale = scale_of(step_size, depth)
    for p in range(n):
        ranks[order[p]] = p
    rank = [ranks[source(n, me, k)] for k in rounds(n)]
    rows, strip = out.shape[1:]
    for b in range(strip // LANES):
        at = pl.ds(b * LANES, LANES)
        optical = [
            (
                part[3, :, at].astype(jnp.float32)
                + (part[4, :, at].astype(jnp.float32) + float(HALF)) * (0.5 / HALF)
            )
            * (1.0 / scale)
            for part in parts
        ]
        whole = optical[0]
        for k in range(1, n):
            whole = whole + optical[k]
        picture = [None] * 3
        for k in range(n):
            covered = jnp.zeros_like(whole)
            for e in range(n):
                if e != k:
                    covered = covered + jnp.where(rank[e] < rank[k], 1.0, 0.0) * optical[e]
            share = jnp.exp(-covered) * (1.0 - jnp.exp(-optical[k])) * (1.0 / TOP)
            for c in range(3):
                term = share * (parts[k][c, :, at].astype(jnp.float32) + float(HALF))
                picture[c] = term if k == 0 else picture[c] + term
        for c in range(3):
            out[c, :, at] = picture[c]
        out[3, :, at] = 1.0 - jnp.exp(-whole)


def composite(order, parts, step_size, depth):
    n = len(parts)
    rows, strip = parts[0].shape[1:]
    return pl.pallas_call(
        functools.partial(composite_kernel, step_size, depth, n),
        in_specs=[SMEM] + [VMEM] * n,
        out_specs=VMEM,
        out_shape=jax.ShapeDtypeStruct((4, rows, strip), jnp.float32),
        scratch_shapes=[pltpu.SMEM((n,), jnp.int32)],
        compiler_params=pltpu.CompilerParams(vmem_limit_bytes=16 * 1024 * 1024),
        name="composite",
    )(order, *parts)


def on_device(volume, brick_mask, brick_order):
    channels, depth, rows, cols = volume.shape
    n = lax.axis_size("depth")
    assert lax.axis_size("tile") == 2
    step_size = 3.0 / (depth * n)
    mask = jnp.repeat(brick_mask, cols // brick_mask.shape[1] // LANES, axis=1)

    density, near, far, edge, mask = edges(volume, mask)
    border = lax.ppermute(edge, "tile", [(0, 1), (1, 0)])
    pairs = [(i, i ^ 1) for i in range(n) if i ^ 1 < n]
    near = lax.ppermute(near, "depth", pairs)
    pairs = [(i, i + 1) for i in range(1, n - 1, 2)]
    far = lax.ppermute(far, "depth", pairs + [(b, a) for a, b in pairs])

    first, second = rounds(n)[: n // 2], rounds(n)[n // 2 :]
    sums, ends = march_far(volume, density, border, mask, step_size, n, first)
    strips = finish(sums, ends, near, far, step_size, depth, n, first)
    strips, mask = lax.optimization_barrier((strips, mask))
    strips = list(strips) + list(
        march_near(volume, density, border, near, far, mask, step_size, n, second)
    )
    parts = [
        lax.ppermute(strip, "depth", partners(n, k)) if k else strip
        for strip, k in zip(strips, rounds(n))
    ]
    picture = composite(brick_order, parts, step_size, depth)
    return lax.all_gather(picture, "tile", axis=1, tiled=True)


def solution(mesh):
    return jax.shard_map(
        on_device,
        mesh=mesh,
        in_specs=(
            P(None, ("parts", "depth"), "tile", None),
            P(("parts", "depth"), None),
            P("parts"),
        ),
        out_specs=P(None, "parts", "depth"),
        check_vma=False,
    )
```

time: 41 us -> 37.8 us (0.922)
  Pallas kernels: 10.3 us -> 9.08 us
  starting transfers between devices: 21.3 us -> 20.1 us
    ppermute x2, starting transfers between devices: 5.86 us -> 3.25 us  [the longest x1 2.59 us: on_device(): near = lax.ppermute(near, 'depth', pairs)]
    ppermute x7, starting transfers between devices: 15 us -> 16.3 us  [on_device(): lax.ppermute(strip, 'depth', partners(n, k))]
    pallas_call x3 -> x4, Pallas kernels: 9.25 us -> 8.06 us  [the longest x1 2.58 us: edges(): pl.pallas_call(edges_kernel, in_specs=[HBM, HBM], out_specs=[VMEM] * 4 +...]
    ppermute x7, waiting for transfers between devices: 4.65 us -> 4.23 us  [on_device(): lax.ppermute(strip, 'depth', partners(n, k))]
  transfers between devices with their start and end apart: 10 -> 10, of which waited for: 3 -> 5; matrix products, arithmetic and copies ran while one was open for 0% -> 0% of each run, Pallas kernels for 13% -> 14%
where the time goes in v3:
time: 37.8 us; the launch traced here: 37.6 us
  starting transfers between devices  20.1 us (53%)
  Pallas kernels  9.08 us (24%)
  waiting for transfers between devices  5.07 us (13%)
  blocking collectives  1.99 us (5%)
  local copies, waits for them, and re-layouts  1.37 us (4%)
    ppermute x7, starting transfers between devices, on_device(): lax.ppermute(strip, 'depth', partners(n, k))  16.3 us
    ppermute x7, waiting for transfers between devices, on_device(): lax.ppermute(strip, 'depth', partners(n, k))  4.23 us
    ppermute x1, starting transfers between devices, on_device(): near = lax.ppermute(near, 'depth', pairs)  2.59 us
    pallas_call x1, Pallas kernels, edges(): pl.pallas_call(edges_kernel, in_specs=[HBM, HBM], out_specs=[VMEM] * 4 +...  2.58 us
    pallas_call x1, Pallas kernels, march_far(): pl.pallas_call(functools.partial(far_kernel, step_size, n, ks), in_specs=...  2.56 us
    pallas_call x1, Pallas kernels, march_near(): pl.pallas_call(functools.partial(near_kernel, step_size, n, ks), in_specs...  2.55 us
    all_gather x1, blocking collectives, on_device(): return lax.all_gather(picture, 'tile', axis=1, tiled=True)  1.99 us
    unnamed x7, local copies, waits for them, and re-layouts  1.37 us
  transfers between devices with their start and end apart: 10, of which 5 were waited for; matrix products, arithmetic and copies ran while one was open for 0% of the time, Pallas kernels for 14%

profile of v3, /device:TPU:0, one launch (start us, length us, event | category | flops | bytes accessed | tf_op | source)
XLA Modules:
  0.0 37.6 jit_solution(2460808722825854269)
XLA Ops:
  0.0 0.0 copy-start.1
  0.0 0.7 %copy-done.1 = s32[1,32]{1,0:T(1,128)S(1)} copy-done((s32[1,32]{1,0:T(1,128)S(1)}, s32[1,32]{1,0:T(1,128)}, u32[]{:S(2)}) %copy-start.1) | copy-done | bytes 152
  0.7 0.0 copy-start
  0.7 2.6 %edges.1 = (bf16[16,16,4096]{2,1,0:T(8,128)(2,1)S(1)}, bf16[16,4096]{1,0:T(8,128)(2,1)S(1)}, bf16[16,4096]{1,0:T(8,128)(2,1)S(1)}, bf16[16,4096]{1,0:T(8,128)(2,1)S(1)}, s32[1,32]{1,0:T(1,128)S(1)}) custom-call(s32[1,32]{1,0:T(1,128)S(1)} %copy-done.1, bf16[4,16,16,4096]{3,2,1,0:T(8,128)(2,1)} %vol.5), custom_call_target="tpu_custom_call" | custom-call | flops 1000000 | bytes 2097152 | tf_op jit(solution)/shard_map/edges/pallas_call | solution.py:82
  3.3 0.5 %collective-permute-start = (bf16[16,4096]{1,0:T(8,128)(2,1)S(1)}, bf16[16,4096]{1,0:T(8,128)(2,1)S(1)}, u32[]{:S(2)}, u32[]{:S(2)}) collective-permute-start(bf16[16,4096]{1,0:T(8,128)(2,1)S(1)} %get-tuple-element.27), channel_id=1, source_target_pairs={{0,1},{1,0},{2,3},{3,2},{4,5},{5,4},{6,7},{7,6},{8,9},{9,8},{10,11... | collective-permute-start | bytes 393224 | tf_op jit(solution)/shard_map/ppermute | solution.py:392
  3.8 2.6 %collective-permute-start.1 = (bf16[16,4096]{1,0:T(8,128)(2,1)S(1)}, bf16[16,4096]{1,0:T(8,128)(2,1)S(1)}, u32[]{:S(2)}, u32[]{:S(2)}) collective-permute-start(bf16[16,4096]{1,0:T(8,128)(2,1)S(1)} %get-tuple-element.30), channel_id=1, source_target_pairs={{0,2},{2,0},{4,6},{6,4},{8,10},{10,8},{12,14},{14,12},{1,3},{3,1},... | collective-permute-start | bytes 393224 | tf_op jit(solution)/shard_map/ppermute | solution.py:394
  6.4 0.7 %collective-permute-start.2 = (bf16[16,4096]{1,0:T(8,128)(2,1)S(1)}, bf16[16,4096]{1,0:T(8,128)(2,1)S(1)}, u32[]{:S(2)}, u32[]{:S(2)}) collective-permute-start(bf16[16,4096]{1,0:T(8,128)(2,1)S(1)} %get-tuple-element.31), channel_id=1, source_target_pairs={{2,4},{6,8},{10,12},{4,2},{8,6},{12,10},{3,5},{7,9},{11,13},{5,3},... | collective-permute-start | bytes 393224 | tf_op jit(solution)/shard_map/ppermute | solution.py:396
  7.0 0.0 collective-permute-done.border
  7.0 0.0 copy-done
  7.0 2.6 %march_far.1 = (f32[4,16,2048]{2,1,0:T(8,128)S(1)}, f32[2,6,16,2048]{3,2,1,0:T(8,128)S(1)}) custom-call(s32[1,32]{1,0:T(1,128)S(1)} %get-tuple-element.40.mask, bf16[4,16,16,4096]{3,2,1,0:T(8,128)(2,1)S(1)} %copy-done, bf16[16,16,4096]{2,1,0:T(8,128)(2,1)S(1)} %get-tuple-element.26.density, bf16[16,4096]{1,0:T(8,128)(2,1)S(1)} %collective-permute-done.border), custom_call_target="tpu_custom_call" | custom-call | flops 20971520 | bytes 4194304 | tf_op jit(solution)/shard_map/march_far/pallas_call | solution.py:231
  9.6 0.8 %collective-permute-done.1.near = bf16[16,4096]{1,0:T(8,128)(2,1)S(1)} collective-permute-done((bf16[16,4096]{1,0:T(8,128)(2,1)S(1)}, bf16[16,4096]{1,0:T(8,128)(2,1)S(1)}, u32[]{:S(2)}, u32[]{:S(2)}) %collective-permute-start.1) | collective-permute-done | bytes 131104 | tf_op jit(solution)/shard_map/ppermute | solution.py:394
  10.5 0.0 collective-permute-done.2.far
  10.5 0.4 finish.1
  10.8 0.0 copy-start.2
  10.8 4.9 %collective-permute-start.3 = (s16[5,16,512]{2,1,0:T(8,128)(2,1)S(1)}, s16[5,16,512]{2,1,0:T(8,128)(2,1)S(1)}, u32[]{:S(2)}, u32[]{:S(2)}) collective-permute-start(s16[5,16,512]{2,1,0:T(8,128)(2,1)S(1)} %get-tuple-element.36), channel_id=1, source_target_pairs={{0,14},{2,12},{4,10},{6,8},{8,6},{10,4},{12,2},{14,0},{1,15},{3,13... | collective-permute-start | bytes 245768 | tf_op jit(solution)/shard_map/ppermute | solution.py:406
  15.7 3.1 %collective-permute-start.4 = (s16[5,16,512]{2,1,0:T(8,128)(2,1)S(1)}, s16[5,16,512]{2,1,0:T(8,128)(2,1)S(1)}, u32[]{:S(2)}, u32[]{:S(2)}) collective-permute-start(s16[5,16,512]{2,1,0:T(8,128)(2,1)S(1)} %get-tuple-element.37), channel_id=1, source_target_pairs={{0,12},{2,14},{4,8},{6,10},{8,4},{10,6},{12,0},{14,2},{1,13},{3,15... | collective-permute-start | bytes 245768 | tf_op jit(solution)/shard_map/ppermute | solution.py:406
  18.8 1.8 %collective-permute-start.5 = (s16[5,16,512]{2,1,0:T(8,128)(2,1)S(1)}, s16[5,16,512]{2,1,0:T(8,128)(2,1)S(1)}, u32[]{:S(2)}, u32[]{:S(2)}) collective-permute-start(s16[5,16,512]{2,1,0:T(8,128)(2,1)S(1)} %get-tuple-element.38), channel_id=1, source_target_pairs={{0,10},{2,8},{4,14},{6,12},{8,2},{10,0},{12,6},{14,4},{1,11},{3,9}... | collective-permute-start | bytes 245768 | tf_op jit(solution)/shard_map/ppermute | solution.py:406
  20.7 1.9 %collective-permute-start.6 = (s16[5,16,512]{2,1,0:T(8,128)(2,1)S(1)}, s16[5,16,512]{2,1,0:T(8,128)(2,1)S(1)}, u32[]{:S(2)}, u32[]{:S(2)}) collective-permute-start(s16[5,16,512]{2,1,0:T(8,128)(2,1)S(1)} %get-tuple-element.39), channel_id=1, source_target_pairs={{0,8},{2,10},{4,12},{6,14},{8,0},{10,2},{12,4},{14,6},{1,9},{3,11}... | collective-permute-start | bytes 245768 | tf_op jit(solution)/shard_map/ppermute | solution.py:406
  22.6 2.5 %march_near.1 = (s16[5,16,512]{2,1,0:T(8,128)(2,1)S(1)}, s16[5,16,512]{2,1,0:T(8,128)(2,1)S(1)}, s16[5,16,512]{2,1,0:T(8,128)(2,1)S(1)}, s16[5,16,512]{2,1,0:T(8,128)(2,1)S(1)}) custom-call(s32[1,32]{1,0:T(1,128)S(1)} %get-tuple-element.40.mask, bf16[4,16,16,4096]{3,2,1,0:T(8,128)(2,1)S(1)} %copy-done, bf16[16,16,4096]{2,1,0:T(8,128)(2,1)S(1)} %get-tuple-element.26.density, ...), custom_call_target="tpu_custom_call" | custom-call | flops 20971520 | bytes 4194304 | tf_op jit(solution)/shard_map/march_near/pallas_call | solution.py:323
  25.1 2.4 %collective-permute-start.7 = (s16[5,16,512]{2,1,0:T(8,128)(2,1)S(1)}, s16[5,16,512]{2,1,0:T(8,128)(2,1)S(1)}, u32[]{:S(2)}, u32[]{:S(2)}) collective-permute-start(s16[5,16,512]{2,1,0:T(8,128)(2,1)S(1)} %get-tuple-element.41), channel_id=1, source_target_pairs={{0,6},{2,4},{4,2},{6,0},{8,14},{10,12},{12,10},{14,8},{1,7},{3,5},... | collective-permute-start | bytes 245768 | tf_op jit(solution)/shard_map/ppermute | solution.py:406
  27.5 0.0 collective-permute-done.3.refs_0_
  27.5 0.0 collective-permute-start.8
  27.5 0.0 collective-permute-done.4.refs_1_
  27.5 2.2 %collective-permute-start.9 = (s16[5,16,512]{2,1,0:T(8,128)(2,1)S(1)}, s16[5,16,512]{2,1,0:T(8,128)(2,1)S(1)}, u32[]{:S(2)}, u32[]{:S(2)}) collective-permute-start(s16[5,16,512]{2,1,0:T(8,128)(2,1)S(1)} %get-tuple-element.43), channel_id=1, source_target_pairs={{0,2},{2,0},{4,6},{6,4},{8,10},{10,8},{12,14},{14,12},{1,3},{3,1},... | collective-permute-start | bytes 245768 | tf_op jit(solution)/shard_map/ppermute | solution.py:406
  29.7 1.3 %collective-permute-done.5.refs_2_ = s16[5,16,512]{2,1,0:T(8,128)(2,1)S(1)} collective-permute-done((s16[5,16,512]{2,1,0:T(8,128)(2,1)S(1)}, s16[5,16,512]{2,1,0:T(8,128)(2,1)S(1)}, u32[]{:S(2)}, u32[]{:S(2)}) %collective-permute-start.5) | collective-permute-done | bytes 81952 | tf_op jit(solution)/shard_map/ppermute | solution.py:406
  31.0 1.4 %collective-permute-done.6.refs_3_ = s16[5,16,512]{2,1,0:T(8,128)(2,1)S(1)} collective-permute-done((s16[5,16,512]{2,1,0:T(8,128)(2,1)S(1)}, s16[5,16,512]{2,1,0:T(8,128)(2,1)S(1)}, u32[]{:S(2)}, u32[]{:S(2)}) %collective-permute-start.6) | collective-permute-done | bytes 81952 | tf_op jit(solution)/shard_map/ppermute | solution.py:406
  32.3 0.7 %collective-permute-done.7.refs_4_ = s16[5,16,512]{2,1,0:T(8,128)(2,1)S(1)} collective-permute-done((s16[5,16,512]{2,1,0:T(8,128)(2,1)S(1)}, s16[5,16,512]{2,1,0:T(8,128)(2,1)S(1)}, u32[]{:S(2)}, u32[]{:S(2)}) %collective-permute-start.7) | collective-permute-done | bytes 81952 | tf_op jit(solution)/shard_map/ppermute | solution.py:406
  33.0 0.9 %collective-permute-done.8.refs_5_ = s16[5,16,512]{2,1,0:T(8,128)(2,1)S(1)} collective-permute-done((s16[5,16,512]{2,1,0:T(8,128)(2,1)S(1)}, s16[5,16,512]{2,1,0:T(8,128)(2,1)S(1)}, u32[]{:S(2)}, u32[]{:S(2)}) %collective-permute-start.8) | collective-permute-done | bytes 81952 | tf_op jit(solution)/shard_map/ppermute | solution.py:406
  33.9 0.0 collective-permute-done.9.refs_6_
  33.9 0.0 copy-done.2
  33.9 1.0 %composite.1 = f32[4,16,512]{2,1,0:T(8,128)S(1)} custom-call(s32[8]{0:T(128)S(1)} %copy-done.2, s16[5,16,512]{2,1,0:T(8,128)(2,1)S(1)} %collective-permute-done.3.refs_0_, s16[5,16,512]{2,1,0:T(8,128)(2,1)S(1)} %collective-permute-done.4.refs_1_, s16[5,16,512]{2,1,0:T(8,128)(2,1)S(1)} %collective-permute-done.5.refs_2_, ...), custom_call_target="tpu_custom_call" | custom-call | tf_op jit(solution)/shard_map/composite/pallas_call | solution.py:373
  34.9 2.0 %all_gather.3 = f32[4,32,512]{2,1,0:T(8,128)S(1)} all-gather(f32[4,16,512]{2,1,0:T(8,128)S(1)} %composite.1), channel_id=1, replica_groups=mesh['parts'=2,'depth'=8,'tile'=2] {'tile'}, dimensions={1}, use_global_device_ids=true | all-gather | bytes 393216 | tf_op jit(solution)/shard_map/all_gather | solution.py:410
  36.9 0.7 %copy.5 = f32[4,32,512]{2,1,0:T(8,128)} copy(f32[4,32,512]{2,1,0:T(8,128)S(1)} %all_gather.3) | data formatting | bytes 524288
Async XLA Ops:
  0.0 0.7 %copy-start.1 = (s32[1,32]{1,0:T(1,128)S(1)}, s32[1,32]{1,0:T(1,128)}, u32[]{:S(2)}) copy-start(s32[1,32]{1,0:T(1,128)} %mask_hbm.1) | copy-start | bytes 388
  0.7 6.4 %copy-start = (bf16[4,16,16,4096]{3,2,1,0:T(8,128)(2,1)S(1)}, bf16[4,16,16,4096]{3,2,1,0:T(8,128)(2,1)}, u32[]{:S(2)}) copy-start(bf16[4,16,16,4096]{3,2,1,0:T(8,128)(2,1)} %vol.5) | copy-start | bytes 25165828
  3.3 3.8 %collective-permute-start = (bf16[16,4096]{1,0:T(8,128)(2,1)S(1)}, bf16[16,4096]{1,0:T(8,128)(2,1)S(1)}, u32[]{:S(2)}, u32[]{:S(2)}) collective-permute-start(bf16[16,4096]{1,0:T(8,128)(2,1)S(1)} %get-tuple-element.27), channel_id=1, source_target_pairs={{0,1},{1,0},{2,3},{3,2},{4,5},{5,4},{6,7},{7,6},{8,9},{9,8},{10,11... | collective-permute-start | bytes 393224 | tf_op jit(solution)/shard_map/ppermute | solution.py:392
  3.8 6.7 %collective-permute-start.1 = (bf16[16,4096]{1,0:T(8,128)(2,1)S(1)}, bf16[16,4096]{1,0:T(8,128)(2,1)S(1)}, u32[]{:S(2)}, u32[]{:S(2)}) collective-permute-start(bf16[16,4096]{1,0:T(8,128)(2,1)S(1)} %get-tuple-element.30), channel_id=1, source_target_pairs={{0,2},{2,0},{4,6},{6,4},{8,10},{10,8},{12,14},{14,12},{1,3},{3,1},... | collective-permute-start | bytes 393224 | tf_op jit(solution)/shard_map/ppermute | solution.py:394
  6.4 4.1 %collective-permute-start.2 = (bf16[16,4096]{1,0:T(8,128)(2,1)S(1)}, bf16[16,4096]{1,0:T(8,128)(2,1)S(1)}, u32[]{:S(2)}, u32[]{:S(2)}) collective-permute-start(bf16[16,4096]{1,0:T(8,128)(2,1)S(1)} %get-tuple-element.31), channel_id=1, source_target_pairs={{2,4},{6,8},{10,12},{4,2},{8,6},{12,10},{3,5},{7,9},{11,13},{5,3},... | collective-permute-start | bytes 393224 | tf_op jit(solution)/shard_map/ppermute | solution.py:396
  10.8 23.1 %copy-start.2 = (s32[8]{0:T(128)S(1)}, s32[8]{0:T(128)}, u32[]{:S(2)}) copy-start(s32[8]{0:T(128)} %order.1) | copy-start | bytes 100
  10.8 16.7 %collective-permute-start.3 = (s16[5,16,512]{2,1,0:T(8,128)(2,1)S(1)}, s16[5,16,512]{2,1,0:T(8,128)(2,1)S(1)}, u32[]{:S(2)}, u32[]{:S(2)}) collective-permute-start(s16[5,16,512]{2,1,0:T(8,128)(2,1)S(1)} %get-tuple-element.36), channel_id=1, source_target_pairs={{0,14},{2,12},{4,10},{6,8},{8,6},{10,4},{12,2},{14,0},{1,15},{3,13... | collective-permute-start | bytes 245768 | tf_op jit(solution)/shard_map/ppermute | solution.py:406
  15.7 11.8 %collective-permute-start.4 = (s16[5,16,512]{2,1,0:T(8,128)(2,1)S(1)}, s16[5,16,512]{2,1,0:T(8,128)(2,1)S(1)}, u32[]{:S(2)}, u32[]{:S(2)}) collective-permute-start(s16[5,16,512]{2,1,0:T(8,128)(2,1)S(1)} %get-tuple-element.37), channel_id=1, source_target_pairs={{0,12},{2,14},{4,8},{6,10},{8,4},{10,6},{12,0},{14,2},{1,13},{3,15... | collective-permute-start | bytes 245768 | tf_op jit(solution)/shard_map/ppermute | solution.py:406
  18.8 12.1 %collective-permute-start.5 = (s16[5,16,512]{2,1,0:T(8,128)(2,1)S(1)}, s16[5,16,512]{2,1,0:T(8,128)(2,1)S(1)}, u32[]{:S(2)}, u32[]{:S(2)}) collective-permute-start(s16[5,16,512]{2,1,0:T(8,128)(2,1)S(1)} %get-tuple-element.38), channel_id=1, source_target_pairs={{0,10},{2,8},{4,14},{6,12},{8,2},{10,0},{12,6},{14,4},{1,11},{3,9}... | collective-permute-start | bytes 245768 | tf_op jit(solution)/shard_map/ppermute | solution.py:406
  20.7 11.7 %collective-permute-start.6 = (s16[5,16,512]{2,1,0:T(8,128)(2,1)S(1)}, s16[5,16,512]{2,1,0:T(8,128)(2,1)S(1)}, u32[]{:S(2)}, u32[]{:S(2)}) collective-permute-start(s16[5,16,512]{2,1,0:T(8,128)(2,1)S(1)} %get-tuple-element.39), channel_id=1, source_target_pairs={{0,8},{2,10},{4,12},{6,14},{8,0},{10,2},{12,4},{14,6},{1,9},{3,11}... | collective-permute-start | bytes 245768 | tf_op jit(solution)/shard_map/ppermute | solution.py:406
  25.1 7.9 %collective-permute-start.7 = (s16[5,16,512]{2,1,0:T(8,128)(2,1)S(1)}, s16[5,16,512]{2,1,0:T(8,128)(2,1)S(1)}, u32[]{:S(2)}, u32[]{:S(2)}) collective-permute-start(s16[5,16,512]{2,1,0:T(8,128)(2,1)S(1)} %get-tuple-element.41), channel_id=1, source_target_pairs={{0,6},{2,4},{4,2},{6,0},{8,14},{10,12},{12,10},{14,8},{1,7},{3,5},... | collective-permute-start | bytes 245768 | tf_op jit(solution)/shard_map/ppermute | solution.py:406
  27.5 6.4 %collective-permute-start.8 = (s16[5,16,512]{2,1,0:T(8,128)(2,1)S(1)}, s16[5,16,512]{2,1,0:T(8,128)(2,1)S(1)}, u32[]{:S(2)}, u32[]{:S(2)}) collective-permute-start(s16[5,16,512]{2,1,0:T(8,128)(2,1)S(1)} %get-tuple-element.42), channel_id=1, source_target_pairs={{0,4},{2,6},{4,0},{6,2},{8,12},{10,14},{12,8},{14,10},{1,5},{3,7},... | collective-permute-start | bytes 245768 | tf_op jit(solution)/shard_map/ppermute | solution.py:406
  27.5 6.4 %collective-permute-start.9 = (s16[5,16,512]{2,1,0:T(8,128)(2,1)S(1)}, s16[5,16,512]{2,1,0:T(8,128)(2,1)S(1)}, u32[]{:S(2)}, u32[]{:S(2)}) collective-permute-start(s16[5,16,512]{2,1,0:T(8,128)(2,1)S(1)} %get-tuple-element.43), channel_id=1, source_target_pairs={{0,2},{2,0},{4,6},{6,4},{8,10},{10,8},{12,14},{14,12},{1,3},{3,1},... | collective-permute-start | bytes 245768 | tf_op jit(solution)/shard_map/ppermute | solution.py:406

commit v4 on v3

--- a/solution.py
+++ b/solution.py
@@ -11,8 +11,6 @@
 LANES = 128
 TOP = 65535.0
 HALF = 32768
-LARGEST = 36.0
-TAU_STEPS = 32000.0
 
 VMEM = pl.BlockSpec(memory_space=pltpu.VMEM)
 SMEM = pl.BlockSpec(memory_space=pltpu.SMEM)
@@ -162,26 +160,23 @@
             for k in range(3):
                 sums[k] = sums[k] + weight * glow[k]
         before, here = here, after
-    put([0.5 * (plain + sums[k]) for k in range(3)], total)
-
-
-def scale_of(step_size, depth):
-    return TAU_STEPS / (LARGEST * step_size * depth)
-
-
-def encode(out, there, colours, total, step_size, depth):
-    scale = scale_of(step_size, depth)
-    ticks = total * (step_size * scale)
-    upper = jnp.minimum(ticks.astype(jnp.int32), HALF - 1)
-    lower = jnp.minimum((ticks - upper.astype(jnp.float32)) * (2.0 * HALF), TOP).astype(jnp.int32)
-    optical = (upper.astype(jnp.float32) + lower.astype(jnp.float32) * (0.5 / HALF)) * (1.0 / scale)
-    opacity = 1.0 - jnp.exp(-optical)
-    gain = TOP / jnp.maximum(opacity, 1e-30)
+    put([0.5 * (plain + sums[k]) for k in range(3)], clear)
+
+
+def encode(out, there, colours, clear):
+    root = jnp.sqrt(jnp.sqrt(jnp.sqrt(1.0 - clear)))
+    level = (root * TOP + 0.5).astype(jnp.int32)
+    out[3, :, there] = (level - HALF).astype(jnp.int16)
+    gain = TOP / jnp.maximum(eighth_power(level.astype(jnp.float32) * (1.0 / TOP)), 1e-30)
     for k in range(3):
         level = jnp.minimum(colours[k] * gain + 0.5, TOP)
         out[k, :, there] = (level.astype(jnp.int32) - HALF).astype(jnp.int16)
-    out[3, :, there] = upper.astype(jnp.int16)
-    out[4, :, there] = (lower - HALF).astype(jnp.int16)
+
+
+def eighth_power(root):
+    square = root * root
+    square = square * square
+    return square * square
 
 
 def far_kernel(step_size, n, ks, mask, vol, density, border, sums_out, ends):
@@ -190,15 +185,15 @@
     me = lax.axis_index("depth")
 
     def step(i, carry):
-        place = target(n, me, ks[0] - i // bricks) * bricks + i % bricks
+        place = target(n, me, lax.select(i // bricks < n // 2, n - 1 - i // bricks, 0)) * bricks + i % bricks
         here = columns(i)
 
         def put_end(end, values):
             for v, value in enumerate(values):
                 ends[end, v, :, here] = value
 
-        def put(colours, total):
-            for v, value in enumerate(colours + [total]):
+        def put(colours, clear):
+            for v, value in enumerate(colours + [clear]):
                 sums_out[v, :, here] = value
 
         keep = mask[0, place] != 0
@@ -212,7 +207,7 @@
         @pl.when(jnp.logical_not(keep))
         def _():
             empty = jnp.zeros((rows, LANES), jnp.float32)
-            put([empty] * 3, empty)
+            put([empty] * 3, empty + 1.0)
             put_end(0, [empty] * 6)
             put_end(1, [empty] * 6)
 
@@ -242,7 +237,7 @@
     )(mask, volume, density, border)
 
 
-def finish_kernel(step_size, depth, n, ks, sums, ends, near, far, *outs):
+def finish_kernel(n, ks, sums, ends, near, far, *outs):
     rows, cols = near.shape
     strip = cols // n
     width = math.gcd(strip, 2 * LANES)
@@ -263,17 +258,17 @@
                 shading = shade(g_depth, ends[end, 1, :, here], ends[end, 2, :, here])
                 for v in range(3):
                     colours[v] = colours[v] + shading * ends[end, 3 + v, :, here]
-            encode(outs[j], pl.ds(c * width, width), colours, sums[3, :, here], step_size, depth)
-
-
-def finish(sums, ends, near, far, step_size, depth, n, ks):
+            encode(outs[j], pl.ds(c * width, width), colours, sums[3, :, here])
+
+
+def finish(sums, ends, near, far, n, ks):
     rows, cols = near.shape
     cells = rows * cols // n * len(ks)
     return pl.pallas_call(
-        functools.partial(finish_kernel, step_size, depth, n, ks),
+        functools.partial(finish_kernel, n, ks),
         in_specs=[VMEM] * 4,
         out_specs=[VMEM] * len(ks),
-        out_shape=[jax.ShapeDtypeStruct((5, rows, cols // n), jnp.int16)] * len(ks),
+        out_shape=[jax.ShapeDtypeStruct((4, rows, cols // n), jnp.int16)] * len(ks),
         cost_estimate=pl.CostEstimate(
             flops=60 * cells, bytes_accessed=64 * cells, transcendentals=4 * cells
         ),
@@ -299,8 +294,8 @@
             def _():
                 planes = halves(even, near, far, columns(place))
 
-                def put(colours, total):
-                    encode(out, there, colours, total, step_size, depth)
+                def put(colours, clear):
+                    encode(out, there, colours, clear)
 
                 march_brick(
                     step_size, vol, density, border, mask, place, planes, None, put
@@ -309,8 +304,8 @@
             @pl.when(jnp.logical_not(keep))
             def _():
                 low = jnp.full((rows, LANES), -HALF, jnp.int32).astype(jnp.int16)
-                for c in range(5):
-                    out[c, :, there] = jnp.zeros((rows, LANES), jnp.int16) if c == 3 else low
+                for c in range(4):
+                    out[c, :, there] = low
 
             return carry
 
@@ -324,54 +319,50 @@
         functools.partial(near_kernel, step_size, n, ks),
         in_specs=[SMEM] + [VMEM] * 5,
         out_specs=[VMEM] * len(ks),
-        out_shape=[jax.ShapeDtypeStruct((5, rows, cols // n), jnp.int16)] * len(ks),
+        out_shape=[jax.ShapeDtypeStruct((4, rows, cols // n), jnp.int16)] * len(ks),
         cost_estimate=costs(depth * rows * width),
         compiler_params=pltpu.CompilerParams(vmem_limit_bytes=20 * 1024 * 1024),
         name="march_near",
     )(mask, volume, density, border, near, far)
 
 
-def composite_kernel(step_size, depth, n, order, *refs):
+def composite_kernel(ks, order, *refs):
+    n = len(ks)
     parts, out, ranks = refs[:n], refs[n], refs[n + 1]
     me = lax.axis_index("depth")
-    scale = scale_of(step_size, depth)
     for p in range(n):
         ranks[order[p]] = p
-    rank = [ranks[source(n, me, k)] for k in rounds(n)]
+    rank = [ranks[source(n, me, k)] for k in ks]
+    before = [[jnp.where(a < b, 1.0, 0.0) for a in rank] for b in rank]
     rows, strip = out.shape[1:]
     for b in range(strip // LANES):
         at = pl.ds(b * LANES, LANES)
-        optical = [
-            (
-                part[3, :, at].astype(jnp.float32)
-                + (part[4, :, at].astype(jnp.float32) + float(HALF)) * (0.5 / HALF)
-            )
-            * (1.0 / scale)
+        opacity = [
+            eighth_power((part[3, :, at].astype(jnp.float32) + float(HALF)) * (1.0 / TOP))
             for part in parts
         ]
-        whole = optical[0]
+        whole = opacity[0]
         for k in range(1, n):
-            whole = whole + optical[k]
+            whole = whole + opacity[k] * (1.0 - whole)
         picture = [None] * 3
         for k in range(n):
-            covered = jnp.zeros_like(whole)
+            share = opacity[k] * (1.0 / TOP)
             for e in range(n):
                 if e != k:
-                    covered = covered + jnp.where(rank[e] < rank[k], 1.0, 0.0) * optical[e]
-            share = jnp.exp(-covered) * (1.0 - jnp.exp(-optical[k])) * (1.0 / TOP)
+                    share = share * (1.0 - before[k][e] * opacity[e])
             for c in range(3):
                 term = share * (parts[k][c, :, at].astype(jnp.float32) + float(HALF))
                 picture[c] = term if k == 0 else picture[c] + term
         for c in range(3):
             out[c, :, at] = picture[c]
-        out[3, :, at] = 1.0 - jnp.exp(-whole)
-
-
-def composite(order, parts, step_size, depth):
+        out[3, :, at] = whole
+
+
+def composite(order, parts, ks):
     n = len(parts)
     rows, strip = parts[0].shape[1:]
     return pl.pallas_call(
-        functools.partial(composite_kernel, step_size, depth, n),
+        functools.partial(composite_kernel, ks),
         in_specs=[SMEM] + [VMEM] * n,
         out_specs=VMEM,
         out_shape=jax.ShapeDtypeStruct((4, rows, strip), jnp.float32),
@@ -395,18 +386,18 @@
     pairs = [(i, i + 1) for i in range(1, n - 1, 2)]
     far = lax.ppermute(far, "depth", pairs + [(b, a) for a, b in pairs])
 
-    first, second = rounds(n)[: n // 2], rounds(n)[n // 2 :]
+    first, second = rounds(n)[: n // 2] + [0], rounds(n)[n // 2 : -1]
     sums, ends = march_far(volume, density, border, mask, step_size, n, first)
-    strips = finish(sums, ends, near, far, step_size, depth, n, first)
+    strips = finish(sums, ends, near, far, n, first)
     strips, mask = lax.optimization_barrier((strips, mask))
     strips = list(strips) + list(
         march_near(volume, density, border, near, far, mask, step_size, n, second)
     )
     parts = [
         lax.ppermute(strip, "depth", partners(n, k)) if k else strip
-        for strip, k in zip(strips, rounds(n))
+        for strip, k in zip(strips, first + second)
     ]
-    picture = composite(brick_order, parts, step_size, depth)
+    picture = composite(brick_order, parts, first + second)
     return lax.all_gather(picture, "tile", axis=1, tiled=True)
 
 

time: 37.8 us -> 36.1 us (0.955)
  waiting for transfers between devices: 5.07 us -> 3.71 us
  starting transfers between devices: 20.1 us -> 19.1 us
  Pallas kernels: 9.08 us -> 9.84 us
    ppermute x7, starting transfers between devices: 16.3 us -> 15.3 us  [on_device(): lax.ppermute(strip, 'depth', partners(n, k))]
    ppermute x7, waiting for transfers between devices: 4.23 us -> 3.51 us  [on_device(): lax.ppermute(strip, 'depth', partners(n, k))]
    pallas_call x1, Pallas kernels: 2.56 us -> 3.21 us  [march_far(): pl.pallas_call(functools.partial(far_kernel, step_size, n, ks), in_specs=...]
    ppermute x1, waiting for transfers between devices: 0.84 us -> 0.19 us  [on_device(): near = lax.ppermute(near, 'depth', pairs)]
  transfers between devices with their start and end apart: 10 -> 10, of which waited for: 5 -> 5; matrix products, arithmetic and copies ran while one was open for 0% -> 0% of each run, Pallas kernels for 14% -> 16%
where the time goes in v4:
time: 36.1 us
  starting transfers between devices  19.1 us (53%)
  Pallas kernels  9.84 us (27%)
  waiting for transfers between devices  3.71 us (10%)
  blocking collectives  1.99 us (6%)
  local copies, waits for them, and re-layouts  1.37 us (4%)
    ppermute x7, starting transfers between devices, on_device(): lax.ppermute(strip, 'depth', partners(n, k))  15.3 us
    ppermute x7, waiting for transfers between devices, on_device(): lax.ppermute(strip, 'depth', partners(n, k))  3.51 us
    pallas_call x1, Pallas kernels, march_far(): pl.pallas_call(functools.partial(far_kernel, step_size, n, ks), in_specs=...  3.21 us
    ppermute x1, starting transfers between devices, on_device(): near = lax.ppermute(near, 'depth', pairs)  2.59 us
    pallas_call x1, Pallas kernels, edges(): pl.pallas_call(edges_kernel, in_specs=[HBM, HBM], out_specs=[VMEM] * 4 +...  2.58 us
    pallas_call x1, Pallas kernels, march_near(): pl.pallas_call(functools.partial(near_kernel, step_size, n, ks), in_specs...  2.57 us
    all_gather x1, blocking collectives, on_device(): return lax.all_gather(picture, 'tile', axis=1, tiled=True)  1.99 us
    unnamed x7, local copies, waits for them, and re-layouts  1.37 us
  transfers between devices with their start and end apart: 10, of which 5 were waited for; matrix products, arithmetic and copies ran while one was open for 0% of the time, Pallas kernels for 16%

profile of v4, /device:TPU:0, one launch (start us, length us, event | category | flops | bytes accessed | tf_op | source)
XLA Modules:
  0.0 36.1 jit_solution(960177205585906237)
XLA Ops:
  0.0 0.0 copy-start.1
  0.0 0.7 %copy-done.1 = s32[1,32]{1,0:T(1,128)S(1)} copy-done((s32[1,32]{1,0:T(1,128)S(1)}, s32[1,32]{1,0:T(1,128)}, u32[]{:S(2)}) %copy-start.1) | copy-done | bytes 152
  0.7 0.0 copy-start
  0.7 2.6 %edges.1 = (bf16[16,16,4096]{2,1,0:T(8,128)(2,1)S(1)}, bf16[16,4096]{1,0:T(8,128)(2,1)S(1)}, bf16[16,4096]{1,0:T(8,128)(2,1)S(1)}, bf16[16,4096]{1,0:T(8,128)(2,1)S(1)}, s32[1,32]{1,0:T(1,128)S(1)}) custom-call(s32[1,32]{1,0:T(1,128)S(1)} %copy-done.1, bf16[4,16,16,4096]{3,2,1,0:T(8,128)(2,1)} %vol.5), custom_call_target="tpu_custom_call" | custom-call | flops 1000000 | bytes 2097152 | tf_op jit(solution)/shard_map/edges/pallas_call | solution.py:80
  3.3 0.5 %collective-permute-start = (bf16[16,4096]{1,0:T(8,128)(2,1)S(1)}, bf16[16,4096]{1,0:T(8,128)(2,1)S(1)}, u32[]{:S(2)}, u32[]{:S(2)}) collective-permute-start(bf16[16,4096]{1,0:T(8,128)(2,1)S(1)} %get-tuple-element.28), channel_id=1, source_target_pairs={{0,1},{1,0},{2,3},{3,2},{4,5},{5,4},{6,7},{7,6},{8,9},{9,8},{10,11... | collective-permute-start | bytes 393224 | tf_op jit(solution)/shard_map/ppermute | solution.py:383
  3.8 2.6 %collective-permute-start.1 = (bf16[16,4096]{1,0:T(8,128)(2,1)S(1)}, bf16[16,4096]{1,0:T(8,128)(2,1)S(1)}, u32[]{:S(2)}, u32[]{:S(2)}) collective-permute-start(bf16[16,4096]{1,0:T(8,128)(2,1)S(1)} %get-tuple-element.31), channel_id=1, source_target_pairs={{0,2},{2,0},{4,6},{6,4},{8,10},{10,8},{12,14},{14,12},{1,3},{3,1},... | collective-permute-start | bytes 393224 | tf_op jit(solution)/shard_map/ppermute | solution.py:385
  6.4 0.7 %collective-permute-start.2 = (bf16[16,4096]{1,0:T(8,128)(2,1)S(1)}, bf16[16,4096]{1,0:T(8,128)(2,1)S(1)}, u32[]{:S(2)}, u32[]{:S(2)}) collective-permute-start(bf16[16,4096]{1,0:T(8,128)(2,1)S(1)} %get-tuple-element.32), channel_id=1, source_target_pairs={{2,4},{6,8},{10,12},{4,2},{8,6},{12,10},{3,5},{7,9},{11,13},{5,3},... | collective-permute-start | bytes 393224 | tf_op jit(solution)/shard_map/ppermute | solution.py:387
  7.0 0.0 collective-permute-done.border
  7.0 0.0 copy-done
  7.0 3.2 %march_far.1 = (f32[4,16,2560]{2,1,0:T(8,128)S(1)}, f32[2,6,16,2560]{3,2,1,0:T(8,128)S(1)}) custom-call(s32[1,32]{1,0:T(1,128)S(1)} %get-tuple-element.43.mask, bf16[4,16,16,4096]{3,2,1,0:T(8,128)(2,1)S(1)} %copy-done, bf16[16,16,4096]{2,1,0:T(8,128)(2,1)S(1)} %get-tuple-element.27.density, bf16[16,4096]{1,0:T(8,128)(2,1)S(1)} %collective-permute-done.border), custom_call_target="tpu_custom_call" | custom-call | flops 26214400 | bytes 5242880 | tf_op jit(solution)/shard_map/march_far/pallas_call | solution.py:226
  10.3 0.2 collective-permute-done.1.near
  10.5 0.0 collective-permute-done.2.far
  10.5 0.5 %finish.1 = (s16[4,16,512]{2,1,0:T(8,128)(2,1)S(1)}, s16[4,16,512]{2,1,0:T(8,128)(2,1)S(1)}, s16[4,16,512]{2,1,0:T(8,128)(2,1)S(1)}, s16[4,16,512]{2,1,0:T(8,128)(2,1)S(1)}, s16[4,16,512]{2,1,0:T(8,128)(2,1)S(1)}) custom-call(f32[4,16,2560]{2,1,0:T(8,128)S(1)} %get-tuple-element.29.sums, f32[2,6,16,2560]{3,2,1,0:T(8,128)S(1)} %get-tuple-element.30.ends, ...), custom_call_target="tpu_custom_call" | custom-call | flops 2457600 | bytes 2621440 | tf_op jit(solution)/shard_map/finish/pallas_call | solution.py:267
  11.0 0.0 copy-start.2
  11.0 5.0 %collective-permute-start.3 = (s16[4,16,512]{2,1,0:T(8,128)(2,1)S(1)}, s16[4,16,512]{2,1,0:T(8,128)(2,1)S(1)}, u32[]{:S(2)}, u32[]{:S(2)}) collective-permute-start(s16[4,16,512]{2,1,0:T(8,128)(2,1)S(1)} %get-tuple-element.38), channel_id=1, source_target_pairs={{0,14},{2,12},{4,10},{6,8},{8,6},{10,4},{12,2},{14,0},{1,15},{3,13... | collective-permute-start | bytes 196616 | tf_op jit(solution)/shard_map/ppermute | solution.py:397
  16.0 3.4 %collective-permute-start.4 = (s16[4,16,512]{2,1,0:T(8,128)(2,1)S(1)}, s16[4,16,512]{2,1,0:T(8,128)(2,1)S(1)}, u32[]{:S(2)}, u32[]{:S(2)}) collective-permute-start(s16[4,16,512]{2,1,0:T(8,128)(2,1)S(1)} %get-tuple-element.39), channel_id=1, source_target_pairs={{0,12},{2,14},{4,8},{6,10},{8,4},{10,6},{12,0},{14,2},{1,13},{3,15... | collective-permute-start | bytes 196616 | tf_op jit(solution)/shard_map/ppermute | solution.py:397
  19.4 1.4 %collective-permute-start.5 = (s16[4,16,512]{2,1,0:T(8,128)(2,1)S(1)}, s16[4,16,512]{2,1,0:T(8,128)(2,1)S(1)}, u32[]{:S(2)}, u32[]{:S(2)}) collective-permute-start(s16[4,16,512]{2,1,0:T(8,128)(2,1)S(1)} %get-tuple-element.40), channel_id=1, source_target_pairs={{0,10},{2,8},{4,14},{6,12},{8,2},{10,0},{12,6},{14,4},{1,11},{3,9}... | collective-permute-start | bytes 196616 | tf_op jit(solution)/shard_map/ppermute | solution.py:397
  20.8 1.9 %collective-permute-start.6 = (s16[4,16,512]{2,1,0:T(8,128)(2,1)S(1)}, s16[4,16,512]{2,1,0:T(8,128)(2,1)S(1)}, u32[]{:S(2)}, u32[]{:S(2)}) collective-permute-start(s16[4,16,512]{2,1,0:T(8,128)(2,1)S(1)} %get-tuple-element.41), channel_id=1, source_target_pairs={{0,8},{2,10},{4,12},{6,14},{8,0},{10,2},{12,4},{14,6},{1,9},{3,11}... | collective-permute-start | bytes 196616 | tf_op jit(solution)/shard_map/ppermute | solution.py:397
  22.7 2.6 %march_near.1 = (s16[4,16,512]{2,1,0:T(8,128)(2,1)S(1)}, s16[4,16,512]{2,1,0:T(8,128)(2,1)S(1)}, s16[4,16,512]{2,1,0:T(8,128)(2,1)S(1)}) custom-call(s32[1,32]{1,0:T(1,128)S(1)} %get-tuple-element.43.mask, bf16[4,16,16,4096]{3,2,1,0:T(8,128)(2,1)S(1)} %copy-done, bf16[16,16,4096]{2,1,0:T(8,128)(2,1)S(1)} %get-tuple-element.27.density, ...), custom_call_target="tpu_custom_call" | custom-call | flops 15728640 | bytes 3145728 | tf_op jit(solution)/shard_map/march_near/pallas_call | solution.py:318
  25.3 2.4 %collective-permute-start.7 = (s16[4,16,512]{2,1,0:T(8,128)(2,1)S(1)}, s16[4,16,512]{2,1,0:T(8,128)(2,1)S(1)}, u32[]{:S(2)}, u32[]{:S(2)}) collective-permute-start(s16[4,16,512]{2,1,0:T(8,128)(2,1)S(1)} %get-tuple-element.44), channel_id=1, source_target_pairs={{0,6},{2,4},{4,2},{6,0},{8,14},{10,12},{12,10},{14,8},{1,7},{3,5},... | collective-permute-start | bytes 196616 | tf_op jit(solution)/shard_map/ppermute | solution.py:397
  27.7 0.0 collective-permute-done.3.refs_0_
  27.7 0.2 collective-permute-start.8
  27.9 0.0 collective-permute-done.4.refs_1_
  27.9 1.0 %collective-permute-start.9 = (s16[4,16,512]{2,1,0:T(8,128)(2,1)S(1)}, s16[4,16,512]{2,1,0:T(8,128)(2,1)S(1)}, u32[]{:S(2)}, u32[]{:S(2)}) collective-permute-start(s16[4,16,512]{2,1,0:T(8,128)(2,1)S(1)} %get-tuple-element.46), channel_id=1, source_target_pairs={{0,2},{2,0},{4,6},{6,4},{8,10},{10,8},{12,14},{14,12},{1,3},{3,1},... | collective-permute-start | bytes 196616 | tf_op jit(solution)/shard_map/ppermute | solution.py:397
  28.9 0.2 collective-permute-done.5.refs_2_
  29.1 1.3 %collective-permute-done.6.refs_3_ = s16[4,16,512]{2,1,0:T(8,128)(2,1)S(1)} collective-permute-done((s16[4,16,512]{2,1,0:T(8,128)(2,1)S(1)}, s16[4,16,512]{2,1,0:T(8,128)(2,1)S(1)}, u32[]{:S(2)}, u32[]{:S(2)}) %collective-permute-start.6) | collective-permute-done | bytes 65568 | tf_op jit(solution)/shard_map/ppermute | solution.py:397
  30.4 1.3 %collective-permute-done.7.refs_5_ = s16[4,16,512]{2,1,0:T(8,128)(2,1)S(1)} collective-permute-done((s16[4,16,512]{2,1,0:T(8,128)(2,1)S(1)}, s16[4,16,512]{2,1,0:T(8,128)(2,1)S(1)}, u32[]{:S(2)}, u32[]{:S(2)}) %collective-permute-start.7) | collective-permute-done | bytes 65568 | tf_op jit(solution)/shard_map/ppermute | solution.py:397
  31.7 0.7 %collective-permute-done.8.refs_6_ = s16[4,16,512]{2,1,0:T(8,128)(2,1)S(1)} collective-permute-done((s16[4,16,512]{2,1,0:T(8,128)(2,1)S(1)}, s16[4,16,512]{2,1,0:T(8,128)(2,1)S(1)}, u32[]{:S(2)}, u32[]{:S(2)}) %collective-permute-start.8) | collective-permute-done | bytes 65568 | tf_op jit(solution)/shard_map/ppermute | solution.py:397
  32.4 0.0 collective-permute-done.9.refs_7_
  32.4 0.0 copy-done.2
  32.4 1.0 %composite.1 = f32[4,16,512]{2,1,0:T(8,128)S(1)} custom-call(s32[8]{0:T(128)S(1)} %copy-done.2, s16[4,16,512]{2,1,0:T(8,128)(2,1)S(1)} %collective-permute-done.3.refs_0_, s16[4,16,512]{2,1,0:T(8,128)(2,1)S(1)} %collective-permute-done.4.refs_1_, s16[4,16,512]{2,1,0:T(8,128)(2,1)S(1)} %collective-permute-done.5.refs_2_, ...), custom_call_target="tpu_custom_call" | custom-call | tf_op jit(solution)/shard_map/composite/pallas_call | solution.py:364
  33.4 2.0 %all_gather.3 = f32[4,32,512]{2,1,0:T(8,128)S(1)} all-gather(f32[4,16,512]{2,1,0:T(8,128)S(1)} %composite.1), channel_id=1, replica_groups=mesh['parts'=2,'depth'=8,'tile'=2] {'tile'}, dimensions={1}, use_global_device_ids=true | all-gather | bytes 393216 | tf_op jit(solution)/shard_map/all_gather | solution.py:401
  35.3 0.7 %copy.5 = f32[4,32,512]{2,1,0:T(8,128)} copy(f32[4,32,512]{2,1,0:T(8,128)S(1)} %all_gather.3) | data formatting | bytes 524288
Async XLA Ops:
  0.0 0.7 %copy-start.1 = (s32[1,32]{1,0:T(1,128)S(1)}, s32[1,32]{1,0:T(1,128)}, u32[]{:S(2)}) copy-start(s32[1,32]{1,0:T(1,128)} %mask_hbm.1) | copy-start | bytes 388
  0.7 6.4 %copy-start = (bf16[4,16,16,4096]{3,2,1,0:T(8,128)(2,1)S(1)}, bf16[4,16,16,4096]{3,2,1,0:T(8,128)(2,1)}, u32[]{:S(2)}) copy-start(bf16[4,16,16,4096]{3,2,1,0:T(8,128)(2,1)} %vol.5) | copy-start | bytes 25165828
  3.3 3.8 %collective-permute-start = (bf16[16,4096]{1,0:T(8,128)(2,1)S(1)}, bf16[16,4096]{1,0:T(8,128)(2,1)S(1)}, u32[]{:S(2)}, u32[]{:S(2)}) collective-permute-start(bf16[16,4096]{1,0:T(8,128)(2,1)S(1)} %get-tuple-element.28), channel_id=1, source_target_pairs={{0,1},{1,0},{2,3},{3,2},{4,5},{5,4},{6,7},{7,6},{8,9},{9,8},{10,11... | collective-permute-start | bytes 393224 | tf_op jit(solution)/shard_map/ppermute | solution.py:383
  3.8 6.7 %collective-permute-start.1 = (bf16[16,4096]{1,0:T(8,128)(2,1)S(1)}, bf16[16,4096]{1,0:T(8,128)(2,1)S(1)}, u32[]{:S(2)}, u32[]{:S(2)}) collective-permute-start(bf16[16,4096]{1,0:T(8,128)(2,1)S(1)} %get-tuple-element.31), channel_id=1, source_target_pairs={{0,2},{2,0},{4,6},{6,4},{8,10},{10,8},{12,14},{14,12},{1,3},{3,1},... | collective-permute-start | bytes 393224 | tf_op jit(solution)/shard_map/ppermute | solution.py:385
  6.4 4.1 %collective-permute-start.2 = (bf16[16,4096]{1,0:T(8,128)(2,1)S(1)}, bf16[16,4096]{1,0:T(8,128)(2,1)S(1)}, u32[]{:S(2)}, u32[]{:S(2)}) collective-permute-start(bf16[16,4096]{1,0:T(8,128)(2,1)S(1)} %get-tuple-element.32), channel_id=1, source_target_pairs={{2,4},{6,8},{10,12},{4,2},{8,6},{12,10},{3,5},{7,9},{11,13},{5,3},... | collective-permute-start | bytes 393224 | tf_op jit(solution)/shard_map/ppermute | solution.py:387
  11.0 21.4 %copy-start.2 = (s32[8]{0:T(128)S(1)}, s32[8]{0:T(128)}, u32[]{:S(2)}) copy-start(s32[8]{0:T(128)} %order.1) | copy-start | bytes 100
  11.0 16.8 %collective-permute-start.3 = (s16[4,16,512]{2,1,0:T(8,128)(2,1)S(1)}, s16[4,16,512]{2,1,0:T(8,128)(2,1)S(1)}, u32[]{:S(2)}, u32[]{:S(2)}) collective-permute-start(s16[4,16,512]{2,1,0:T(8,128)(2,1)S(1)} %get-tuple-element.38), channel_id=1, source_target_pairs={{0,14},{2,12},{4,10},{6,8},{8,6},{10,4},{12,2},{14,0},{1,15},{3,13... | collective-permute-start | bytes 196616 | tf_op jit(solution)/shard_map/ppermute | solution.py:397
  16.0 11.9 %collective-permute-start.4 = (s16[4,16,512]{2,1,0:T(8,128)(2,1)S(1)}, s16[4,16,512]{2,1,0:T(8,128)(2,1)S(1)}, u32[]{:S(2)}, u32[]{:S(2)}) collective-permute-start(s16[4,16,512]{2,1,0:T(8,128)(2,1)S(1)} %get-tuple-element.39), channel_id=1, source_target_pairs={{0,12},{2,14},{4,8},{6,10},{8,4},{10,6},{12,0},{14,2},{1,13},{3,15... | collective-permute-start | bytes 196616 | tf_op jit(solution)/shard_map/ppermute | solution.py:397
  19.4 9.7 %collective-permute-start.5 = (s16[4,16,512]{2,1,0:T(8,128)(2,1)S(1)}, s16[4,16,512]{2,1,0:T(8,128)(2,1)S(1)}, u32[]{:S(2)}, u32[]{:S(2)}) collective-permute-start(s16[4,16,512]{2,1,0:T(8,128)(2,1)S(1)} %get-tuple-element.40), channel_id=1, source_target_pairs={{0,10},{2,8},{4,14},{6,12},{8,2},{10,0},{12,6},{14,4},{1,11},{3,9}... | collective-permute-start | bytes 196616 | tf_op jit(solution)/shard_map/ppermute | solution.py:397
  20.8 9.6 %collective-permute-start.6 = (s16[4,16,512]{2,1,0:T(8,128)(2,1)S(1)}, s16[4,16,512]{2,1,0:T(8,128)(2,1)S(1)}, u32[]{:S(2)}, u32[]{:S(2)}) collective-permute-start(s16[4,16,512]{2,1,0:T(8,128)(2,1)S(1)} %get-tuple-element.41), channel_id=1, source_target_pairs={{0,8},{2,10},{4,12},{6,14},{8,0},{10,2},{12,4},{14,6},{1,9},{3,11}... | collective-permute-start | bytes 196616 | tf_op jit(solution)/shard_map/ppermute | solution.py:397
  25.3 6.4 %collective-permute-start.7 = (s16[4,16,512]{2,1,0:T(8,128)(2,1)S(1)}, s16[4,16,512]{2,1,0:T(8,128)(2,1)S(1)}, u32[]{:S(2)}, u32[]{:S(2)}) collective-permute-start(s16[4,16,512]{2,1,0:T(8,128)(2,1)S(1)} %get-tuple-element.44), channel_id=1, source_target_pairs={{0,6},{2,4},{4,2},{6,0},{8,14},{10,12},{12,10},{14,8},{1,7},{3,5},... | collective-permute-start | bytes 196616 | tf_op jit(solution)/shard_map/ppermute | solution.py:397
  27.7 4.6 %collective-permute-start.8 = (s16[4,16,512]{2,1,0:T(8,128)(2,1)S(1)}, s16[4,16,512]{2,1,0:T(8,128)(2,1)S(1)}, u32[]{:S(2)}, u32[]{:S(2)}) collective-permute-start(s16[4,16,512]{2,1,0:T(8,128)(2,1)S(1)} %get-tuple-element.45), channel_id=1, source_target_pairs={{0,4},{2,6},{4,0},{6,2},{8,12},{10,14},{12,8},{14,10},{1,5},{3,7},... | collective-permute-start | bytes 196616 | tf_op jit(solution)/shard_map/ppermute | solution.py:397
  27.9 4.5 %collective-permute-start.9 = (s16[4,16,512]{2,1,0:T(8,128)(2,1)S(1)}, s16[4,16,512]{2,1,0:T(8,128)(2,1)S(1)}, u32[]{:S(2)}, u32[]{:S(2)}) collective-permute-start(s16[4,16,512]{2,1,0:T(8,128)(2,1)S(1)} %get-tuple-element.46), channel_id=1, source_target_pairs={{0,2},{2,0},{4,6},{6,4},{8,10},{10,8},{12,14},{14,12},{1,3},{3,1},... | collective-permute-start | bytes 196616 | tf_op jit(solution)/shard_map/ppermute | solution.py:397

commit v5 on v4

--- a/solution.py
+++ b/solution.py
@@ -11,6 +11,7 @@
 LANES = 128
 TOP = 65535.0
 HALF = 32768
+CHUNKS = 4
 
 VMEM = pl.BlockSpec(memory_space=pltpu.VMEM)
 SMEM = pl.BlockSpec(memory_space=pltpu.SMEM)
@@ -49,10 +50,16 @@
     return pl.ds(pl.multiple_of(place * LANES, LANES), LANES)
 
 
-def edges_kernel(mask_hbm, vol, density, near, far, edge, mask, sem, mask_sem):
+def edges_kernel(mask_hbm, vol, density, near, far, edge, mask, sems, mask_sem):
     depth, rows, cols = density.shape
-    copy = pltpu.make_async_copy(vol.at[0], density, sem)
-    copy.start()
+    chunk = cols // CHUNKS
+    copies = []
+    for c in range(CHUNKS):
+        where = pl.ds(c * chunk, chunk)
+        copies.append(
+            pltpu.make_async_copy(vol.at[0, :, :, where], density.at[:, :, where], sems.at[c])
+        )
+        copies[-1].start()
     mask_copy = pltpu.make_async_copy(mask_hbm, mask, mask_sem)
     mask_copy.start()
     row = jnp.where(lax.axis_index("tile") == 0, rows - 1, 0)
@@ -61,8 +68,9 @@
     cell = lax.broadcasted_iota(jnp.int32, (depth, depth * rows), 0)
     pick = (at == cell * rows + row).astype(jnp.bfloat16)
     mask_copy.wait()
-    copy.wait()
     for b in range(cols // LANES):
+        if b % (chunk // LANES) == 0:
+            copies[b // (chunk // LANES)].wait()
         keep = mask[0, b].astype(jnp.float32)
         here = pl.ds(b * LANES, LANES)
         planes = density[:, :, here].reshape(depth * rows, LANES)
@@ -88,7 +96,7 @@
             jax.ShapeDtypeStruct((depth, cols), jnp.bfloat16),
             jax.ShapeDtypeStruct(mask.shape, jnp.int32),
         ],
-        scratch_shapes=[pltpu.SemaphoreType.DMA, pltpu.SemaphoreType.DMA],
+        scratch_shapes=[pltpu.SemaphoreType.DMA((CHUNKS,)), pltpu.SemaphoreType.DMA],
         compiler_params=pltpu.CompilerParams(vmem_limit_bytes=48 * 1024 * 1024),
         cost_estimate=pl.CostEstimate(
             flops=1000000, bytes_accessed=2 * depth * rows * cols, transcendentals=0
@@ -328,11 +336,14 @@
 
 def composite_kernel(ks, order, *refs):
     n = len(ks)
-    parts, out, ranks = refs[:n], refs[n], refs[n + 1]
+    parts, out = refs[:n], refs[n]
     me = lax.axis_index("depth")
-    for p in range(n):
-        ranks[order[p]] = p
-    rank = [ranks[source(n, me, k)] for k in ks]
+    place = lax.broadcasted_iota(jnp.int32, order.shape, 1).astype(jnp.float32)
+    slabs = order[...]
+    rank = [
+        jnp.sum(jnp.where(slabs == source(n, me, k), place, 0.0), axis=1, keepdims=True)
+        for k in ks
+    ]
     before = [[jnp.where(a < b, 1.0, 0.0) for a in rank] for b in rank]
     rows, strip = out.shape[1:]
     for b in range(strip // LANES):
@@ -363,13 +374,12 @@
     rows, strip = parts[0].shape[1:]
     return pl.pallas_call(
         functools.partial(composite_kernel, ks),
-        in_specs=[SMEM] + [VMEM] * n,
+        in_specs=[VMEM] * (n + 1),
         out_specs=VMEM,
         out_shape=jax.ShapeDtypeStruct((4, rows, strip), jnp.float32),
-        scratch_shapes=[pltpu.SMEM((n,), jnp.int32)],
         compiler_params=pltpu.CompilerParams(vmem_limit_bytes=16 * 1024 * 1024),
         name="composite",
-    )(order, *parts)
+    )(order.reshape(1, n), *parts)
 
 
 def on_device(volume, brick_mask, brick_order):

time: 36.1 us -> 35.3 us (0.978)
  Pallas kernels: 9.84 us -> 9.12 us
    pallas_call x1, Pallas kernels: 0.96 us -> 0.47 us  [composite(): pl.pallas_call(functools.partial(composite_kernel, ks), in_specs=[VMEM] *...]
  transfers between devices with their start and end apart: 10 -> 10, of which waited for: 5 -> 4; matrix products, arithmetic and copies ran while one was open for 0% -> 0% of each run, Pallas kernels for 16% -> 16%
where the time goes in v5:
time: 35.3 us; the launch traced here: 35.1 us
  starting transfers between devices  19 us (54%)
  Pallas kernels  9.12 us (26%)
  waiting for transfers between devices  3.58 us (10%)
  blocking collectives  1.99 us (6%)
  local copies, waits for them, and re-layouts  1.37 us (4%)
    ppermute x7, starting transfers between devices, on_device(): lax.ppermute(strip, 'depth', partners(n, k))  15.2 us
    ppermute x7, waiting for transfers between devices, on_device(): lax.ppermute(strip, 'depth', partners(n, k))  3.57 us
    pallas_call x1, Pallas kernels, march_far(): pl.pallas_call(functools.partial(far_kernel, step_size, n, ks), in_specs=...  3.46 us
    ppermute x1, starting transfers between devices, on_device(): near = lax.ppermute(near, 'depth', pairs)  2.59 us
    pallas_call x1, Pallas kernels, edges(): pl.pallas_call(edges_kernel, in_specs=[HBM, HBM], out_specs=[VMEM] * 4 +...  2.4 us
    pallas_call x1, Pallas kernels, march_near(): pl.pallas_call(functools.partial(near_kernel, step_size, n, ks), in_specs...  2.28 us
    all_gather x1, blocking collectives, on_device(): return lax.all_gather(picture, 'tile', axis=1, tiled=True)  1.99 us
    unnamed x7, local copies, waits for them, and re-layouts  1.37 us
  transfers between devices with their start and end apart: 10, of which 4 were waited for; matrix products, arithmetic and copies ran while one was open for 0% of the time, Pallas kernels for 16%

profile of v5, /device:TPU:0, one launch (start us, length us, event | category | flops | bytes accessed | tf_op | source)
XLA Modules:
  0.0 35.1 jit_solution(13494327656160561000)
XLA Ops:
  0.0 0.0 copy-start.1
  0.0 0.7 %copy-done.1 = s32[1,32]{1,0:T(1,128)S(1)} copy-done((s32[1,32]{1,0:T(1,128)S(1)}, s32[1,32]{1,0:T(1,128)}, u32[]{:S(2)}) %copy-start.1) | copy-done | bytes 152
  0.7 0.0 copy-start
  0.7 2.4 %edges.1 = (bf16[16,16,4096]{2,1,0:T(8,128)(2,1)S(1)}, bf16[16,4096]{1,0:T(8,128)(2,1)S(1)}, bf16[16,4096]{1,0:T(8,128)(2,1)S(1)}, bf16[16,4096]{1,0:T(8,128)(2,1)S(1)}, s32[1,32]{1,0:T(1,128)S(1)}) custom-call(s32[1,32]{1,0:T(1,128)S(1)} %copy-done.1, bf16[4,16,16,4096]{3,2,1,0:T(8,128)(2,1)} %vol.5), custom_call_target="tpu_custom_call" | custom-call | flops 1000000 | bytes 2097152 | tf_op jit(solution)/shard_map/edges/pallas_call | solution.py:88
  3.1 0.5 %collective-permute-start = (bf16[16,4096]{1,0:T(8,128)(2,1)S(1)}, bf16[16,4096]{1,0:T(8,128)(2,1)S(1)}, u32[]{:S(2)}, u32[]{:S(2)}) collective-permute-start(bf16[16,4096]{1,0:T(8,128)(2,1)S(1)} %get-tuple-element.28), channel_id=1, source_target_pairs={{0,1},{1,0},{2,3},{3,2},{4,5},{5,4},{6,7},{7,6},{8,9},{9,8},{10,11... | collective-permute-start | bytes 393224 | tf_op jit(solution)/shard_map/ppermute | solution.py:393
  3.6 2.6 %collective-permute-start.1 = (bf16[16,4096]{1,0:T(8,128)(2,1)S(1)}, bf16[16,4096]{1,0:T(8,128)(2,1)S(1)}, u32[]{:S(2)}, u32[]{:S(2)}) collective-permute-start(bf16[16,4096]{1,0:T(8,128)(2,1)S(1)} %get-tuple-element.31), channel_id=1, source_target_pairs={{0,2},{2,0},{4,6},{6,4},{8,10},{10,8},{12,14},{14,12},{1,3},{3,1},... | collective-permute-start | bytes 393224 | tf_op jit(solution)/shard_map/ppermute | solution.py:395
  6.2 0.7 %collective-permute-start.2 = (bf16[16,4096]{1,0:T(8,128)(2,1)S(1)}, bf16[16,4096]{1,0:T(8,128)(2,1)S(1)}, u32[]{:S(2)}, u32[]{:S(2)}) collective-permute-start(bf16[16,4096]{1,0:T(8,128)(2,1)S(1)} %get-tuple-element.32), channel_id=1, source_target_pairs={{2,4},{6,8},{10,12},{4,2},{8,6},{12,10},{3,5},{7,9},{11,13},{5,3},... | collective-permute-start | bytes 393224 | tf_op jit(solution)/shard_map/ppermute | solution.py:397
  6.8 0.0 collective-permute-done.border
  6.9 0.0 copy-done
  6.9 3.5 %march_far.1 = (f32[4,16,2560]{2,1,0:T(8,128)S(1)}, f32[2,6,16,2560]{3,2,1,0:T(8,128)S(1)}) custom-call(s32[1,32]{1,0:T(1,128)S(1)} %get-tuple-element.43.mask, bf16[4,16,16,4096]{3,2,1,0:T(8,128)(2,1)S(1)} %copy-done, bf16[16,16,4096]{2,1,0:T(8,128)(2,1)S(1)} %get-tuple-element.27.density, bf16[16,4096]{1,0:T(8,128)(2,1)S(1)} %collective-permute-done.border), custom_call_target="tpu_custom_call" | custom-call | flops 26214400 | bytes 5242880 | tf_op jit(solution)/shard_map/march_far/pallas_call | solution.py:234
  10.3 0.0 collective-permute-done.1.near
  10.3 0.0 collective-permute-done.2.far
  10.4 0.5 %finish.1 = (s16[4,16,512]{2,1,0:T(8,128)(2,1)S(1)}, s16[4,16,512]{2,1,0:T(8,128)(2,1)S(1)}, s16[4,16,512]{2,1,0:T(8,128)(2,1)S(1)}, s16[4,16,512]{2,1,0:T(8,128)(2,1)S(1)}, s16[4,16,512]{2,1,0:T(8,128)(2,1)S(1)}) custom-call(f32[4,16,2560]{2,1,0:T(8,128)S(1)} %get-tuple-element.29.sums, f32[2,6,16,2560]{3,2,1,0:T(8,128)S(1)} %get-tuple-element.30.ends, ...), custom_call_target="tpu_custom_call" | custom-call | flops 2457600 | bytes 2621440 | tf_op jit(solution)/shard_map/finish/pallas_call | solution.py:275
  10.9 0.0 copy-start.2
  10.9 4.8 %collective-permute-start.3 = (s16[4,16,512]{2,1,0:T(8,128)(2,1)S(1)}, s16[4,16,512]{2,1,0:T(8,128)(2,1)S(1)}, u32[]{:S(2)}, u32[]{:S(2)}) collective-permute-start(s16[4,16,512]{2,1,0:T(8,128)(2,1)S(1)} %get-tuple-element.38), channel_id=1, source_target_pairs={{0,14},{2,12},{4,10},{6,8},{8,6},{10,4},{12,2},{14,0},{1,15},{3,13... | collective-permute-start | bytes 196616 | tf_op jit(solution)/shard_map/ppermute | solution.py:407
  15.7 3.3 %collective-permute-start.4 = (s16[4,16,512]{2,1,0:T(8,128)(2,1)S(1)}, s16[4,16,512]{2,1,0:T(8,128)(2,1)S(1)}, u32[]{:S(2)}, u32[]{:S(2)}) collective-permute-start(s16[4,16,512]{2,1,0:T(8,128)(2,1)S(1)} %get-tuple-element.39), channel_id=1, source_target_pairs={{0,12},{2,14},{4,8},{6,10},{8,4},{10,6},{12,0},{14,2},{1,13},{3,15... | collective-permute-start | bytes 196616 | tf_op jit(solution)/shard_map/ppermute | solution.py:407
  19.0 1.7 %collective-permute-start.5 = (s16[4,16,512]{2,1,0:T(8,128)(2,1)S(1)}, s16[4,16,512]{2,1,0:T(8,128)(2,1)S(1)}, u32[]{:S(2)}, u32[]{:S(2)}) collective-permute-start(s16[4,16,512]{2,1,0:T(8,128)(2,1)S(1)} %get-tuple-element.40), channel_id=1, source_target_pairs={{0,10},{2,8},{4,14},{6,12},{8,2},{10,0},{12,6},{14,4},{1,11},{3,9}... | collective-permute-start | bytes 196616 | tf_op jit(solution)/shard_map/ppermute | solution.py:407
  20.6 1.9 %collective-permute-start.6 = (s16[4,16,512]{2,1,0:T(8,128)(2,1)S(1)}, s16[4,16,512]{2,1,0:T(8,128)(2,1)S(1)}, u32[]{:S(2)}, u32[]{:S(2)}) collective-permute-start(s16[4,16,512]{2,1,0:T(8,128)(2,1)S(1)} %get-tuple-element.41), channel_id=1, source_target_pairs={{0,8},{2,10},{4,12},{6,14},{8,0},{10,2},{12,4},{14,6},{1,9},{3,11}... | collective-permute-start | bytes 196616 | tf_op jit(solution)/shard_map/ppermute | solution.py:407
  22.5 2.3 %march_near.1 = (s16[4,16,512]{2,1,0:T(8,128)(2,1)S(1)}, s16[4,16,512]{2,1,0:T(8,128)(2,1)S(1)}, s16[4,16,512]{2,1,0:T(8,128)(2,1)S(1)}) custom-call(s32[1,32]{1,0:T(1,128)S(1)} %get-tuple-element.43.mask, bf16[4,16,16,4096]{3,2,1,0:T(8,128)(2,1)S(1)} %copy-done, bf16[16,16,4096]{2,1,0:T(8,128)(2,1)S(1)} %get-tuple-element.27.density, ...), custom_call_target="tpu_custom_call" | custom-call | flops 15728640 | bytes 3145728 | tf_op jit(solution)/shard_map/march_near/pallas_call | solution.py:326
  24.8 2.4 %collective-permute-start.7 = (s16[4,16,512]{2,1,0:T(8,128)(2,1)S(1)}, s16[4,16,512]{2,1,0:T(8,128)(2,1)S(1)}, u32[]{:S(2)}, u32[]{:S(2)}) collective-permute-start(s16[4,16,512]{2,1,0:T(8,128)(2,1)S(1)} %get-tuple-element.44), channel_id=1, source_target_pairs={{0,6},{2,4},{4,2},{6,0},{8,14},{10,12},{12,10},{14,8},{1,7},{3,5},... | collective-permute-start | bytes 196616 | tf_op jit(solution)/shard_map/ppermute | solution.py:407
  27.3 0.0 collective-permute-done.3.refs_0_
  27.3 0.2 collective-permute-start.8
  27.5 0.0 collective-permute-done.4.refs_1_
  27.5 0.9 %collective-permute-start.9 = (s16[4,16,512]{2,1,0:T(8,128)(2,1)S(1)}, s16[4,16,512]{2,1,0:T(8,128)(2,1)S(1)}, u32[]{:S(2)}, u32[]{:S(2)}) collective-permute-start(s16[4,16,512]{2,1,0:T(8,128)(2,1)S(1)} %get-tuple-element.46), channel_id=1, source_target_pairs={{0,2},{2,0},{4,6},{6,4},{8,10},{10,8},{12,14},{14,12},{1,3},{3,1},... | collective-permute-start | bytes 196616 | tf_op jit(solution)/shard_map/ppermute | solution.py:407
  28.4 0.5 %collective-permute-done.5.refs_2_ = s16[4,16,512]{2,1,0:T(8,128)(2,1)S(1)} collective-permute-done((s16[4,16,512]{2,1,0:T(8,128)(2,1)S(1)}, s16[4,16,512]{2,1,0:T(8,128)(2,1)S(1)}, u32[]{:S(2)}, u32[]{:S(2)}) %collective-permute-start.5) | collective-permute-done | bytes 65568 | tf_op jit(solution)/shard_map/ppermute | solution.py:407
  28.9 1.2 %collective-permute-done.6.refs_3_ = s16[4,16,512]{2,1,0:T(8,128)(2,1)S(1)} collective-permute-done((s16[4,16,512]{2,1,0:T(8,128)(2,1)S(1)}, s16[4,16,512]{2,1,0:T(8,128)(2,1)S(1)}, u32[]{:S(2)}, u32[]{:S(2)}) %collective-permute-start.6) | collective-permute-done | bytes 65568 | tf_op jit(solution)/shard_map/ppermute | solution.py:407
  30.1 1.4 %collective-permute-done.7.refs_5_ = s16[4,16,512]{2,1,0:T(8,128)(2,1)S(1)} collective-permute-done((s16[4,16,512]{2,1,0:T(8,128)(2,1)S(1)}, s16[4,16,512]{2,1,0:T(8,128)(2,1)S(1)}, u32[]{:S(2)}, u32[]{:S(2)}) %collective-permute-start.7) | collective-permute-done | bytes 65568 | tf_op jit(solution)/shard_map/ppermute | solution.py:407
  31.5 0.5 %collective-permute-done.8.refs_6_ = s16[4,16,512]{2,1,0:T(8,128)(2,1)S(1)} collective-permute-done((s16[4,16,512]{2,1,0:T(8,128)(2,1)S(1)}, s16[4,16,512]{2,1,0:T(8,128)(2,1)S(1)}, u32[]{:S(2)}, u32[]{:S(2)}) %collective-permute-start.8) | collective-permute-done | bytes 65568 | tf_op jit(solution)/shard_map/ppermute | solution.py:407
  31.9 0.0 collective-permute-done.9.refs_7_
  32.0 0.0 copy-done.2
  32.0 0.5 %composite.1 = f32[4,16,512]{2,1,0:T(8,128)S(1)} custom-call(s32[1,8]{1,0:T(1,128)S(1)} %bitcast.1, s16[4,16,512]{2,1,0:T(8,128)(2,1)S(1)} %collective-permute-done.3.refs_0_, s16[4,16,512]{2,1,0:T(8,128)(2,1)S(1)} %collective-permute-done.4.refs_1_, s16[4,16,512]{2,1,0:T(8,128)(2,1)S(1)} %collective-permute-done.5.refs_2_, ...), custom_call_target="tpu_custom_call" | custom-call | tf_op jit(solution)/shard_map/composite/pallas_call | solution.py:375
  32.4 2.0 %all_gather.3 = f32[4,32,512]{2,1,0:T(8,128)S(1)} all-gather(f32[4,16,512]{2,1,0:T(8,128)S(1)} %composite.1), channel_id=1, replica_groups=mesh['parts'=2,'depth'=8,'tile'=2] {'tile'}, dimensions={1}, use_global_device_ids=true | all-gather | bytes 393216 | tf_op jit(solution)/shard_map/all_gather | solution.py:411
  34.4 0.7 %copy.5 = f32[4,32,512]{2,1,0:T(8,128)} copy(f32[4,32,512]{2,1,0:T(8,128)S(1)} %all_gather.3) | data formatting | bytes 524288
Async XLA Ops:
  0.0 0.7 %copy-start.1 = (s32[1,32]{1,0:T(1,128)S(1)}, s32[1,32]{1,0:T(1,128)}, u32[]{:S(2)}) copy-start(s32[1,32]{1,0:T(1,128)} %mask_hbm.1) | copy-start | bytes 388
  0.7 6.2 %copy-start = (bf16[4,16,16,4096]{3,2,1,0:T(8,128)(2,1)S(1)}, bf16[4,16,16,4096]{3,2,1,0:T(8,128)(2,1)}, u32[]{:S(2)}) copy-start(bf16[4,16,16,4096]{3,2,1,0:T(8,128)(2,1)} %vol.5) | copy-start | bytes 25165828
  3.1 3.8 %collective-permute-start = (bf16[16,4096]{1,0:T(8,128)(2,1)S(1)}, bf16[16,4096]{1,0:T(8,128)(2,1)S(1)}, u32[]{:S(2)}, u32[]{:S(2)}) collective-permute-start(bf16[16,4096]{1,0:T(8,128)(2,1)S(1)} %get-tuple-element.28), channel_id=1, source_target_pairs={{0,1},{1,0},{2,3},{3,2},{4,5},{5,4},{6,7},{7,6},{8,9},{9,8},{10,11... | collective-permute-start | bytes 393224 | tf_op jit(solution)/shard_map/ppermute | solution.py:393
  3.6 6.7 %collective-permute-start.1 = (bf16[16,4096]{1,0:T(8,128)(2,1)S(1)}, bf16[16,4096]{1,0:T(8,128)(2,1)S(1)}, u32[]{:S(2)}, u32[]{:S(2)}) collective-permute-start(bf16[16,4096]{1,0:T(8,128)(2,1)S(1)} %get-tuple-element.31), channel_id=1, source_target_pairs={{0,2},{2,0},{4,6},{6,4},{8,10},{10,8},{12,14},{14,12},{1,3},{3,1},... | collective-permute-start | bytes 393224 | tf_op jit(solution)/shard_map/ppermute | solution.py:395
  6.2 4.2 %collective-permute-start.2 = (bf16[16,4096]{1,0:T(8,128)(2,1)S(1)}, bf16[16,4096]{1,0:T(8,128)(2,1)S(1)}, u32[]{:S(2)}, u32[]{:S(2)}) collective-permute-start(bf16[16,4096]{1,0:T(8,128)(2,1)S(1)} %get-tuple-element.32), channel_id=1, source_target_pairs={{2,4},{6,8},{10,12},{4,2},{8,6},{12,10},{3,5},{7,9},{11,13},{5,3},... | collective-permute-start | bytes 393224 | tf_op jit(solution)/shard_map/ppermute | solution.py:397
  10.9 21.1 %copy-start.2 = (s32[8]{0:T(128)S(1)}, s32[8]{0:T(128)}, u32[]{:S(2)}) copy-start(s32[8]{0:T(128)} %param.5) | copy-start | bytes 100
  10.9 16.4 %collective-permute-start.3 = (s16[4,16,512]{2,1,0:T(8,128)(2,1)S(1)}, s16[4,16,512]{2,1,0:T(8,128)(2,1)S(1)}, u32[]{:S(2)}, u32[]{:S(2)}) collective-permute-start(s16[4,16,512]{2,1,0:T(8,128)(2,1)S(1)} %get-tuple-element.38), channel_id=1, source_target_pairs={{0,14},{2,12},{4,10},{6,8},{8,6},{10,4},{12,2},{14,0},{1,15},{3,13... | collective-permute-start | bytes 196616 | tf_op jit(solution)/shard_map/ppermute | solution.py:407
  15.7 11.8 %collective-permute-start.4 = (s16[4,16,512]{2,1,0:T(8,128)(2,1)S(1)}, s16[4,16,512]{2,1,0:T(8,128)(2,1)S(1)}, u32[]{:S(2)}, u32[]{:S(2)}) collective-permute-start(s16[4,16,512]{2,1,0:T(8,128)(2,1)S(1)} %get-tuple-element.39), channel_id=1, source_target_pairs={{0,12},{2,14},{4,8},{6,10},{8,4},{10,6},{12,0},{14,2},{1,13},{3,15... | collective-permute-start | bytes 196616 | tf_op jit(solution)/shard_map/ppermute | solution.py:407
  19.0 9.9 %collective-permute-start.5 = (s16[4,16,512]{2,1,0:T(8,128)(2,1)S(1)}, s16[4,16,512]{2,1,0:T(8,128)(2,1)S(1)}, u32[]{:S(2)}, u32[]{:S(2)}) collective-permute-start(s16[4,16,512]{2,1,0:T(8,128)(2,1)S(1)} %get-tuple-element.40), channel_id=1, source_target_pairs={{0,10},{2,8},{4,14},{6,12},{8,2},{10,0},{12,6},{14,4},{1,11},{3,9}... | collective-permute-start | bytes 196616 | tf_op jit(solution)/shard_map/ppermute | solution.py:407
  20.6 9.4 %collective-permute-start.6 = (s16[4,16,512]{2,1,0:T(8,128)(2,1)S(1)}, s16[4,16,512]{2,1,0:T(8,128)(2,1)S(1)}, u32[]{:S(2)}, u32[]{:S(2)}) collective-permute-start(s16[4,16,512]{2,1,0:T(8,128)(2,1)S(1)} %get-tuple-element.41), channel_id=1, source_target_pairs={{0,8},{2,10},{4,12},{6,14},{8,0},{10,2},{12,4},{14,6},{1,9},{3,11}... | collective-permute-start | bytes 196616 | tf_op jit(solution)/shard_map/ppermute | solution.py:407
  24.8 6.6 %collective-permute-start.7 = (s16[4,16,512]{2,1,0:T(8,128)(2,1)S(1)}, s16[4,16,512]{2,1,0:T(8,128)(2,1)S(1)}, u32[]{:S(2)}, u32[]{:S(2)}) collective-permute-start(s16[4,16,512]{2,1,0:T(8,128)(2,1)S(1)} %get-tuple-element.44), channel_id=1, source_target_pairs={{0,6},{2,4},{4,2},{6,0},{8,14},{10,12},{12,10},{14,8},{1,7},{3,5},... | collective-permute-start | bytes 196616 | tf_op jit(solution)/shard_map/ppermute | solution.py:407
  27.3 4.7 %collective-permute-start.8 = (s16[4,16,512]{2,1,0:T(8,128)(2,1)S(1)}, s16[4,16,512]{2,1,0:T(8,128)(2,1)S(1)}, u32[]{:S(2)}, u32[]{:S(2)}) collective-permute-start(s16[4,16,512]{2,1,0:T(8,128)(2,1)S(1)} %get-tuple-element.45), channel_id=1, source_target_pairs={{0,4},{2,6},{4,0},{6,2},{8,12},{10,14},{12,8},{14,10},{1,5},{3,7},... | collective-permute-start | bytes 196616 | tf_op jit(solution)/shard_map/ppermute | solution.py:407
  27.5 4.5 %collective-permute-start.9 = (s16[4,16,512]{2,1,0:T(8,128)(2,1)S(1)}, s16[4,16,512]{2,1,0:T(8,128)(2,1)S(1)}, u32[]{:S(2)}, u32[]{:S(2)}) collective-permute-start(s16[4,16,512]{2,1,0:T(8,128)(2,1)S(1)} %get-tuple-element.46), channel_id=1, source_target_pairs={{0,2},{2,0},{4,6},{6,4},{8,10},{10,8},{12,14},{14,12},{1,3},{3,1},... | collective-permute-start | bytes 196616 | tf_op jit(solution)/shard_map/ppermute | solution.py:407

commit v6 on v5

--- a/solution.py
+++ b/solution.py
@@ -168,11 +168,13 @@
             for k in range(3):
                 sums[k] = sums[k] + weight * glow[k]
         before, here = here, after
-    put([0.5 * (plain + sums[k]) for k in range(3)], clear)
-
-
-def encode(out, there, colours, clear):
-    root = jnp.sqrt(jnp.sqrt(jnp.sqrt(1.0 - clear)))
+    put([0.5 * (plain + sums[k]) for k in range(3)], total * step_size)
+
+
+def encode(out, there, colours, optical):
+    thin = optical * (1.0 - optical * (0.5 - optical * (1.0 / 6.0 - optical * (1.0 / 24.0))))
+    opacity = jnp.where(optical < 0.03, thin, 1.0 - jnp.exp(-optical))
+    root = jnp.sqrt(jnp.sqrt(jnp.sqrt(opacity)))
     level = (root * TOP + 0.5).astype(jnp.int32)
     out[3, :, there] = (level - HALF).astype(jnp.int16)
     gain = TOP / jnp.maximum(eighth_power(level.astype(jnp.float32) * (1.0 / TOP)), 1e-30)
@@ -200,8 +202,8 @@
             for v, value in enumerate(values):
                 ends[end, v, :, here] = value
 
-        def put(colours, clear):
-            for v, value in enumerate(colours + [clear]):
+        def put(colours, optical):
+            for v, value in enumerate(colours + [optical]):
                 sums_out[v, :, here] = value
 
         keep = mask[0, place] != 0
@@ -215,7 +217,7 @@
         @pl.when(jnp.logical_not(keep))
         def _():
             empty = jnp.zeros((rows, LANES), jnp.float32)
-            put([empty] * 3, empty + 1.0)
+            put([empty] * 3, empty)
             put_end(0, [empty] * 6)
             put_end(1, [empty] * 6)
 
@@ -302,8 +304,8 @@
             def _():
                 planes = halves(even, near, far, columns(place))
 
-                def put(colours, clear):
-                    encode(out, there, colours, clear)
+                def put(colours, optical):
+                    encode(out, there, colours, optical)
 
                 march_brick(
                     step_size, vol, density, border, mask, place, planes, None, put

time: 35.3 us -> 35.7 us (1.011)
  Pallas kernels: 9.12 us -> 9.59 us
  waiting for transfers between devices: 3.58 us -> 3.15 us
    pallas_call x1, Pallas kernels: 2.28 us -> 2.91 us  [march_near(): pl.pallas_call(functools.partial(near_kernel, step_size, n, ks), in_specs...]
    ppermute x7, waiting for transfers between devices: 3.57 us -> 2.98 us  [on_device(): lax.ppermute(strip, 'depth', partners(n, k))]
  transfers between devices with their start and end apart: 10 -> 10, of which waited for: 4 -> 5; matrix products, arithmetic and copies ran while one was open for 0% -> 0% of each run, Pallas kernels for 16% -> 17%
where the time goes in v6:
time: 35.7 us; the launch traced here: 35.2 us
  starting transfers between devices  19.1 us (54%)
  Pallas kernels  9.59 us (27%)
  waiting for transfers between devices  3.15 us (9%)
  blocking collectives  1.99 us (6%)
  local copies, waits for them, and re-layouts  1.37 us (4%)
    ppermute x7, starting transfers between devices, on_device(): lax.ppermute(strip, 'depth', partners(n, k))  15.3 us
    pallas_call x1, Pallas kernels, march_far(): pl.pallas_call(functools.partial(far_kernel, step_size, n, ks), in_specs=...  3.23 us
    ppermute x7, waiting for transfers between devices, on_device(): lax.ppermute(strip, 'depth', partners(n, k))  2.98 us
    pallas_call x1, Pallas kernels, march_near(): pl.pallas_call(functools.partial(near_kernel, step_size, n, ks), in_specs...  2.91 us
    ppermute x1, starting transfers between devices, on_device(): near = lax.ppermute(near, 'depth', pairs)  2.59 us
    pallas_call x1, Pallas kernels, edges(): pl.pallas_call(edges_kernel, in_specs=[HBM, HBM], out_specs=[VMEM] * 4 +...  2.4 us
    all_gather x1, blocking collectives, on_device(): return lax.all_gather(picture, 'tile', axis=1, tiled=True)  1.99 us
    unnamed x7, local copies, waits for them, and re-layouts  1.37 us
  transfers between devices with their start and end apart: 10, of which 5 were waited for; matrix products, arithmetic and copies ran while one was open for 0% of the time, Pallas kernels for 17%

profile of v6, /device:TPU:0, one launch (start us, length us, event | category | flops | bytes accessed | tf_op | source)
XLA Modules:
  0.0 35.2 jit_solution(16143881839570428471)
XLA Ops:
  0.0 0.0 copy-start.1
  0.0 0.7 %copy-done.1 = s32[1,32]{1,0:T(1,128)S(1)} copy-done((s32[1,32]{1,0:T(1,128)S(1)}, s32[1,32]{1,0:T(1,128)}, u32[]{:S(2)}) %copy-start.1) | copy-done | bytes 152
  0.7 0.0 copy-start
  0.7 2.4 %edges.1 = (bf16[16,16,4096]{2,1,0:T(8,128)(2,1)S(1)}, bf16[16,4096]{1,0:T(8,128)(2,1)S(1)}, bf16[16,4096]{1,0:T(8,128)(2,1)S(1)}, bf16[16,4096]{1,0:T(8,128)(2,1)S(1)}, s32[1,32]{1,0:T(1,128)S(1)}) custom-call(s32[1,32]{1,0:T(1,128)S(1)} %copy-done.1, bf16[4,16,16,4096]{3,2,1,0:T(8,128)(2,1)} %vol.5), custom_call_target="tpu_custom_call" | custom-call | flops 1000000 | bytes 2097152 | tf_op jit(solution)/shard_map/edges/pallas_call | solution.py:88
  3.1 0.5 %collective-permute-start = (bf16[16,4096]{1,0:T(8,128)(2,1)S(1)}, bf16[16,4096]{1,0:T(8,128)(2,1)S(1)}, u32[]{:S(2)}, u32[]{:S(2)}) collective-permute-start(bf16[16,4096]{1,0:T(8,128)(2,1)S(1)} %get-tuple-element.28), channel_id=1, source_target_pairs={{0,1},{1,0},{2,3},{3,2},{4,5},{5,4},{6,7},{7,6},{8,9},{9,8},{10,11... | collective-permute-start | bytes 393224 | tf_op jit(solution)/shard_map/ppermute | solution.py:395
  3.6 2.6 %collective-permute-start.1 = (bf16[16,4096]{1,0:T(8,128)(2,1)S(1)}, bf16[16,4096]{1,0:T(8,128)(2,1)S(1)}, u32[]{:S(2)}, u32[]{:S(2)}) collective-permute-start(bf16[16,4096]{1,0:T(8,128)(2,1)S(1)} %get-tuple-element.31), channel_id=1, source_target_pairs={{0,2},{2,0},{4,6},{6,4},{8,10},{10,8},{12,14},{14,12},{1,3},{3,1},... | collective-permute-start | bytes 393224 | tf_op jit(solution)/shard_map/ppermute | solution.py:397
  6.2 0.7 %collective-permute-start.2 = (bf16[16,4096]{1,0:T(8,128)(2,1)S(1)}, bf16[16,4096]{1,0:T(8,128)(2,1)S(1)}, u32[]{:S(2)}, u32[]{:S(2)}) collective-permute-start(bf16[16,4096]{1,0:T(8,128)(2,1)S(1)} %get-tuple-element.32), channel_id=1, source_target_pairs={{2,4},{6,8},{10,12},{4,2},{8,6},{12,10},{3,5},{7,9},{11,13},{5,3},... | collective-permute-start | bytes 393224 | tf_op jit(solution)/shard_map/ppermute | solution.py:399
  6.8 0.0 collective-permute-done.border
  6.9 0.0 copy-done
  6.9 3.2 %march_far.1 = (f32[4,16,2560]{2,1,0:T(8,128)S(1)}, f32[2,6,16,2560]{3,2,1,0:T(8,128)S(1)}) custom-call(s32[1,32]{1,0:T(1,128)S(1)} %get-tuple-element.43.mask, bf16[4,16,16,4096]{3,2,1,0:T(8,128)(2,1)S(1)} %copy-done, bf16[16,16,4096]{2,1,0:T(8,128)(2,1)S(1)} %get-tuple-element.27.density, bf16[16,4096]{1,0:T(8,128)(2,1)S(1)} %collective-permute-done.border), custom_call_target="tpu_custom_call" | custom-call | flops 26214400 | bytes 5242880 | tf_op jit(solution)/shard_map/march_far/pallas_call | solution.py:236
  10.1 0.2 collective-permute-done.1.near
  10.3 0.0 collective-permute-done.2.far
  10.3 0.6 %finish.1 = (s16[4,16,512]{2,1,0:T(8,128)(2,1)S(1)}, s16[4,16,512]{2,1,0:T(8,128)(2,1)S(1)}, s16[4,16,512]{2,1,0:T(8,128)(2,1)S(1)}, s16[4,16,512]{2,1,0:T(8,128)(2,1)S(1)}, s16[4,16,512]{2,1,0:T(8,128)(2,1)S(1)}) custom-call(f32[4,16,2560]{2,1,0:T(8,128)S(1)} %get-tuple-element.29.sums, f32[2,6,16,2560]{3,2,1,0:T(8,128)S(1)} %get-tuple-element.30.ends, ...), custom_call_target="tpu_custom_call" | custom-call | flops 2457600 | bytes 2621440 | tf_op jit(solution)/shard_map/finish/pallas_call | solution.py:277
  10.9 0.0 copy-start.2
  10.9 4.9 %collective-permute-start.3 = (s16[4,16,512]{2,1,0:T(8,128)(2,1)S(1)}, s16[4,16,512]{2,1,0:T(8,128)(2,1)S(1)}, u32[]{:S(2)}, u32[]{:S(2)}) collective-permute-start(s16[4,16,512]{2,1,0:T(8,128)(2,1)S(1)} %get-tuple-element.38), channel_id=1, source_target_pairs={{0,14},{2,12},{4,10},{6,8},{8,6},{10,4},{12,2},{14,0},{1,15},{3,13... | collective-permute-start | bytes 196616 | tf_op jit(solution)/shard_map/ppermute | solution.py:409
  15.7 3.4 %collective-permute-start.4 = (s16[4,16,512]{2,1,0:T(8,128)(2,1)S(1)}, s16[4,16,512]{2,1,0:T(8,128)(2,1)S(1)}, u32[]{:S(2)}, u32[]{:S(2)}) collective-permute-start(s16[4,16,512]{2,1,0:T(8,128)(2,1)S(1)} %get-tuple-element.39), channel_id=1, source_target_pairs={{0,12},{2,14},{4,8},{6,10},{8,4},{10,6},{12,0},{14,2},{1,13},{3,15... | collective-permute-start | bytes 196616 | tf_op jit(solution)/shard_map/ppermute | solution.py:409
  19.1 1.6 %collective-permute-start.5 = (s16[4,16,512]{2,1,0:T(8,128)(2,1)S(1)}, s16[4,16,512]{2,1,0:T(8,128)(2,1)S(1)}, u32[]{:S(2)}, u32[]{:S(2)}) collective-permute-start(s16[4,16,512]{2,1,0:T(8,128)(2,1)S(1)} %get-tuple-element.40), channel_id=1, source_target_pairs={{0,10},{2,8},{4,14},{6,12},{8,2},{10,0},{12,6},{14,4},{1,11},{3,9}... | collective-permute-start | bytes 196616 | tf_op jit(solution)/shard_map/ppermute | solution.py:409
  20.7 1.9 %collective-permute-start.6 = (s16[4,16,512]{2,1,0:T(8,128)(2,1)S(1)}, s16[4,16,512]{2,1,0:T(8,128)(2,1)S(1)}, u32[]{:S(2)}, u32[]{:S(2)}) collective-permute-start(s16[4,16,512]{2,1,0:T(8,128)(2,1)S(1)} %get-tuple-element.41), channel_id=1, source_target_pairs={{0,8},{2,10},{4,12},{6,14},{8,0},{10,2},{12,4},{14,6},{1,9},{3,11}... | collective-permute-start | bytes 196616 | tf_op jit(solution)/shard_map/ppermute | solution.py:409
  22.6 2.9 %march_near.1 = (s16[4,16,512]{2,1,0:T(8,128)(2,1)S(1)}, s16[4,16,512]{2,1,0:T(8,128)(2,1)S(1)}, s16[4,16,512]{2,1,0:T(8,128)(2,1)S(1)}) custom-call(s32[1,32]{1,0:T(1,128)S(1)} %get-tuple-element.43.mask, bf16[4,16,16,4096]{3,2,1,0:T(8,128)(2,1)S(1)} %copy-done, bf16[16,16,4096]{2,1,0:T(8,128)(2,1)S(1)} %get-tuple-element.27.density, ...), custom_call_target="tpu_custom_call" | custom-call | flops 15728640 | bytes 3145728 | tf_op jit(solution)/shard_map/march_near/pallas_call | solution.py:328
  25.5 0.9 %collective-permute-start.7 = (s16[4,16,512]{2,1,0:T(8,128)(2,1)S(1)}, s16[4,16,512]{2,1,0:T(8,128)(2,1)S(1)}, u32[]{:S(2)}, u32[]{:S(2)}) collective-permute-start(s16[4,16,512]{2,1,0:T(8,128)(2,1)S(1)} %get-tuple-element.44), channel_id=1, source_target_pairs={{0,6},{2,4},{4,2},{6,0},{8,14},{10,12},{12,10},{14,8},{1,7},{3,5},... | collective-permute-start | bytes 196616 | tf_op jit(solution)/shard_map/ppermute | solution.py:409
  26.5 0.0 collective-permute-done.3.refs_0_
  26.5 0.8 %collective-permute-start.8 = (s16[4,16,512]{2,1,0:T(8,128)(2,1)S(1)}, s16[4,16,512]{2,1,0:T(8,128)(2,1)S(1)}, u32[]{:S(2)}, u32[]{:S(2)}) collective-permute-start(s16[4,16,512]{2,1,0:T(8,128)(2,1)S(1)} %get-tuple-element.45), channel_id=1, source_target_pairs={{0,4},{2,6},{4,0},{6,2},{8,12},{10,14},{12,8},{14,10},{1,5},{3,7},... | collective-permute-start | bytes 196616 | tf_op jit(solution)/shard_map/ppermute | solution.py:409
  27.3 0.0 collective-permute-done.4.refs_1_
  27.3 1.8 %collective-permute-start.9 = (s16[4,16,512]{2,1,0:T(8,128)(2,1)S(1)}, s16[4,16,512]{2,1,0:T(8,128)(2,1)S(1)}, u32[]{:S(2)}, u32[]{:S(2)}) collective-permute-start(s16[4,16,512]{2,1,0:T(8,128)(2,1)S(1)} %get-tuple-element.46), channel_id=1, source_target_pairs={{0,2},{2,0},{4,6},{6,4},{8,10},{10,8},{12,14},{14,12},{1,3},{3,1},... | collective-permute-start | bytes 196616 | tf_op jit(solution)/shard_map/ppermute | solution.py:409
  29.1 0.0 collective-permute-done.5.refs_2_
  29.1 1.0 %collective-permute-done.6.refs_3_ = s16[4,16,512]{2,1,0:T(8,128)(2,1)S(1)} collective-permute-done((s16[4,16,512]{2,1,0:T(8,128)(2,1)S(1)}, s16[4,16,512]{2,1,0:T(8,128)(2,1)S(1)}, u32[]{:S(2)}, u32[]{:S(2)}) %collective-permute-start.6) | collective-permute-done | bytes 65568 | tf_op jit(solution)/shard_map/ppermute | solution.py:409
  30.1 1.4 %collective-permute-done.7.refs_5_ = s16[4,16,512]{2,1,0:T(8,128)(2,1)S(1)} collective-permute-done((s16[4,16,512]{2,1,0:T(8,128)(2,1)S(1)}, s16[4,16,512]{2,1,0:T(8,128)(2,1)S(1)}, u32[]{:S(2)}, u32[]{:S(2)}) %collective-permute-start.7) | collective-permute-done | bytes 65568 | tf_op jit(solution)/shard_map/ppermute | solution.py:409
  31.5 0.3 collective-permute-done.8.refs_6_
  31.7 0.3 collective-permute-done.9.refs_7_
  32.1 0.0 copy-done.2
  32.1 0.5 %composite.1 = f32[4,16,512]{2,1,0:T(8,128)S(1)} custom-call(s32[1,8]{1,0:T(1,128)S(1)} %bitcast.1, s16[4,16,512]{2,1,0:T(8,128)(2,1)S(1)} %collective-permute-done.3.refs_0_, s16[4,16,512]{2,1,0:T(8,128)(2,1)S(1)} %collective-permute-done.4.refs_1_, s16[4,16,512]{2,1,0:T(8,128)(2,1)S(1)} %collective-permute-done.5.refs_2_, ...), custom_call_target="tpu_custom_call" | custom-call | tf_op jit(solution)/shard_map/composite/pallas_call | solution.py:377
  32.5 2.0 %all_gather.3 = f32[4,32,512]{2,1,0:T(8,128)S(1)} all-gather(f32[4,16,512]{2,1,0:T(8,128)S(1)} %composite.1), channel_id=1, replica_groups=mesh['parts'=2,'depth'=8,'tile'=2] {'tile'}, dimensions={1}, use_global_device_ids=true | all-gather | bytes 393216 | tf_op jit(solution)/shard_map/all_gather | solution.py:413
  34.5 0.7 %copy.5 = f32[4,32,512]{2,1,0:T(8,128)} copy(f32[4,32,512]{2,1,0:T(8,128)S(1)} %all_gather.3) | data formatting | bytes 524288
Async XLA Ops:
  0.0 0.7 %copy-start.1 = (s32[1,32]{1,0:T(1,128)S(1)}, s32[1,32]{1,0:T(1,128)}, u32[]{:S(2)}) copy-start(s32[1,32]{1,0:T(1,128)} %mask_hbm.1) | copy-start | bytes 388
  0.7 6.2 %copy-start = (bf16[4,16,16,4096]{3,2,1,0:T(8,128)(2,1)S(1)}, bf16[4,16,16,4096]{3,2,1,0:T(8,128)(2,1)}, u32[]{:S(2)}) copy-start(bf16[4,16,16,4096]{3,2,1,0:T(8,128)(2,1)} %vol.5) | copy-start | bytes 25165828
  3.1 3.8 %collective-permute-start = (bf16[16,4096]{1,0:T(8,128)(2,1)S(1)}, bf16[16,4096]{1,0:T(8,128)(2,1)S(1)}, u32[]{:S(2)}, u32[]{:S(2)}) collective-permute-start(bf16[16,4096]{1,0:T(8,128)(2,1)S(1)} %get-tuple-element.28), channel_id=1, source_target_pairs={{0,1},{1,0},{2,3},{3,2},{4,5},{5,4},{6,7},{7,6},{8,9},{9,8},{10,11... | collective-permute-start | bytes 393224 | tf_op jit(solution)/shard_map/ppermute | solution.py:395
  3.6 6.7 %collective-permute-start.1 = (bf16[16,4096]{1,0:T(8,128)(2,1)S(1)}, bf16[16,4096]{1,0:T(8,128)(2,1)S(1)}, u32[]{:S(2)}, u32[]{:S(2)}) collective-permute-start(bf16[16,4096]{1,0:T(8,128)(2,1)S(1)} %get-tuple-element.31), channel_id=1, source_target_pairs={{0,2},{2,0},{4,6},{6,4},{8,10},{10,8},{12,14},{14,12},{1,3},{3,1},... | collective-permute-start | bytes 393224 | tf_op jit(solution)/shard_map/ppermute | solution.py:397
  6.2 4.1 %collective-permute-start.2 = (bf16[16,4096]{1,0:T(8,128)(2,1)S(1)}, bf16[16,4096]{1,0:T(8,128)(2,1)S(1)}, u32[]{:S(2)}, u32[]{:S(2)}) collective-permute-start(bf16[16,4096]{1,0:T(8,128)(2,1)S(1)} %get-tuple-element.32), channel_id=1, source_target_pairs={{2,4},{6,8},{10,12},{4,2},{8,6},{12,10},{3,5},{7,9},{11,13},{5,3},... | collective-permute-start | bytes 393224 | tf_op jit(solution)/shard_map/ppermute | solution.py:399
  10.9 21.2 %copy-start.2 = (s32[8]{0:T(128)S(1)}, s32[8]{0:T(128)}, u32[]{:S(2)}) copy-start(s32[8]{0:T(128)} %param.5) | copy-start | bytes 100
  10.9 15.6 %collective-permute-start.3 = (s16[4,16,512]{2,1,0:T(8,128)(2,1)S(1)}, s16[4,16,512]{2,1,0:T(8,128)(2,1)S(1)}, u32[]{:S(2)}, u32[]{:S(2)}) collective-permute-start(s16[4,16,512]{2,1,0:T(8,128)(2,1)S(1)} %get-tuple-element.38), channel_id=1, source_target_pairs={{0,14},{2,12},{4,10},{6,8},{8,6},{10,4},{12,2},{14,0},{1,15},{3,13... | collective-permute-start | bytes 196616 | tf_op jit(solution)/shard_map/ppermute | solution.py:409
  15.7 11.6 %collective-permute-start.4 = (s16[4,16,512]{2,1,0:T(8,128)(2,1)S(1)}, s16[4,16,512]{2,1,0:T(8,128)(2,1)S(1)}, u32[]{:S(2)}, u32[]{:S(2)}) collective-permute-start(s16[4,16,512]{2,1,0:T(8,128)(2,1)S(1)} %get-tuple-element.39), channel_id=1, source_target_pairs={{0,12},{2,14},{4,8},{6,10},{8,4},{10,6},{12,0},{14,2},{1,13},{3,15... | collective-permute-start | bytes 196616 | tf_op jit(solution)/shard_map/ppermute | solution.py:409
  19.1 10.0 %collective-permute-start.5 = (s16[4,16,512]{2,1,0:T(8,128)(2,1)S(1)}, s16[4,16,512]{2,1,0:T(8,128)(2,1)S(1)}, u32[]{:S(2)}, u32[]{:S(2)}) collective-permute-start(s16[4,16,512]{2,1,0:T(8,128)(2,1)S(1)} %get-tuple-element.40), channel_id=1, source_target_pairs={{0,10},{2,8},{4,14},{6,12},{8,2},{10,0},{12,6},{14,4},{1,11},{3,9}... | collective-permute-start | bytes 196616 | tf_op jit(solution)/shard_map/ppermute | solution.py:409
  20.7 9.4 %collective-permute-start.6 = (s16[4,16,512]{2,1,0:T(8,128)(2,1)S(1)}, s16[4,16,512]{2,1,0:T(8,128)(2,1)S(1)}, u32[]{:S(2)}, u32[]{:S(2)}) collective-permute-start(s16[4,16,512]{2,1,0:T(8,128)(2,1)S(1)} %get-tuple-element.41), channel_id=1, source_target_pairs={{0,8},{2,10},{4,12},{6,14},{8,0},{10,2},{12,4},{14,6},{1,9},{3,11}... | collective-permute-start | bytes 196616 | tf_op jit(solution)/shard_map/ppermute | solution.py:409
  25.5 5.9 %collective-permute-start.7 = (s16[4,16,512]{2,1,0:T(8,128)(2,1)S(1)}, s16[4,16,512]{2,1,0:T(8,128)(2,1)S(1)}, u32[]{:S(2)}, u32[]{:S(2)}) collective-permute-start(s16[4,16,512]{2,1,0:T(8,128)(2,1)S(1)} %get-tuple-element.44), channel_id=1, source_target_pairs={{0,6},{2,4},{4,2},{6,0},{8,14},{10,12},{12,10},{14,8},{1,7},{3,5},... | collective-permute-start | bytes 196616 | tf_op jit(solution)/shard_map/ppermute | solution.py:409
  26.5 5.3 %collective-permute-start.8 = (s16[4,16,512]{2,1,0:T(8,128)(2,1)S(1)}, s16[4,16,512]{2,1,0:T(8,128)(2,1)S(1)}, u32[]{:S(2)}, u32[]{:S(2)}) collective-permute-start(s16[4,16,512]{2,1,0:T(8,128)(2,1)S(1)} %get-tuple-element.45), channel_id=1, source_target_pairs={{0,4},{2,6},{4,0},{6,2},{8,12},{10,14},{12,8},{14,10},{1,5},{3,7},... | collective-permute-start | bytes 196616 | tf_op jit(solution)/shard_map/ppermute | solution.py:409
  27.3 4.8 %collective-permute-start.9 = (s16[4,16,512]{2,1,0:T(8,128)(2,1)S(1)}, s16[4,16,512]{2,1,0:T(8,128)(2,1)S(1)}, u32[]{:S(2)}, u32[]{:S(2)}) collective-permute-start(s16[4,16,512]{2,1,0:T(8,128)(2,1)S(1)} %get-tuple-element.46), channel_id=1, source_target_pairs={{0,2},{2,0},{4,6},{6,4},{8,10},{10,8},{12,14},{14,12},{1,3},{3,1},... | collective-permute-start | bytes 196616 | tf_op jit(solution)/shard_map/ppermute | solution.py:409

commit v7 on v6

--- a/solution.py
+++ b/solution.py
@@ -195,7 +195,7 @@
     me = lax.axis_index("depth")
 
     def step(i, carry):
-        place = target(n, me, lax.select(i // bricks < n // 2, n - 1 - i // bricks, 0)) * bricks + i % bricks
+        place = target(n, me, lax.select(i // bricks < n // 2, lax.bitwise_xor(n - 1 - i // bricks, n // 4), 0)) * bricks + i % bricks
         here = columns(i)
 
         def put_end(end, values):
@@ -398,7 +398,7 @@
     pairs = [(i, i + 1) for i in range(1, n - 1, 2)]
     far = lax.ppermute(far, "depth", pairs + [(b, a) for a, b in pairs])
 
-    first, second = rounds(n)[: n // 2] + [0], rounds(n)[n // 2 : -1]
+    first, second = [k ^ (n // 4) for k in rounds(n)[: n // 2]] + [0], rounds(n)[n // 2 : -1]
     sums, ends = march_far(volume, density, border, mask, step_size, n, first)
     strips = finish(sums, ends, near, far, n, first)
     strips, mask = lax.optimization_barrier((strips, mask))

time: 35.7 us -> 34.9 us (0.978); the launches traced: 35.2 us -> 35 us
  starting transfers between devices: 19.1 us -> 18.6 us
    pallas_call x1, Pallas kernels: 3.23 us -> 3.98 us  [march_far(): pl.pallas_call(functools.partial(far_kernel, step_size, n, ks), in_specs=...]
    pallas_call x1, Pallas kernels: 2.91 us -> 2.3 us  [march_near(): pl.pallas_call(functools.partial(near_kernel, step_size, n, ks), in_specs...]
    ppermute x7, starting transfers between devices: 15.3 us -> 14.8 us  [on_device(): lax.ppermute(strip, 'depth', partners(n, k))]
  transfers between devices with their start and end apart: 10 -> 10, of which waited for: 5 -> 4; matrix products, arithmetic and copies ran while one was open for 0% -> 0% of each run, Pallas kernels for 17% -> 18%
where the time goes in v7:
time: 34.9 us; the launch traced here: 35 us
  starting transfers between devices  18.6 us (53%)
  Pallas kernels  9.73 us (28%)
  waiting for transfers between devices  3.2 us (9%)
  blocking collectives  1.99 us (6%)
  local copies, waits for them, and re-layouts  1.37 us (4%)
    ppermute x7, starting transfers between devices, on_device(): lax.ppermute(strip, 'depth', partners(n, k))  14.8 us
    pallas_call x1, Pallas kernels, march_far(): pl.pallas_call(functools.partial(far_kernel, step_size, n, ks), in_specs=...  3.98 us
    ppermute x7, waiting for transfers between devices, on_device(): lax.ppermute(strip, 'depth', partners(n, k))  3.19 us
    ppermute x1, starting transfers between devices, on_device(): near = lax.ppermute(near, 'depth', pairs)  2.59 us
    pallas_call x1, Pallas kernels, edges(): pl.pallas_call(edges_kernel, in_specs=[HBM, HBM], out_specs=[VMEM] * 4 +...  2.4 us
    pallas_call x1, Pallas kernels, march_near(): pl.pallas_call(functools.partial(near_kernel, step_size, n, ks), in_specs...  2.3 us
    all_gather x1, blocking collectives, on_device(): return lax.all_gather(picture, 'tile', axis=1, tiled=True)  1.99 us
    unnamed x7, local copies, waits for them, and re-layouts  1.37 us
  transfers between devices with their start and end apart: 10, of which 4 were waited for; matrix products, arithmetic and copies ran while one was open for 0% of the time, Pallas kernels for 18%

profile of v7, /device:TPU:0, one launch (start us, length us, event | category | flops | bytes accessed | tf_op | source)
XLA Modules:
  0.0 35.0 jit_solution(7456743884560392577)
XLA Ops:
  0.0 0.0 copy-start.1
  0.0 0.7 %copy-done.1 = s32[1,32]{1,0:T(1,128)S(1)} copy-done((s32[1,32]{1,0:T(1,128)S(1)}, s32[1,32]{1,0:T(1,128)}, u32[]{:S(2)}) %copy-start.1) | copy-done | bytes 152
  0.7 0.0 copy-start
  0.7 2.4 %edges.1 = (bf16[16,16,4096]{2,1,0:T(8,128)(2,1)S(1)}, bf16[16,4096]{1,0:T(8,128)(2,1)S(1)}, bf16[16,4096]{1,0:T(8,128)(2,1)S(1)}, bf16[16,4096]{1,0:T(8,128)(2,1)S(1)}, s32[1,32]{1,0:T(1,128)S(1)}) custom-call(s32[1,32]{1,0:T(1,128)S(1)} %copy-done.1, bf16[4,16,16,4096]{3,2,1,0:T(8,128)(2,1)} %vol.5), custom_call_target="tpu_custom_call" | custom-call | flops 1000000 | bytes 2097152 | tf_op jit(solution)/shard_map/edges/pallas_call | solution.py:88
  3.1 0.5 %collective-permute-start = (bf16[16,4096]{1,0:T(8,128)(2,1)S(1)}, bf16[16,4096]{1,0:T(8,128)(2,1)S(1)}, u32[]{:S(2)}, u32[]{:S(2)}) collective-permute-start(bf16[16,4096]{1,0:T(8,128)(2,1)S(1)} %get-tuple-element.28), channel_id=1, source_target_pairs={{0,1},{1,0},{2,3},{3,2},{4,5},{5,4},{6,7},{7,6},{8,9},{9,8},{10,11... | collective-permute-start | bytes 393224 | tf_op jit(solution)/shard_map/ppermute | solution.py:395
  3.6 2.6 %collective-permute-start.1 = (bf16[16,4096]{1,0:T(8,128)(2,1)S(1)}, bf16[16,4096]{1,0:T(8,128)(2,1)S(1)}, u32[]{:S(2)}, u32[]{:S(2)}) collective-permute-start(bf16[16,4096]{1,0:T(8,128)(2,1)S(1)} %get-tuple-element.31), channel_id=1, source_target_pairs={{0,2},{2,0},{4,6},{6,4},{8,10},{10,8},{12,14},{14,12},{1,3},{3,1},... | collective-permute-start | bytes 393224 | tf_op jit(solution)/shard_map/ppermute | solution.py:397
  6.2 0.7 %collective-permute-start.2 = (bf16[16,4096]{1,0:T(8,128)(2,1)S(1)}, bf16[16,4096]{1,0:T(8,128)(2,1)S(1)}, u32[]{:S(2)}, u32[]{:S(2)}) collective-permute-start(bf16[16,4096]{1,0:T(8,128)(2,1)S(1)} %get-tuple-element.32), channel_id=1, source_target_pairs={{2,4},{6,8},{10,12},{4,2},{8,6},{12,10},{3,5},{7,9},{11,13},{5,3},... | collective-permute-start | bytes 393224 | tf_op jit(solution)/shard_map/ppermute | solution.py:399
  6.8 0.0 collective-permute-done.border
  6.9 0.0 copy-done
  6.9 4.0 %march_far.1 = (f32[4,16,2560]{2,1,0:T(8,128)S(1)}, f32[2,6,16,2560]{3,2,1,0:T(8,128)S(1)}) custom-call(s32[1,32]{1,0:T(1,128)S(1)} %get-tuple-element.43.mask, bf16[4,16,16,4096]{3,2,1,0:T(8,128)(2,1)S(1)} %copy-done, bf16[16,16,4096]{2,1,0:T(8,128)(2,1)S(1)} %get-tuple-element.27.density, bf16[16,4096]{1,0:T(8,128)(2,1)S(1)} %collective-permute-done.border), custom_call_target="tpu_custom_call" | custom-call | flops 26214400 | bytes 5242880 | tf_op jit(solution)/shard_map/march_far/pallas_call | solution.py:236
  10.9 0.0 collective-permute-done.1.near
  10.9 0.0 collective-permute-done.2.far
  10.9 0.6 %finish.1 = (s16[4,16,512]{2,1,0:T(8,128)(2,1)S(1)}, s16[4,16,512]{2,1,0:T(8,128)(2,1)S(1)}, s16[4,16,512]{2,1,0:T(8,128)(2,1)S(1)}, s16[4,16,512]{2,1,0:T(8,128)(2,1)S(1)}, s16[4,16,512]{2,1,0:T(8,128)(2,1)S(1)}) custom-call(f32[4,16,2560]{2,1,0:T(8,128)S(1)} %get-tuple-element.29.sums, f32[2,6,16,2560]{3,2,1,0:T(8,128)S(1)} %get-tuple-element.30.ends, ...), custom_call_target="tpu_custom_call" | custom-call | flops 2457600 | bytes 2621440 | tf_op jit(solution)/shard_map/finish/pallas_call | solution.py:277
  11.5 0.0 copy-start.2
  11.5 6.6 %collective-permute-start.3 = (s16[4,16,512]{2,1,0:T(8,128)(2,1)S(1)}, s16[4,16,512]{2,1,0:T(8,128)(2,1)S(1)}, u32[]{:S(2)}, u32[]{:S(2)}) collective-permute-start(s16[4,16,512]{2,1,0:T(8,128)(2,1)S(1)} %get-tuple-element.38), channel_id=1, source_target_pairs={{0,10},{2,8},{4,14},{6,12},{8,2},{10,0},{12,6},{14,4},{1,11},{3,9}... | collective-permute-start | bytes 196616 | tf_op jit(solution)/shard_map/ppermute | solution.py:409
  18.1 0.0 collective-permute-start.4
  18.1 4.5 %collective-permute-start.5 = (s16[4,16,512]{2,1,0:T(8,128)(2,1)S(1)}, s16[4,16,512]{2,1,0:T(8,128)(2,1)S(1)}, u32[]{:S(2)}, u32[]{:S(2)}) collective-permute-start(s16[4,16,512]{2,1,0:T(8,128)(2,1)S(1)} %get-tuple-element.40), channel_id=1, source_target_pairs={{0,14},{2,12},{4,10},{6,8},{8,6},{10,4},{12,2},{14,0},{1,15},{3,13... | collective-permute-start | bytes 196616 | tf_op jit(solution)/shard_map/ppermute | solution.py:409
  22.6 0.0 collective-permute-start.6
  22.6 2.3 %march_near.1 = (s16[4,16,512]{2,1,0:T(8,128)(2,1)S(1)}, s16[4,16,512]{2,1,0:T(8,128)(2,1)S(1)}, s16[4,16,512]{2,1,0:T(8,128)(2,1)S(1)}) custom-call(s32[1,32]{1,0:T(1,128)S(1)} %get-tuple-element.43.mask, bf16[4,16,16,4096]{3,2,1,0:T(8,128)(2,1)S(1)} %copy-done, bf16[16,16,4096]{2,1,0:T(8,128)(2,1)S(1)} %get-tuple-element.27.density, ...), custom_call_target="tpu_custom_call" | custom-call | flops 15728640 | bytes 3145728 | tf_op jit(solution)/shard_map/march_near/pallas_call | solution.py:328
  24.9 0.1 collective-permute-start.7
  25.0 0.0 collective-permute-done.3.refs_0_
  25.0 2.5 %collective-permute-start.8 = (s16[4,16,512]{2,1,0:T(8,128)(2,1)S(1)}, s16[4,16,512]{2,1,0:T(8,128)(2,1)S(1)}, u32[]{:S(2)}, u32[]{:S(2)}) collective-permute-start(s16[4,16,512]{2,1,0:T(8,128)(2,1)S(1)} %get-tuple-element.45), channel_id=1, source_target_pairs={{0,4},{2,6},{4,0},{6,2},{8,12},{10,14},{12,8},{14,10},{1,5},{3,7},... | collective-permute-start | bytes 196616 | tf_op jit(solution)/shard_map/ppermute | solution.py:409
  27.5 0.0 collective-permute-done.4.refs_1_
  27.5 1.1 %collective-permute-start.9 = (s16[4,16,512]{2,1,0:T(8,128)(2,1)S(1)}, s16[4,16,512]{2,1,0:T(8,128)(2,1)S(1)}, u32[]{:S(2)}, u32[]{:S(2)}) collective-permute-start(s16[4,16,512]{2,1,0:T(8,128)(2,1)S(1)} %get-tuple-element.46), channel_id=1, source_target_pairs={{0,2},{2,0},{4,6},{6,4},{8,10},{10,8},{12,14},{14,12},{1,3},{3,1},... | collective-permute-start | bytes 196616 | tf_op jit(solution)/shard_map/ppermute | solution.py:409
  28.6 0.0 collective-permute-done.5.refs_2_
  28.6 0.7 %collective-permute-done.6.refs_3_ = s16[4,16,512]{2,1,0:T(8,128)(2,1)S(1)} collective-permute-done((s16[4,16,512]{2,1,0:T(8,128)(2,1)S(1)}, s16[4,16,512]{2,1,0:T(8,128)(2,1)S(1)}, u32[]{:S(2)}, u32[]{:S(2)}) %collective-permute-start.6) | collective-permute-done | bytes 65568 | tf_op jit(solution)/shard_map/ppermute | solution.py:409
  29.3 0.8 %collective-permute-done.7.refs_5_ = s16[4,16,512]{2,1,0:T(8,128)(2,1)S(1)} collective-permute-done((s16[4,16,512]{2,1,0:T(8,128)(2,1)S(1)}, s16[4,16,512]{2,1,0:T(8,128)(2,1)S(1)}, u32[]{:S(2)}, u32[]{:S(2)}) %collective-permute-start.7) | collective-permute-done | bytes 65568 | tf_op jit(solution)/shard_map/ppermute | solution.py:409
  30.1 0.5 %collective-permute-done.8.refs_6_ = s16[4,16,512]{2,1,0:T(8,128)(2,1)S(1)} collective-permute-done((s16[4,16,512]{2,1,0:T(8,128)(2,1)S(1)}, s16[4,16,512]{2,1,0:T(8,128)(2,1)S(1)}, u32[]{:S(2)}, u32[]{:S(2)}) %collective-permute-start.8) | collective-permute-done | bytes 65568 | tf_op jit(solution)/shard_map/ppermute | solution.py:409
  30.6 1.1 %collective-permute-done.9.refs_7_ = s16[4,16,512]{2,1,0:T(8,128)(2,1)S(1)} collective-permute-done((s16[4,16,512]{2,1,0:T(8,128)(2,1)S(1)}, s16[4,16,512]{2,1,0:T(8,128)(2,1)S(1)}, u32[]{:S(2)}, u32[]{:S(2)}) %collective-permute-start.9) | collective-permute-done | bytes 65568 | tf_op jit(solution)/shard_map/ppermute | solution.py:409
  31.8 0.0 copy-done.2
  31.8 0.5 %composite.1 = f32[4,16,512]{2,1,0:T(8,128)S(1)} custom-call(s32[1,8]{1,0:T(1,128)S(1)} %bitcast.1, s16[4,16,512]{2,1,0:T(8,128)(2,1)S(1)} %collective-permute-done.3.refs_0_, s16[4,16,512]{2,1,0:T(8,128)(2,1)S(1)} %collective-permute-done.4.refs_1_, s16[4,16,512]{2,1,0:T(8,128)(2,1)S(1)} %collective-permute-done.5.refs_2_, ...), custom_call_target="tpu_custom_call" | custom-call | tf_op jit(solution)/shard_map/composite/pallas_call | solution.py:377
  32.3 2.0 %all_gather.3 = f32[4,32,512]{2,1,0:T(8,128)S(1)} all-gather(f32[4,16,512]{2,1,0:T(8,128)S(1)} %composite.1), channel_id=1, replica_groups=mesh['parts'=2,'depth'=8,'tile'=2] {'tile'}, dimensions={1}, use_global_device_ids=true | all-gather | bytes 393216 | tf_op jit(solution)/shard_map/all_gather | solution.py:413
  34.3 0.7 %copy.5 = f32[4,32,512]{2,1,0:T(8,128)} copy(f32[4,32,512]{2,1,0:T(8,128)S(1)} %all_gather.3) | data formatting | bytes 524288
Async XLA Ops:
  0.0 0.7 %copy-start.1 = (s32[1,32]{1,0:T(1,128)S(1)}, s32[1,32]{1,0:T(1,128)}, u32[]{:S(2)}) copy-start(s32[1,32]{1,0:T(1,128)} %mask_hbm.1) | copy-start | bytes 388
  0.7 6.2 %copy-start = (bf16[4,16,16,4096]{3,2,1,0:T(8,128)(2,1)S(1)}, bf16[4,16,16,4096]{3,2,1,0:T(8,128)(2,1)}, u32[]{:S(2)}) copy-start(bf16[4,16,16,4096]{3,2,1,0:T(8,128)(2,1)} %vol.5) | copy-start | bytes 25165828
  3.1 3.8 %collective-permute-start = (bf16[16,4096]{1,0:T(8,128)(2,1)S(1)}, bf16[16,4096]{1,0:T(8,128)(2,1)S(1)}, u32[]{:S(2)}, u32[]{:S(2)}) collective-permute-start(bf16[16,4096]{1,0:T(8,128)(2,1)S(1)} %get-tuple-element.28), channel_id=1, source_target_pairs={{0,1},{1,0},{2,3},{3,2},{4,5},{5,4},{6,7},{7,6},{8,9},{9,8},{10,11... | collective-permute-start | bytes 393224 | tf_op jit(solution)/shard_map/ppermute | solution.py:395
  3.6 7.3 %collective-permute-start.1 = (bf16[16,4096]{1,0:T(8,128)(2,1)S(1)}, bf16[16,4096]{1,0:T(8,128)(2,1)S(1)}, u32[]{:S(2)}, u32[]{:S(2)}) collective-permute-start(bf16[16,4096]{1,0:T(8,128)(2,1)S(1)} %get-tuple-element.31), channel_id=1, source_target_pairs={{0,2},{2,0},{4,6},{6,4},{8,10},{10,8},{12,14},{14,12},{1,3},{3,1},... | collective-permute-start | bytes 393224 | tf_op jit(solution)/shard_map/ppermute | solution.py:397
  6.2 4.7 %collective-permute-start.2 = (bf16[16,4096]{1,0:T(8,128)(2,1)S(1)}, bf16[16,4096]{1,0:T(8,128)(2,1)S(1)}, u32[]{:S(2)}, u32[]{:S(2)}) collective-permute-start(bf16[16,4096]{1,0:T(8,128)(2,1)S(1)} %get-tuple-element.32), channel_id=1, source_target_pairs={{2,4},{6,8},{10,12},{4,2},{8,6},{12,10},{3,5},{7,9},{11,13},{5,3},... | collective-permute-start | bytes 393224 | tf_op jit(solution)/shard_map/ppermute | solution.py:399
  11.5 20.3 %copy-start.2 = (s32[8]{0:T(128)S(1)}, s32[8]{0:T(128)}, u32[]{:S(2)}) copy-start(s32[8]{0:T(128)} %param.5) | copy-start | bytes 100
  11.5 13.5 %collective-permute-start.3 = (s16[4,16,512]{2,1,0:T(8,128)(2,1)S(1)}, s16[4,16,512]{2,1,0:T(8,128)(2,1)S(1)}, u32[]{:S(2)}, u32[]{:S(2)}) collective-permute-start(s16[4,16,512]{2,1,0:T(8,128)(2,1)S(1)} %get-tuple-element.38), channel_id=1, source_target_pairs={{0,10},{2,8},{4,14},{6,12},{8,2},{10,0},{12,6},{14,4},{1,11},{3,9}... | collective-permute-start | bytes 196616 | tf_op jit(solution)/shard_map/ppermute | solution.py:409
  18.1 9.4 %collective-permute-start.4 = (s16[4,16,512]{2,1,0:T(8,128)(2,1)S(1)}, s16[4,16,512]{2,1,0:T(8,128)(2,1)S(1)}, u32[]{:S(2)}, u32[]{:S(2)}) collective-permute-start(s16[4,16,512]{2,1,0:T(8,128)(2,1)S(1)} %get-tuple-element.39), channel_id=1, source_target_pairs={{0,8},{2,10},{4,12},{6,14},{8,0},{10,2},{12,4},{14,6},{1,9},{3,11}... | collective-permute-start | bytes 196616 | tf_op jit(solution)/shard_map/ppermute | solution.py:409
  18.1 10.5 %collective-permute-start.5 = (s16[4,16,512]{2,1,0:T(8,128)(2,1)S(1)}, s16[4,16,512]{2,1,0:T(8,128)(2,1)S(1)}, u32[]{:S(2)}, u32[]{:S(2)}) collective-permute-start(s16[4,16,512]{2,1,0:T(8,128)(2,1)S(1)} %get-tuple-element.40), channel_id=1, source_target_pairs={{0,14},{2,12},{4,10},{6,8},{8,6},{10,4},{12,2},{14,0},{1,15},{3,13... | collective-permute-start | bytes 196616 | tf_op jit(solution)/shard_map/ppermute | solution.py:409
  22.6 6.7 %collective-permute-start.6 = (s16[4,16,512]{2,1,0:T(8,128)(2,1)S(1)}, s16[4,16,512]{2,1,0:T(8,128)(2,1)S(1)}, u32[]{:S(2)}, u32[]{:S(2)}) collective-permute-start(s16[4,16,512]{2,1,0:T(8,128)(2,1)S(1)} %get-tuple-element.41), channel_id=1, source_target_pairs={{0,12},{2,14},{4,8},{6,10},{8,4},{10,6},{12,0},{14,2},{1,13},{3,15... | collective-permute-start | bytes 196616 | tf_op jit(solution)/shard_map/ppermute | solution.py:409
  24.9 5.2 %collective-permute-start.7 = (s16[4,16,512]{2,1,0:T(8,128)(2,1)S(1)}, s16[4,16,512]{2,1,0:T(8,128)(2,1)S(1)}, u32[]{:S(2)}, u32[]{:S(2)}) collective-permute-start(s16[4,16,512]{2,1,0:T(8,128)(2,1)S(1)} %get-tuple-element.44), channel_id=1, source_target_pairs={{0,6},{2,4},{4,2},{6,0},{8,14},{10,12},{12,10},{14,8},{1,7},{3,5},... | collective-permute-start | bytes 196616 | tf_op jit(solution)/shard_map/ppermute | solution.py:409
  25.0 5.6 %collective-permute-start.8 = (s16[4,16,512]{2,1,0:T(8,128)(2,1)S(1)}, s16[4,16,512]{2,1,0:T(8,128)(2,1)S(1)}, u32[]{:S(2)}, u32[]{:S(2)}) collective-permute-start(s16[4,16,512]{2,1,0:T(8,128)(2,1)S(1)} %get-tuple-element.45), channel_id=1, source_target_pairs={{0,4},{2,6},{4,0},{6,2},{8,12},{10,14},{12,8},{14,10},{1,5},{3,7},... | collective-permute-start | bytes 196616 | tf_op jit(solution)/shard_map/ppermute | solution.py:409
  27.5 4.3 %collective-permute-start.9 = (s16[4,16,512]{2,1,0:T(8,128)(2,1)S(1)}, s16[4,16,512]{2,1,0:T(8,128)(2,1)S(1)}, u32[]{:S(2)}, u32[]{:S(2)}) collective-permute-start(s16[4,16,512]{2,1,0:T(8,128)(2,1)S(1)} %get-tuple-element.46), channel_id=1, source_target_pairs={{0,2},{2,0},{4,6},{6,4},{8,10},{10,8},{12,14},{14,12},{1,3},{3,1},... | collective-permute-start | bytes 196616 | tf_op jit(solution)/shard_map/ppermute | solution.py:409
